TPU v7x, 512 devices: a whole 4x8x8 slice. The times are simulated.
512 devices in a mesh: gx: 8 (over y), gy: 8 (over z_lo, core), gz: 8 (over z_hi, x).
Axes of the slice: x: 4, y: 8, z: 8 (z_hi: 2, z_lo: 4; z = z_hi * 4 + z_lo), core: 2. Of those that a mesh axis runs over, the one named last changes fastest.
Arguments:
- tokens: bfloat16 [1024, 8192], P('gz', ('gx', 'gy')), may hold values from -6 to 6
- gate_weight: bfloat16 [8192, 14336], P(('gx', 'gz'), 'gy'), may hold values from -0.0625 to 0.0625
- up_weight: bfloat16 [8192, 14336], P(('gx', 'gz'), 'gy'), may hold values from -0.0625 to 0.0625
- down_weight: bfloat16 [8192, 14336], P(('gx', 'gz'), 'gy'), may hold values from -0.046875 to 0.046875
- grad_mixed: bfloat16 [1024, 8192], P('gz', ('gx', 'gy')), may hold values from -6 to 6
Outputs:
- mixed: bfloat16 [1024, 8192], P('gz', ('gx', 'gy'))
- tokens_grad: bfloat16 [1024, 8192], P('gz', ('gx', 'gy'))
All inputs are finite; a program needn't handle non-finite values.
Results may differ from a plain program's by a relative error of at most 0.0049.
Values may be sent and summed in bfloat16 or wider, within the bound.
No kernel may reach another device: no remote copies, remote signals or barrier semaphores. Data moves between devices by JAX's collectives and lax.ppermute only.
A program may use at most 64 MiB of HBM per device.

v0:
```python
import jax
import jax.numpy as jnp
from jax import lax
from jax.sharding import PartitionSpec as P


def widen_cols(values):
    return lax.all_gather(values, "gy", axis=1, tiled=True)


def narrow(values):
    return lax.psum_scatter(values, "gy", scatter_dimension=1, tiled=True)


def combine(partial_value):
    return lax.psum(partial_value, "gx")


def gate_grads(hidden_grad, gate_value, up_value, silu_gate):
    sigmoid_gate = jax.nn.sigmoid(gate_value)
    gate_grad = (
        hidden_grad * up_value * sigmoid_gate * (1.0 + gate_value * (1.0 - sigmoid_gate))
    ).astype(jnp.bfloat16)
    up_grad = (hidden_grad * silu_gate).astype(jnp.bfloat16)
    return (gate_grad, up_grad)


def on_device(tokens, gate_weight, up_weight, down_weight, grad_mixed):
    contract = (((1,), (1,)), ((), ()))
    gate_full, up_full, down_full = (
        lax.all_gather(gate_weight, "gz", axis=0, tiled=True),
        lax.all_gather(up_weight, "gz", axis=0, tiled=True),
        lax.all_gather(down_weight, "gz", axis=0, tiled=True),
    )
    hidden_width = gate_full.shape[1]
    wide_tokens = widen_cols(tokens)
    partial_value = jnp.concatenate(
        [
            jnp.dot(wide_tokens, gate_full, preferred_element_type=jnp.float32),
            jnp.dot(wide_tokens, up_full, preferred_element_type=jnp.float32),
        ],
        axis=1,
    )
    summed = combine(partial_value)
    gate_value = summed[:, :hidden_width]
    up_value = summed[:, hidden_width:]
    silu_gate = jax.nn.silu(gate_value)
    hidden_rows = (silu_gate * up_value).astype(jnp.bfloat16)
    output_terms = lax.dot_general(
        hidden_rows, down_full, contract, preferred_element_type=jnp.float32
    )
    mixed = narrow(output_terms).astype(jnp.bfloat16)
    wide_grad = widen_cols(grad_mixed)
    hidden_grad = combine(jnp.dot(wide_grad, down_full, preferred_element_type=jnp.float32))
    gate_grad, up_grad = gate_grads(hidden_grad, gate_value, up_value, silu_gate)
    both_grads = jnp.concatenate([gate_grad, up_grad], axis=1)
    grad_terms = lax.dot_general(
        both_grads[:, :hidden_width], gate_full, contract, preferred_element_type=jnp.float32
    )
    grad_terms = grad_terms + lax.dot_general(
        both_grads[:, hidden_width:], up_full, contract, preferred_element_type=jnp.float32
    )
    tokens_grad = narrow(grad_terms).astype(jnp.bfloat16)
    return (mixed, tokens_grad)


def solution(mesh):
    placed = (
        P("gz", ("gx", "gy")),
        P(("gx", "gz"), "gy"),
        P(("gx", "gz"), "gy"),
        P(("gx", "gz"), "gy"),
        P("gz", ("gx", "gy")),
    )
    return jax.shard_map(
        on_device,
        mesh=mesh,
        in_specs=placed,
        out_specs=(P("gz", ("gx", "gy")), P("gz", ("gx", "gy"))),
        check_vma=False,
    )
```

profile of v0, /device:TPU:1, one launch (start us, length us, event | category | flops | bytes accessed | tf_op | source)
XLA Modules:
  0.0 513.3 jit_solution(13338420152035894181)
XLA Ops:
  7.2 0.7 all-gather.6.cloned.1.call-update
  7.9 0.7 all-gather.4.cloned.1.call-update
  8.7 0.7 all-gather.8.cloned.1.call-update
  9.4 20.0 %all_gather.15 = bf16[128,1024]{1,0:T(8,128)(2,1)S(1)} all-gather(bf16[128,128]{1,0:T(8,128)(2,1)} %param.5), channel_id=1, replica_groups=mesh['gx'=8,'gy'=8,'gz'=8] {'gy'}, dimensions={1}, use_global_device_ids=true | all-gather | bytes 294912 | tf_op jit(solution)/shard_map/all_gather | solution.py:8
  29.5 15.8 %all_gather.19 = bf16[128,1024]{1,0:T(8,128)(2,1)S(1)} all-gather(bf16[128,128]{1,0:T(8,128)(2,1)} %param.9), channel_id=1, replica_groups=mesh['gx'=8,'gy'=8,'gz'=8] {'gy'}, dimensions={1}, use_global_device_ids=true | all-gather | bytes 294912 | tf_op jit(solution)/shard_map/all_gather | solution.py:8
  45.2 77.7 %all-gather.6.cloned.1.call-done = bf16[1024,1792]{1,0:T(8,128)(2,1)} async-done(((bf16[128,1792]{1,0:T(8,128)(2,1)}), bf16[1024,1792]{1,0:T(8,128)(2,1)}) %all-gather.6.cloned.1.call-update) | async-done | bytes 3670032 | tf_op jit(solution)/shard_map/all_gather | solution.py:32
  122.9 2.7 fusion.10
  125.6 100.8 %all-gather.4.cloned.1.call-done = bf16[1024,1792]{1,0:T(8,128)(2,1)} async-done(((bf16[128,1792]{1,0:T(8,128)(2,1)}), bf16[1024,1792]{1,0:T(8,128)(2,1)}) %all-gather.4.cloned.1.call-update) | async-done | bytes 3670032 | tf_op jit(solution)/shard_map/all_gather | solution.py:31
  226.4 2.7 fusion.9
  229.1 1.4 pad_maximum_fusion
  230.5 99.4 %all-gather.8.cloned.1.call-done = bf16[1024,1792]{1,0:T(8,128)(2,1)} async-done(((bf16[128,1792]{1,0:T(8,128)(2,1)}), bf16[1024,1792]{1,0:T(8,128)(2,1)}) %all-gather.8.cloned.1.call-update) | async-done | bytes 3670032 | tf_op jit(solution)/shard_map/all_gather | solution.py:33
  329.9 3.7 fusion.11
  333.6 0.0 reduce-scatter.5.cloned.1.call-start
  333.6 86.3 %all-reduce.3.cloned.1.call-done = (f32[128,3584]{1,0:T(8,128)}, f32[128,1792]{1,0:T(8,128)}) async-done(((f32[128,3584]{1,0:T(8,128)}, f32[128,1792]{1,0:T(8,128)}), (f32[128,3584]{1,0:T(8,128)}, f32[128,1792]{1,0:T(8,128)})) %all-reduce.3.cloned.1.call-update) | async-done | bytes 2752528 | tf_op jit(solution)/shard_map/psum | solution.py:16
  419.9 4.3 fusion.2
  424.3 0.1 copy-done.1
  424.4 0.2 copy-done.2
  424.6 2.1 convolution_add_fusion
  426.8 0.0 reduce-scatter.3.cloned.1.call-start
  426.8 4.1 fusion.1
  431.0 33.4 %reduce-scatter.5.cloned.1.call-done = f32[128,128]{1,0:T(8,128)} async-done(((f32[128,1024]{1,0:T(8,128)}), f32[128,128]{1,0:T(8,128)}) %reduce-scatter.5.cloned.1.call-update) | async-done | bytes 65552 | tf_op jit(solution)/shard_map/reduce_scatter | solution.py:12
  464.4 1.5 convert_element_type.19
  465.9 39.1 %reduce-scatter.3.cloned.1.call-done = f32[128,128]{1,0:T(8,128)} async-done(((f32[128,1024]{1,0:T(8,128)}), f32[128,128]{1,0:T(8,128)}) %reduce-scatter.3.cloned.1.call-update) | async-done | bytes 65552 | tf_op jit(solution)/shard_map/reduce_scatter | solution.py:12
  505.0 1.5 convert_element_type.16
  (11 shorter events, 0.2 us)
Async XLA Ops:
  7.2 115.7 %all-gather.6.cloned.1.call-start = ((), (), s32[]{:S(2)}) async-start(), calls=%async_computation.3 | async-start | bytes 4128768 | tf_op jit(solution)/shard_map/all_gather | solution.py:32
  7.9 218.5 %all-gather.4.cloned.1.call-start = ((), (), s32[]{:S(2)}) async-start(), calls=%async_computation.2 | async-start | bytes 4128768 | tf_op jit(solution)/shard_map/all_gather | solution.py:31
  8.6 321.3 %all-gather.8.cloned.1.call-start = ((), (), s32[]{:S(2)}) async-start(), calls=%async_computation.4 | async-start | bytes 4128768 | tf_op jit(solution)/shard_map/all_gather | solution.py:33
  9.4 410.5 %all-reduce.3.cloned.1.call-start = ((), (), s32[]{:S(2)}) async-start(), calls=%async_computation.7 | async-start | bytes 5505024 | tf_op jit(solution)/shard_map/psum | solution.py:16
  333.6 130.8 %reduce-scatter.5.cloned.1.call-start = ((), (), s32[]{:S(2)}) async-start(), calls=%async_computation.6 | async-start | bytes 589824 | tf_op jit(solution)/shard_map/reduce_scatter | solution.py:12
  419.9 4.4 copy-start
  419.9 4.5 copy-start.1
  419.9 4.7 copy-start.2
  426.8 78.2 %reduce-scatter.3.cloned.1.call-start = ((), (), s32[]{:S(2)}) async-start(), calls=%async_computation.5 | async-start | bytes 589824 | tf_op jit(solution)/shard_map/reduce_scatter | solution.py:12
Sparse Core Ops, SparseCore 0:
  11.2 111.6 all-gather.5
  126.1 100.2 all-gather.3
  229.6 100.2 all-gather.7
  333.7 86.1 all-reduce.2
  426.9 37.4 reduce-scatter.4
  467.1 37.8 reduce-scatter.2
where the time goes:
time: 516 us; the launch traced here: 513 us
  waiting for transfers between devices  439 us (85%)
  blocking collectives  35.8 us (7%)
  matrix products  19.6 us (4%)
  between operations  14.1 us (3%)
    all_gather x1, waiting for transfers between devices, on_device(): lax.all_gather(gate_weight, 'gz', axis=0, tiled=True)  101 us
    all_gather x1, waiting for transfers between devices, on_device(): lax.all_gather(down_weight, 'gz', axis=0, tiled=True)  99.4 us
    psum x1, waiting for transfers between devices, combine(): return lax.psum(partial_value, 'gx')  86.3 us
    all_gather x1, waiting for transfers between devices, on_device(): lax.all_gather(up_weight, 'gz', axis=0, tiled=True)  77.7 us
    reduce_scatter x2, waiting for transfers between devices, narrow(): return lax.psum_scatter(values, 'gy', scatter_dimension=1, tiled=True)  72.6 us
    all_gather x2, blocking collectives, widen_cols(): return lax.all_gather(values, 'gy', axis=1, tiled=True)  35.8 us
  transfers between devices with their start and end apart: 6, of which 6 were waited for; matrix products, arithmetic and copies ran while one was open for 2% of the time, Pallas kernels for 0%

commit v1 on v0

v1 whole, which is shorter than its diff:
```python
import jax
import jax.numpy as jnp
from jax import lax
from jax.sharding import Mesh, PartitionSpec as P

AXES = ("y", "zl", "core", "zh", "x")
RING = ("zh", "zl", "core")
NT = (((1,), (1,)), ((), ()))
F32, BF16 = jnp.float32, jnp.bfloat16


def shift(values, step):
    return lax.ppermute(values, "x", [(i, (i + step) % 4) for i in range(4)])


def spread(values, axes, n):
    return lax.all_to_all(jnp.broadcast_to(values[None], (n, *values.shape)), axes, 0, 0, tiled=True)


def widen(values):
    blocks = spread(values, RING, 16).reshape(2, 2, 2, 2, 128, 128)
    return blocks.transpose(0, 4, 2, 3, 1, 5).reshape(256, 1024)


def swap(weight):
    return lax.all_to_all(weight, "zh", 1, 0, tiled=True)


def gather(block):
    half = block.shape[0] // 2
    left, right = shift(block, 1), shift(block, -1)
    far = jnp.concatenate([shift(left[:half], 1), shift(right[half:], -1)], axis=0)
    return jnp.concatenate([block, left, right, far], axis=0)


def to_relative(values, x):
    blocks = values.reshape(256, 4, 256)
    return jnp.concatenate(
        [lax.dynamic_index_in_dim(blocks, (x + k) % 4, 1, keepdims=False) for k in (0, 3, 1, 2)], axis=1
    )


def to_absolute(values, x):
    blocks = values.reshape(256, 4, 256)
    slots = jnp.array([0, 2, 3, 1])
    return jnp.stack(
        [lax.dynamic_index_in_dim(blocks, slots[(k - x) % 4], 1, keepdims=False) for k in range(4)], axis=1
    )


def combine(partial_value):
    parts = lax.all_to_all(partial_value.astype(BF16).reshape(8, 32, -1), "y", 0, 0, tiled=True)
    return jnp.sum(parts.astype(F32), axis=0)


def tokens_of(values):
    return spread(values, "y", 8).reshape(256, -1)


def narrow(values, x):
    terms = to_absolute(values, x).astype(BF16).reshape(2, 128, 2, 2, 2, 128)
    terms = terms.transpose(0, 4, 2, 3, 1, 5).reshape(16, 128, 128)
    parts = lax.all_to_all(terms, RING, 0, 0, tiled=True)
    return jnp.sum(parts.astype(F32), axis=0).astype(BF16)


def on_device(tokens, gate_weight, up_weight, down_weight, grad_mixed):
    x = lax.axis_index("x")
    gate = gather(swap(gate_weight))
    wide = to_relative(widen(tokens), x)
    gate_value = combine(jnp.dot(wide, gate, preferred_element_type=F32))
    up = gather(swap(up_weight))
    up_value = combine(jnp.dot(wide, up, preferred_element_type=F32))
    down = gather(swap(down_weight))
    wide_grad = to_relative(widen(grad_mixed), x)
    hidden_grad = combine(jnp.dot(wide_grad, down, preferred_element_type=F32))
    sig = jax.nn.sigmoid(gate_value)
    silu = gate_value * sig
    hidden = tokens_of((silu * up_value).astype(BF16))
    mixed = narrow(lax.dot_general(hidden, down, NT, preferred_element_type=F32), x)
    gate_grad = (hidden_grad * up_value * sig * (1.0 + gate_value * (1.0 - sig))).astype(BF16)
    up_grad = (hidden_grad * silu).astype(BF16)
    grads = tokens_of(jnp.concatenate([gate_grad, up_grad], axis=1))
    terms = lax.dot_general(grads[:, :896], gate, NT, preferred_element_type=F32)
    terms = terms + lax.dot_general(grads[:, 896:], up, NT, preferred_element_type=F32)
    return mixed, narrow(terms, x)


def solution(mesh):
    fine = Mesh(mesh.devices.reshape(8, 4, 2, 2, 4), AXES)
    acts = P(("zh", "x"), ("y", "zl", "core"))
    weights = P(("y", "zh", "x"), ("zl", "core"))
    return jax.shard_map(
        on_device,
        mesh=fine,
        in_specs=(acts, weights, weights, weights, acts),
        out_specs=(acts, acts),
        check_vma=False,
    )
```

time: 516 us -> 281 us (0.54)
  waiting for transfers between devices: 439 us -> 79.1 us
  starting transfers between devices: 0.24 us -> 121 us
  local copies, waits for them, and re-layouts: 0.35 us -> 43.9 us
  blocking collectives: 35.8 us -> 13.6 us
  matrix products: 19.6 us -> 9.73 us
    all_gather x3 -> x0, waiting for transfers between devices: 278 us -> none  [the longest x1 101 us: on_device(): lax.all_gather(gate_weight, 'gz', axis=0, tiled=True)]
    psum x1 -> x0, waiting for transfers between devices: 86.3 us -> none  [combine(): return lax.psum(partial_value, 'gx')]
    all_to_all x0 -> x11, starting transfers between devices: none -> 81.6 us  [the longest x4 34.5 us: spread(): lax.all_to_all(jnp.broadcast_to(values[None], (n, *values.shape)), axes,...]
    all_to_all x0 -> x11, waiting for transfers between devices: none -> 78.3 us  [the longest x2 28.4 us: narrow(): parts = lax.all_to_all(terms, RING, 0, 0, tiled=True)]
    reduce_scatter x2 -> x0, waiting for transfers between devices: 72.6 us -> none  [narrow(): return lax.psum_scatter(values, 'gy', scatter_dimension=1, tiled=True)]
    ppermute x0 -> x12, starting transfers between devices: none -> 39.2 us  [shift(): return lax.ppermute(values, 'x', [(i, (i + step) % 4) for i in range(4)])]
    all_gather x2 -> x0, blocking collectives: 35.8 us -> none  [widen_cols(): return lax.all_gather(values, 'gy', axis=1, tiled=True)]
    unnamed x6 -> x45, local copies, waits for them, and re-layouts: 0.35 us -> 18.2 us
  transfers between devices with their start and end apart: 6 -> 23, of which waited for: 6 -> 9; matrix products, arithmetic and copies ran while one was open for 2% -> 18% of each run, Pallas kernels for 0% -> 0%
where the time goes in v1:
time: 281 us; the launch traced here: 279 us
  starting transfers between devices  121 us (43%)
  waiting for transfers between devices  79.1 us (28%)
  local copies, waits for them, and re-layouts  43.9 us (16%)
  blocking collectives  13.6 us (5%)
  matrix products  9.73 us (3%)
  between operations  8.96 us (3%)
  other arithmetic  2.84 us (1%)
    ppermute x12, starting transfers between devices, shift(): return lax.ppermute(values, 'x', [(i, (i + step) % 4) for i in range(4)])  39.2 us
    all_to_all x4, starting transfers between devices, spread(): lax.all_to_all(jnp.broadcast_to(values[None], (n, *values.shape)), axes,...  34.5 us
    all_to_all x2, waiting for transfers between devices, narrow(): parts = lax.all_to_all(terms, RING, 0, 0, tiled=True)  28.4 us
    all_to_all x4, waiting for transfers between devices, spread(): lax.all_to_all(jnp.broadcast_to(values[None], (n, *values.shape)), axes,...  18.4 us
    unnamed x45, local copies, waits for them, and re-layouts  18.2 us
    all_to_all x2, waiting for transfers between devices, swap(): return lax.all_to_all(weight, 'zh', 1, 0, tiled=True)  17.9 us
    all_to_all x3, starting transfers between devices, combine(): lax.all_to_all(partial_value.astype(BF16).reshape(8, 32, -1), 'y', 0, 0,...  16.9 us
    all_to_all x2, starting transfers between devices, narrow(): parts = lax.all_to_all(terms, RING, 0, 0, tiled=True)  15.8 us
  transfers between devices with their start and end apart: 23, of which 9 were waited for; matrix products, arithmetic and copies ran while one was open for 18% of the time, Pallas kernels for 0%

profile of v1, /device:TPU:1, one launch (start us, length us, event | category | flops | bytes accessed | tf_op | source)
XLA Modules:
  0.0 278.9 jit_solution(10624831356768811671)
XLA Ops:
  2.7 11.0 %all-to-all-start.3 = ((bf16[128,2,896]{0,2,1:T(8,128)(2,1)}), bf16[128,2,896]{0,2,1:T(8,128)(2,1)S(1)}, u32[]{:S(2)}, u32[]{:S(2)}) async-start(bf16[128,2,896]{0,2,1:T(8,128)(2,1)} %bitcast.10), calls=%async_computation.3 | async-start | bytes 917504 | tf_op jit(solution)/shard_map/all_to_all | solution.py:26
  14.9 9.2 %all-to-all-done.3 = bf16[128,2,896]{0,2,1:T(8,128)(2,1)S(1)} async-done(((bf16[128,2,896]{0,2,1:T(8,128)(2,1)}), bf16[128,2,896]{0,2,1:T(8,128)(2,1)S(1)}, u32[]{:S(2)}, u32[]{:S(2)}) %all-to-all-start.3) | async-done | bytes 458784 | tf_op jit(solution)/shard_map/all_to_all | solution.py:26
  24.1 3.5 %all-to-all-start.6 = ((bf16[128,2,896]{2,0,1:T(8,128)(2,1)}), bf16[128,2,896]{2,0,1:T(8,128)(2,1)S(1)}, u32[]{:S(2)}, u32[]{:S(2)}) async-start(bf16[128,2,896]{2,0,1:T(8,128)(2,1)} %copy.43), calls=%async_computation.6 | async-start | bytes 917504 | tf_op jit(solution)/shard_map/all_to_all | solution.py:26
  27.8 8.7 %all-to-all-done.6 = bf16[128,2,896]{2,0,1:T(8,128)(2,1)S(1)} async-done(((bf16[128,2,896]{2,0,1:T(8,128)(2,1)}), bf16[128,2,896]{2,0,1:T(8,128)(2,1)S(1)}, u32[]{:S(2)}, u32[]{:S(2)}) %all-to-all-start.6) | async-done | bytes 458784 | tf_op jit(solution)/shard_map/all_to_all | solution.py:26
  36.5 13.6 %all_to_all.102 = bf16[128,2,896]{0,2,1:T(8,128)(2,1)S(1)} all-to-all(bf16[128,2,896]{0,2,1:T(8,128)(2,1)S(1)} %bitcast.75), channel_id=1, replica_groups=mesh['y'=8,'zl'=4,'core'=2,'zh'=2,'x'=4] {'zh'}, dimensions={1} | all-to-all | bytes 917504 | tf_op jit(solution)/shard_map/all_to_all | solution.py:26
  51.1 18.4 %all-to-all-start = ((bf16[16,128,128]{2,1,0:T(8,128)(2,1)}), bf16[16,128,128]{2,1,0:T(8,128)(2,1)S(1)}, u32[]{:S(2)}, u32[]{:S(2)}) async-start(bf16[16,128,128]{2,1,0:T(8,128)(2,1)} %broadcast_in_dim.8), calls=%async_computation | async-start | bytes 1048576 | tf_op jit(solution)/shard_map/all_to_all | solution.py:17
  78.9 4.6 %collective-permute-start.9 = (bf16[256,896]{1,0:T(8,128)(2,1)S(1)}, bf16[256,896]{1,0:T(8,128)(2,1)}, u32[]{:S(2)}, u32[]{:S(2)}) collective-permute-start(bf16[256,896]{1,0:T(8,128)(2,1)S(1)} %bitcast.71), channel_id=1, source_target_pairs={{0,3},{1,0},{2,1},{3,2},{4,7},{5,4},{6,5},{7,6},{8,11},{9,8},{10,9... | collective-permute-start | bytes 1376264 | tf_op jit(solution)/shard_map/ppermute | solution.py:13
  88.4 8.4 %all-to-all-start.8 = ((bf16[16,128,128]{2,1,0:T(8,128)(2,1)}), bf16[16,128,128]{2,1,0:T(8,128)(2,1)S(1)}, u32[]{:S(2)}, u32[]{:S(2)}) async-start(bf16[16,128,128]{2,1,0:T(8,128)(2,1)} %broadcast_in_dim.10), calls=%async_computation.8 | async-start | bytes 1048576 | tf_op jit(solution)/shard_map/all_to_all | solution.py:17
  97.6 4.9 %collective-permute-start.1 = (bf16[256,896]{1,0:T(8,128)(2,1)}, bf16[256,896]{1,0:T(8,128)(2,1)}, u32[]{:S(2)}, u32[]{:S(2)}) collective-permute-start(bf16[256,896]{1,0:T(8,128)(2,1)} %bitcast.8), channel_id=1, source_target_pairs={{0,3},{1,0},{2,1},{3,2},{4,7},{5,4},{6,5},{7,6},{8,11},{9,8},{10,9... | collective-permute-start | bytes 1376264 | tf_op jit(solution)/shard_map/ppermute | solution.py:13
  107.7 4.6 %collective-permute-start.7 = (bf16[128,896]{1,0:T(8,128)(2,1)}, bf16[128,896]{1,0:T(8,128)(2,1)}, u32[]{:S(2)}, u32[]{:S(2)}) collective-permute-start(bf16[128,896]{1,0:T(8,128)(2,1)} %slice.35), channel_id=1, source_target_pairs={{0,3},{1,0},{2,1},{3,2},{4,7},{5,4},{6,5},{7,6},{8,11},{9,8},{10,9... | collective-permute-start | bytes 688136 | tf_op jit(solution)/shard_map/ppermute | solution.py:13
  120.6 4.6 %collective-permute-start.11 = (bf16[128,896]{1,0:T(8,128)(2,1)}, bf16[128,896]{1,0:T(8,128)(2,1)}, u32[]{:S(2)}, u32[]{:S(2)}) collective-permute-start(bf16[128,896]{1,0:T(8,128)(2,1)} %slice.37), channel_id=1, source_target_pairs={{0,3},{1,0},{2,1},{3,2},{4,7},{5,4},{6,5},{7,6},{8,11},{9,8},{10,9... | collective-permute-start | bytes 688136 | tf_op jit(solution)/shard_map/ppermute | solution.py:13
  128.7 6.8 %all-to-all-start.4 = ((bf16[8,32,896]{2,1,0:T(8,128)(2,1)}), bf16[8,32,896]{2,1,0:T(8,128)(2,1)}, u32[]{:S(2)}, u32[]{:S(2)}) async-start(bf16[8,32,896]{2,1,0:T(8,128)(2,1)} %bitcast.13), calls=%async_computation.4 | async-start | bytes 917504 | tf_op jit(solution)/shard_map/all_to_all | solution.py:52
  146.4 3.7 %all-to-all-done.4 = bf16[8,32,896]{2,1,0:T(8,128)(2,1)} async-done(((bf16[8,32,896]{2,1,0:T(8,128)(2,1)}), bf16[8,32,896]{2,1,0:T(8,128)(2,1)}, u32[]{:S(2)}, u32[]{:S(2)}) %all-to-all-start.4) | async-done | bytes 458784 | tf_op jit(solution)/shard_map/all_to_all | solution.py:52
  150.1 3.5 %all-to-all-start.9 = ((bf16[8,32,896]{2,1,0:T(8,128)(2,1)}), bf16[8,32,896]{2,1,0:T(8,128)(2,1)S(1)}, u32[]{:S(2)}, u32[]{:S(2)}) async-start(bf16[8,32,896]{2,1,0:T(8,128)(2,1)} %bitcast.33), calls=%async_computation.9 | async-start | bytes 917504 | tf_op jit(solution)/shard_map/all_to_all | solution.py:52
  158.6 4.6 %collective-permute-start.3 = (bf16[128,896]{1,0:T(8,128)(2,1)S(1)}, bf16[128,896]{1,0:T(8,128)(2,1)S(1)}, u32[]{:S(2)}, u32[]{:S(2)}) collective-permute-start(bf16[128,896]{1,0:T(8,128)(2,1)S(1)} %slice.33), channel_id=1, source_target_pairs={{0,3},{1,0},{2,1},{3,2},{4,7},{5,4},{6,5},{7,6},{8,11},{9,8},{10,9... | collective-permute-start | bytes 688136 | tf_op jit(solution)/shard_map/ppermute | solution.py:13
  168.9 6.6 %all-to-all-start.2 = ((bf16[8,32,896]{2,1,0:T(8,128)(2,1)}), bf16[8,32,896]{2,1,0:T(8,128)(2,1)S(1)}, u32[]{:S(2)}, u32[]{:S(2)}) async-start(bf16[8,32,896]{2,1,0:T(8,128)(2,1)} %bitcast.9), calls=%async_computation.2 | async-start | bytes 917504 | tf_op jit(solution)/shard_map/all_to_all | solution.py:52
  176.6 10.0 %all-to-all-done.2 = bf16[8,32,896]{2,1,0:T(8,128)(2,1)S(1)} async-done(((bf16[8,32,896]{2,1,0:T(8,128)(2,1)}), bf16[8,32,896]{2,1,0:T(8,128)(2,1)S(1)}, u32[]{:S(2)}, u32[]{:S(2)}) %all-to-all-start.2) | async-done | bytes 458784 | tf_op jit(solution)/shard_map/all_to_all | solution.py:52
  187.6 4.2 %all-to-all-start.5 = ((bf16[8,32,896]{2,1,0:T(8,128)(2,1)}), bf16[8,32,896]{2,1,0:T(8,128)(2,1)S(1)}, u32[]{:S(2)}, u32[]{:S(2)}) async-start(bf16[8,32,896]{2,1,0:T(8,128)(2,1)} %broadcast_in_dim.9), calls=%async_computation.5 | async-start | bytes 917504 | tf_op jit(solution)/shard_map/all_to_all | solution.py:17
  191.8 11.6 %all-to-all-done.5 = bf16[8,32,896]{2,1,0:T(8,128)(2,1)S(1)} async-done(((bf16[8,32,896]{2,1,0:T(8,128)(2,1)}), bf16[8,32,896]{2,1,0:T(8,128)(2,1)S(1)}, u32[]{:S(2)}, u32[]{:S(2)}) %all-to-all-start.5) | async-done | bytes 458784 | tf_op jit(solution)/shard_map/all_to_all | solution.py:17
  204.4 3.6 %all-to-all-start.10 = ((bf16[8,32,1792]{2,1,0:T(8,128)(2,1)}), bf16[8,32,1792]{2,1,0:T(8,128)(2,1)S(1)}, u32[]{:S(2)}, u32[]{:S(2)}) async-start(bf16[8,32,1792]{2,1,0:T(8,128)(2,1)} %broadcast_in_dim.11), calls=%async_computation.10 | async-start | bytes 1835008 | tf_op jit(solution)/shard_map/all_to_all | solution.py:17
  221.6 6.8 %all-to-all-done.10 = bf16[8,32,1792]{2,1,0:T(8,128)(2,1)S(1)} async-done(((bf16[8,32,1792]{2,1,0:T(8,128)(2,1)}), bf16[8,32,1792]{2,1,0:T(8,128)(2,1)S(1)}, u32[]{:S(2)}, u32[]{:S(2)}) %all-to-all-start.10) | async-done | bytes 917536 | tf_op jit(solution)/shard_map/all_to_all | solution.py:17
  228.4 12.3 %all-to-all-start.7 = ((bf16[16,128,128]{2,1,0:T(8,128)(2,1)}), bf16[16,128,128]{2,1,0:T(8,128)(2,1)S(1)}, u32[]{:S(2)}, u32[]{:S(2)}) async-start(bf16[16,128,128]{2,1,0:T(8,128)(2,1)} %bitcast.68), calls=%async_computation.7 | async-start | bytes 1048576 | tf_op jit(solution)/shard_map/all_to_all | solution.py:63
  245.7 12.4 %all-to-all-done.7 = bf16[16,128,128]{2,1,0:T(8,128)(2,1)S(1)} async-done(((bf16[16,128,128]{2,1,0:T(8,128)(2,1)}), bf16[16,128,128]{2,1,0:T(8,128)(2,1)S(1)}, u32[]{:S(2)}, u32[]{:S(2)}) %all-to-all-start.7) | async-done | bytes 524320 | tf_op jit(solution)/shard_map/all_to_all | solution.py:63
  262.2 16.0 %all-to-all-done.11 = bf16[16,128,128]{2,1,0:T(8,128)(2,1)S(1)} async-done(((bf16[16,128,128]{2,1,0:T(8,128)(2,1)}), bf16[16,128,128]{2,1,0:T(8,128)(2,1)S(1)}, u32[]{:S(2)}, u32[]{:S(2)}) %all-to-all-start.11) | async-done | bytes 524320 | tf_op jit(solution)/shard_map/all_to_all | solution.py:63
  (113 shorter events, 76.8 us)
Async XLA Ops:
  2.7 21.4 %all-to-all-start.3 = ((bf16[128,2,896]{0,2,1:T(8,128)(2,1)}), bf16[128,2,896]{0,2,1:T(8,128)(2,1)S(1)}, u32[]{:S(2)}, u32[]{:S(2)}) async-start(bf16[128,2,896]{0,2,1:T(8,128)(2,1)} %bitcast.10), calls=%async_computation.3 | async-start | bytes 917504 | tf_op jit(solution)/shard_map/all_to_all | solution.py:26
  24.1 12.5 %all-to-all-start.6 = ((bf16[128,2,896]{2,0,1:T(8,128)(2,1)}), bf16[128,2,896]{2,0,1:T(8,128)(2,1)S(1)}, u32[]{:S(2)}, u32[]{:S(2)}) async-start(bf16[128,2,896]{2,0,1:T(8,128)(2,1)} %copy.43), calls=%async_computation.6 | async-start | bytes 917504 | tf_op jit(solution)/shard_map/all_to_all | solution.py:26
  51.1 36.5 %copy-start.11 = (bf16[128,128]{1,0:T(8,128)(2,1)S(1)}, bf16[128,128]{1,0:T(8,128)(2,1)}, u32[]{:S(2)}) copy-start(bf16[128,128]{1,0:T(8,128)(2,1)} %param.11) | copy-start | bytes 98308
  51.1 36.4 %all-to-all-start = ((bf16[16,128,128]{2,1,0:T(8,128)(2,1)}), bf16[16,128,128]{2,1,0:T(8,128)(2,1)S(1)}, u32[]{:S(2)}, u32[]{:S(2)}) async-start(bf16[16,128,128]{2,1,0:T(8,128)(2,1)} %broadcast_in_dim.8), calls=%async_computation | async-start | bytes 1048576 | tf_op jit(solution)/shard_map/all_to_all | solution.py:17
  70.5 27.1 %collective-permute-start.4 = (bf16[256,896]{1,0:T(8,128)(2,1)}, bf16[256,896]{1,0:T(8,128)(2,1)}, u32[]{:S(2)}, u32[]{:S(2)}) collective-permute-start(bf16[256,896]{1,0:T(8,128)(2,1)} %bitcast.12), channel_id=1, source_target_pairs={{0,1},{1,2},{2,3},{3,0},{4,5},{5,6},{6,7},{7,4},{8,9},{9,10},{10,1... | collective-permute-start | bytes 1376264 | tf_op jit(solution)/shard_map/ppermute | solution.py:13
  73.6 30.6 %collective-permute-start.5 = (bf16[256,896]{1,0:T(8,128)(2,1)}, bf16[256,896]{1,0:T(8,128)(2,1)}, u32[]{:S(2)}, u32[]{:S(2)}) collective-permute-start(bf16[256,896]{1,0:T(8,128)(2,1)} %bitcast.12), channel_id=1, source_target_pairs={{0,3},{1,0},{2,1},{3,2},{4,7},{5,4},{6,5},{7,6},{8,11},{9,8},{10,9... | collective-permute-start | bytes 1376264 | tf_op jit(solution)/shard_map/ppermute | solution.py:13
  76.9 30.8 %collective-permute-start.8 = (bf16[256,896]{1,0:T(8,128)(2,1)S(1)}, bf16[256,896]{1,0:T(8,128)(2,1)}, u32[]{:S(2)}, u32[]{:S(2)}) collective-permute-start(bf16[256,896]{1,0:T(8,128)(2,1)S(1)} %bitcast.70), channel_id=1, source_target_pairs={{0,1},{1,2},{2,3},{3,0},{4,5},{5,6},{6,7},{7,4},{8,9},{9,10},{10,1... | collective-permute-start | bytes 1376264 | tf_op jit(solution)/shard_map/ppermute | solution.py:13
  78.9 35.1 %collective-permute-start.9 = (bf16[256,896]{1,0:T(8,128)(2,1)S(1)}, bf16[256,896]{1,0:T(8,128)(2,1)}, u32[]{:S(2)}, u32[]{:S(2)}) collective-permute-start(bf16[256,896]{1,0:T(8,128)(2,1)S(1)} %bitcast.71), channel_id=1, source_target_pairs={{0,3},{1,0},{2,1},{3,2},{4,7},{5,4},{6,5},{7,6},{8,11},{9,8},{10,9... | collective-permute-start | bytes 1376264 | tf_op jit(solution)/shard_map/ppermute | solution.py:13
  84.5 70.2 %collective-permute-start = (bf16[256,896]{1,0:T(8,128)(2,1)}, bf16[256,896]{1,0:T(8,128)(2,1)}, u32[]{:S(2)}, u32[]{:S(2)}) collective-permute-start(bf16[256,896]{1,0:T(8,128)(2,1)} %bitcast.8), channel_id=1, source_target_pairs={{0,1},{1,2},{2,3},{3,0},{4,5},{5,6},{6,7},{7,4},{8,9},{9,10},{10,1... | collective-permute-start | bytes 1376264 | tf_op jit(solution)/shard_map/ppermute | solution.py:13
  88.4 40.3 %all-to-all-start.8 = ((bf16[16,128,128]{2,1,0:T(8,128)(2,1)}), bf16[16,128,128]{2,1,0:T(8,128)(2,1)S(1)}, u32[]{:S(2)}, u32[]{:S(2)}) async-start(bf16[16,128,128]{2,1,0:T(8,128)(2,1)} %broadcast_in_dim.10), calls=%async_computation.8 | async-start | bytes 1048576 | tf_op jit(solution)/shard_map/all_to_all | solution.py:17
  97.6 60.0 %collective-permute-start.1 = (bf16[256,896]{1,0:T(8,128)(2,1)}, bf16[256,896]{1,0:T(8,128)(2,1)}, u32[]{:S(2)}, u32[]{:S(2)}) collective-permute-start(bf16[256,896]{1,0:T(8,128)(2,1)} %bitcast.8), channel_id=1, source_target_pairs={{0,3},{1,0},{2,1},{3,2},{4,7},{5,4},{6,5},{7,6},{8,11},{9,8},{10,9... | collective-permute-start | bytes 1376264 | tf_op jit(solution)/shard_map/ppermute | solution.py:13
  104.1 16.5 %collective-permute-start.6 = (bf16[128,896]{1,0:T(8,128)(2,1)}, bf16[128,896]{1,0:T(8,128)(2,1)}, u32[]{:S(2)}, u32[]{:S(2)}) collective-permute-start(bf16[128,896]{1,0:T(8,128)(2,1)} %slice.34), channel_id=1, source_target_pairs={{0,1},{1,2},{2,3},{3,0},{4,5},{5,6},{6,7},{7,4},{8,9},{9,10},{10,1... | collective-permute-start | bytes 688136 | tf_op jit(solution)/shard_map/ppermute | solution.py:13
  107.7 18.5 %collective-permute-start.7 = (bf16[128,896]{1,0:T(8,128)(2,1)}, bf16[128,896]{1,0:T(8,128)(2,1)}, u32[]{:S(2)}, u32[]{:S(2)}) collective-permute-start(bf16[128,896]{1,0:T(8,128)(2,1)} %slice.35), channel_id=1, source_target_pairs={{0,3},{1,0},{2,1},{3,2},{4,7},{5,4},{6,5},{7,6},{8,11},{9,8},{10,9... | collective-permute-start | bytes 688136 | tf_op jit(solution)/shard_map/ppermute | solution.py:13
  114.0 26.2 %collective-permute-start.10 = (bf16[128,896]{1,0:T(8,128)(2,1)}, bf16[128,896]{1,0:T(8,128)(2,1)}, u32[]{:S(2)}, u32[]{:S(2)}) collective-permute-start(bf16[128,896]{1,0:T(8,128)(2,1)} %slice.36), channel_id=1, source_target_pairs={{0,1},{1,2},{2,3},{3,0},{4,5},{5,6},{6,7},{7,4},{8,9},{9,10},{10,1... | collective-permute-start | bytes 688136 | tf_op jit(solution)/shard_map/ppermute | solution.py:13
  120.6 21.2 %collective-permute-start.11 = (bf16[128,896]{1,0:T(8,128)(2,1)}, bf16[128,896]{1,0:T(8,128)(2,1)}, u32[]{:S(2)}, u32[]{:S(2)}) collective-permute-start(bf16[128,896]{1,0:T(8,128)(2,1)} %slice.37), channel_id=1, source_target_pairs={{0,3},{1,0},{2,1},{3,2},{4,7},{5,4},{6,5},{7,6},{8,11},{9,8},{10,9... | collective-permute-start | bytes 688136 | tf_op jit(solution)/shard_map/ppermute | solution.py:13
  128.7 21.4 %all-to-all-start.4 = ((bf16[8,32,896]{2,1,0:T(8,128)(2,1)}), bf16[8,32,896]{2,1,0:T(8,128)(2,1)}, u32[]{:S(2)}, u32[]{:S(2)}) async-start(bf16[8,32,896]{2,1,0:T(8,128)(2,1)} %bitcast.13), calls=%async_computation.4 | async-start | bytes 917504 | tf_op jit(solution)/shard_map/all_to_all | solution.py:52
  150.1 18.8 %all-to-all-start.9 = ((bf16[8,32,896]{2,1,0:T(8,128)(2,1)}), bf16[8,32,896]{2,1,0:T(8,128)(2,1)S(1)}, u32[]{:S(2)}, u32[]{:S(2)}) async-start(bf16[8,32,896]{2,1,0:T(8,128)(2,1)} %bitcast.33), calls=%async_computation.9 | async-start | bytes 917504 | tf_op jit(solution)/shard_map/all_to_all | solution.py:52
  155.7 9.6 %collective-permute-start.2 = (bf16[128,896]{1,0:T(8,128)(2,1)S(1)}, bf16[128,896]{1,0:T(8,128)(2,1)S(1)}, u32[]{:S(2)}, u32[]{:S(2)}) collective-permute-start(bf16[128,896]{1,0:T(8,128)(2,1)S(1)} %slice.32), channel_id=1, source_target_pairs={{0,1},{1,2},{2,3},{3,0},{4,5},{5,6},{6,7},{7,4},{8,9},{9,10},{10,1... | collective-permute-start | bytes 688136 | tf_op jit(solution)/shard_map/ppermute | solution.py:13
  158.6 7.5 %collective-permute-start.3 = (bf16[128,896]{1,0:T(8,128)(2,1)S(1)}, bf16[128,896]{1,0:T(8,128)(2,1)S(1)}, u32[]{:S(2)}, u32[]{:S(2)}) collective-permute-start(bf16[128,896]{1,0:T(8,128)(2,1)S(1)} %slice.33), channel_id=1, source_target_pairs={{0,3},{1,0},{2,1},{3,2},{4,7},{5,4},{6,5},{7,6},{8,11},{9,8},{10,9... | collective-permute-start | bytes 688136 | tf_op jit(solution)/shard_map/ppermute | solution.py:13
  168.9 17.7 %all-to-all-start.2 = ((bf16[8,32,896]{2,1,0:T(8,128)(2,1)}), bf16[8,32,896]{2,1,0:T(8,128)(2,1)S(1)}, u32[]{:S(2)}, u32[]{:S(2)}) async-start(bf16[8,32,896]{2,1,0:T(8,128)(2,1)} %bitcast.9), calls=%async_computation.2 | async-start | bytes 917504 | tf_op jit(solution)/shard_map/all_to_all | solution.py:52
  187.6 15.8 %all-to-all-start.5 = ((bf16[8,32,896]{2,1,0:T(8,128)(2,1)}), bf16[8,32,896]{2,1,0:T(8,128)(2,1)S(1)}, u32[]{:S(2)}, u32[]{:S(2)}) async-start(bf16[8,32,896]{2,1,0:T(8,128)(2,1)} %broadcast_in_dim.9), calls=%async_computation.5 | async-start | bytes 917504 | tf_op jit(solution)/shard_map/all_to_all | solution.py:17
  204.4 24.0 %all-to-all-start.10 = ((bf16[8,32,1792]{2,1,0:T(8,128)(2,1)}), bf16[8,32,1792]{2,1,0:T(8,128)(2,1)S(1)}, u32[]{:S(2)}, u32[]{:S(2)}) async-start(bf16[8,32,1792]{2,1,0:T(8,128)(2,1)} %broadcast_in_dim.11), calls=%async_computation.10 | async-start | bytes 1835008 | tf_op jit(solution)/shard_map/all_to_all | solution.py:17
  228.4 29.7 %all-to-all-start.7 = ((bf16[16,128,128]{2,1,0:T(8,128)(2,1)}), bf16[16,128,128]{2,1,0:T(8,128)(2,1)S(1)}, u32[]{:S(2)}, u32[]{:S(2)}) async-start(bf16[16,128,128]{2,1,0:T(8,128)(2,1)} %bitcast.68), calls=%async_computation.7 | async-start | bytes 1048576 | tf_op jit(solution)/shard_map/all_to_all | solution.py:63
  258.1 20.2 %all-to-all-start.11 = ((bf16[16,128,128]{2,1,0:T(8,128)(2,1)}), bf16[16,128,128]{2,1,0:T(8,128)(2,1)S(1)}, u32[]{:S(2)}, u32[]{:S(2)}) async-start(bf16[16,128,128]{2,1,0:T(8,128)(2,1)} %bitcast.36), calls=%async_computation.11 | async-start | bytes 1048576 | tf_op jit(solution)/shard_map/all_to_all | solution.py:63
  (12 other events, 155.5 us)

commit v2 on v1

v2 whole, which is shorter than its diff:
```python
import jax
import jax.numpy as jnp
from jax import lax
from jax.experimental import pallas as pl
from jax.experimental.pallas import tpu as pltpu
from jax.sharding import Mesh, PartitionSpec as P

AXES = ("y", "zl", "core", "zh", "x")
RING = ("zh", "zl", "core")
NT = (((1,), (1,)), ((), ()))
F32, BF16 = jnp.float32, jnp.bfloat16
STEPS = (0, 3, 1, 2)


def shift(values, step):
    return lax.ppermute(values, "x", [(i, (i + step) % 4) for i in range(4)])


def swap(weight, zh):
    low, high = weight[:, :896], weight[:, 896:]
    other = lax.ppermute(jnp.where(zh == 0, high, low), "zh", [(0, 1), (1, 0)])
    return jnp.concatenate([jnp.where(zh == 0, low, high), other], axis=0)


def gather(block, by_left):
    left, right = shift(block, 1), shift(block, -1)
    far = shift(left, 1) if by_left else shift(right, -1)
    return block, left, right, far


def feature_block(place, slot, row):
    return ((place[1] + row) % 2) * 4 + (place[0] + STEPS[slot]) % 4


def partial_kernel(which, place, acts, b0, b1, b2, b3, out):
    total = None
    for slot, block in enumerate((b0, b1, b2, b3)):
        f0, f1 = feature_block(place, slot, 0), feature_block(place, slot, 1)
        wide = jnp.concatenate(
            [jnp.concatenate([acts[8 * t + f0, 0], acts[8 * t + f1, 0]], axis=1) for t in (0, 1)], axis=0
        )
        term = jnp.dot(wide, block[...], preferred_element_type=F32)
        total = term if total is None else total + term
    out[...] = total.astype(BF16)


def partial_value(which, place, acts, blocks):
    whole = pl.BlockSpec((256, 896), lambda i: (0, 0))
    return pl.pallas_call(
        lambda *refs: partial_kernel(which, *refs),
        grid=(1,),
        out_shape=jax.ShapeDtypeStruct((256, 896), BF16),
        in_specs=[
            pl.BlockSpec(memory_space=pltpu.SMEM),
            pl.BlockSpec((16, 1, 128, 128), lambda i: (0, which, 0, 0)),
            whole, whole, whole, whole,
        ],
        out_specs=whole,
        cost_estimate=pl.CostEstimate(flops=2 * 256 * 1024 * 896, bytes_accessed=3000000, transcendentals=0),
        compiler_params=pltpu.CompilerParams(vmem_limit_bytes=16 << 20),
    )(place, acts, *blocks)


def output_kernel(place, acts, *refs):
    gate, up, down, out = refs[:4], refs[4:8], refs[8:12], refs[12]
    hidden, gate_grad, up_grad = (acts[:, k].reshape(256, 896) for k in range(3))
    for slot in range(4):
        mixed = lax.dot_general(hidden, down[slot][...], NT, preferred_element_type=F32)
        grad = lax.dot_general(gate_grad, gate[slot][...], NT, preferred_element_type=F32)
        grad = grad + lax.dot_general(up_grad, up[slot][...], NT, preferred_element_type=F32)
        for row in (0, 1):
            f = feature_block(place, slot, row)
            for t in (0, 1):
                part = (slice(128 * t, 128 * t + 128), slice(128 * row, 128 * row + 128))
                out[8 * t + f, 0] = mixed[part].astype(BF16)
                out[8 * t + f, 1] = grad[part].astype(BF16)


def output_terms(place, acts, blocks):
    whole = pl.BlockSpec((256, 896), lambda i: (0, 0))
    return pl.pallas_call(
        output_kernel,
        grid=(1,),
        out_shape=jax.ShapeDtypeStruct((16, 2, 128, 128), BF16),
        in_specs=[pl.BlockSpec(memory_space=pltpu.SMEM), pl.BlockSpec((8, 3, 32, 896), lambda i: (0, 0, 0, 0))] + [whole] * 12,
        out_specs=pl.BlockSpec((16, 2, 128, 128), lambda i: (0, 0, 0, 0)),
        cost_estimate=pl.CostEstimate(flops=6 * 256 * 1024 * 896, bytes_accessed=8000000, transcendentals=0),
        compiler_params=pltpu.CompilerParams(vmem_limit_bytes=32 << 20),
    )(place, acts, *blocks)


def combine(partial):
    parts = lax.all_to_all(partial.reshape(8, 32, 896), "y", 0, 0, tiled=True)
    return jnp.sum(parts.astype(F32), axis=0)


def on_device(tokens, gate_weight, up_weight, down_weight, grad_mixed):
    x, zh = lax.axis_index("x"), lax.axis_index("zh")
    place = jnp.stack([x, zh])
    acts = lax.all_gather(jnp.stack([tokens, grad_mixed]), RING, axis=0)
    gate = gather(swap(gate_weight, zh), True)
    gate_value = combine(partial_value(0, place, acts, gate))
    up = gather(swap(up_weight, zh), False)
    up_value = combine(partial_value(0, place, acts, up))
    down = gather(swap(down_weight, zh), True)
    hidden_grad = combine(partial_value(1, place, acts, down))
    sig = jax.nn.sigmoid(gate_value)
    silu = gate_value * sig
    hidden = (silu * up_value).astype(BF16)
    gate_grad = (hidden_grad * up_value * sig * (1.0 + gate_value * (1.0 - sig))).astype(BF16)
    up_grad = (hidden_grad * silu).astype(BF16)
    rows = jnp.stack([hidden, gate_grad, up_grad])
    rows = lax.all_to_all(jnp.broadcast_to(rows[None], (8, 3, 32, 896)), "y", 0, 0, tiled=True)
    terms = lax.all_to_all(output_terms(place, rows, (*gate, *up, *down)), RING, 0, 0, tiled=True)
    both = jnp.sum(terms.astype(F32), axis=0).astype(BF16)
    return both[0], both[1]


def solution(mesh):
    fine = Mesh(mesh.devices.reshape(8, 4, 2, 2, 4), AXES)
    acts = P(("zh", "x"), ("y", "zl", "core"))
    weights = P(("y", "zh", "x"), ("zl", "core"))
    return jax.shard_map(
        on_device,
        mesh=fine,
        in_specs=(acts, weights, weights, weights, acts),
        out_specs=(acts, acts),
        check_vma=False,
    )
```

time: 281 us -> 229 us (0.81)
  blocking collectives: 13.6 us -> 72.1 us
  starting transfers between devices: 121 us -> 74.8 us
  local copies, waits for them, and re-layouts: 43.9 us -> 5.09 us
  waiting for transfers between devices: 79.1 us -> 45.3 us
  Pallas kernels: 0 us -> 10.1 us
  matrix products: 9.73 us -> 0 us
  between operations: 8.96 us -> 14.3 us
  other arithmetic: 2.84 us -> 6.39 us
    all_to_all x11 -> x3, waiting for transfers between devices: 78.3 us -> 8.85 us  [combine(): parts = lax.all_to_all(partial.reshape(8, 32, 896), 'y', 0, 0, tiled=True)]
    all_to_all x11 -> x3, starting transfers between devices: 81.6 us -> 18.9 us  [combine(): parts = lax.all_to_all(partial.reshape(8, 32, 896), 'y', 0, 0, tiled=True)]
    all_to_all x1 -> x2, blocking collectives: 13.6 us -> 72.1 us  [the longest x1 36.9 us: on_device(): lax.all_to_all(output_terms(place, rows, (*gate, *up, *down)), RING, 0, 0...]
    ppermute x0 -> x3, starting transfers between devices: none -> 23.8 us  [swap(): other = lax.ppermute(jnp.where(zh == 0, high, low), 'zh', [(0, 1), (1, 0)])]
    ppermute x12 -> x9, waiting for transfers between devices: 0.78 us -> 21 us  [shift(): return lax.ppermute(values, 'x', [(i, (i + step) % 4) for i in range(4)])]
    unnamed x45 -> x26, local copies, waits for them, and re-layouts: 18.2 us -> 4.36 us
    all_gather x0 -> x1, waiting for transfers between devices: none -> 10.4 us  [on_device(): acts = lax.all_gather(jnp.stack([tokens, grad_mixed]), RING, axis=0)]
    pallas_call x0 -> x4, Pallas kernels: none -> 10.1 us  [the longest x3 7.13 us: partial_value(): pl.pallas_call(lambda *refs: partial_kernel(which, *refs), grid=(1,), out...]
  transfers between devices with their start and end apart: 23 -> 16, of which waited for: 9 -> 8; matrix products, arithmetic and copies ran while one was open for 18% -> 2% of each run, Pallas kernels for 0% -> 3%
where the time goes in v2:
time: 229 us; the launch traced here: 228 us
  starting transfers between devices  74.8 us (33%)
  blocking collectives  72.1 us (31%)
  waiting for transfers between devices  45.3 us (20%)
  between operations  14.3 us (6%)
  Pallas kernels  10.1 us (4%)
  other arithmetic  6.39 us (3%)
  local copies, waits for them, and re-layouts  5.09 us (2%)
    all_to_all x1, blocking collectives, on_device(): lax.all_to_all(output_terms(place, rows, (*gate, *up, *down)), RING, 0, 0...  36.9 us
    all_to_all x1, blocking collectives, on_device(): lax.all_to_all(jnp.broadcast_to(rows[None], (8, 3, 32, 896)), 'y', 0, 0,...  35.1 us
    ppermute x9, starting transfers between devices, shift(): return lax.ppermute(values, 'x', [(i, (i + step) % 4) for i in range(4)])  32.1 us
    ppermute x3, starting transfers between devices, swap(): other = lax.ppermute(jnp.where(zh == 0, high, low), 'zh', [(0, 1), (1, 0)])  23.8 us
    ppermute x9, waiting for transfers between devices, shift(): return lax.ppermute(values, 'x', [(i, (i + step) % 4) for i in range(4)])  21 us
    all_to_all x3, starting transfers between devices, combine(): parts = lax.all_to_all(partial.reshape(8, 32, 896), 'y', 0, 0, tiled=True)  18.9 us
    all_gather x1, waiting for transfers between devices, on_device(): acts = lax.all_gather(jnp.stack([tokens, grad_mixed]), RING, axis=0)  10.4 us
    all_to_all x3, waiting for transfers between devices, combine(): parts = lax.all_to_all(partial.reshape(8, 32, 896), 'y', 0, 0, tiled=True)  8.85 us
  transfers between devices with their start and end apart: 16, of which 8 were waited for; matrix products, arithmetic and copies ran while one was open for 2% of the time, Pallas kernels for 3%

profile of v2, /device:TPU:1, one launch (start us, length us, event | category | flops | bytes accessed | tf_op | source)
XLA Modules:
  0.0 228.1 jit_solution(13663170484764405938)
XLA Ops:
  9.8 11.5 %collective-permute-start.8 = (bf16[128,896]{1,0:T(8,128)(2,1)S(1)}, bf16[128,896]{1,0:T(8,128)(2,1)S(1)}, u32[]{:S(2)}, u32[]{:S(2)}) collective-permute-start(bf16[128,896]{1,0:T(8,128)(2,1)S(1)} %get-tuple-element.7), channel_id=1, source_target_pairs={{0,4},{4,0},{1,5},{5,1},{2,6},{6,2},{3,7},{7,3},{8,12},{12,8},{9,1... | collective-permute-start | bytes 688136 | tf_op jit(solution)/shard_map/ppermute | solution.py:21
  21.3 5.1 %collective-permute-done.8 = bf16[128,896]{1,0:T(8,128)(2,1)S(1)} collective-permute-done((bf16[128,896]{1,0:T(8,128)(2,1)S(1)}, bf16[128,896]{1,0:T(8,128)(2,1)S(1)}, u32[]{:S(2)}, u32[]{:S(2)}) %collective-permute-start.8) | collective-permute-done | bytes 229408 | tf_op jit(solution)/shard_map/ppermute | solution.py:21
  26.4 3.3 %collective-permute-start.9 = (bf16[256,896]{1,0:T(8,128)(2,1)S(1)}, bf16[256,896]{1,0:T(8,128)(2,1)S(1)}, u32[]{:S(2)}, u32[]{:S(2)}) collective-permute-start(bf16[256,896]{1,0:T(8,128)(2,1)S(1)} %pad_maximum_fusion.2.refs_2_.refs_8_), channel_id=1, source_target_pairs={{0,1},{1,2},{2,3},{3,0},{4,5},{5,6},{6,7},{7,4},{8,9},{9,10},{10,1... | collective-permute-start | bytes 1376264 | tf_op jit(solution)/shard_map/ppermute | solution.py:16
  29.8 7.1 %collective-permute-start.4 = (bf16[128,896]{1,0:T(8,128)(2,1)S(1)}, bf16[128,896]{1,0:T(8,128)(2,1)S(1)}, u32[]{:S(2)}, u32[]{:S(2)}) collective-permute-start(bf16[128,896]{1,0:T(8,128)(2,1)S(1)} %get-tuple-element.3), channel_id=1, source_target_pairs={{0,4},{4,0},{1,5},{5,1},{2,6},{6,2},{3,7},{7,3},{8,12},{12,8},{9,1... | collective-permute-start | bytes 688136 | tf_op jit(solution)/shard_map/ppermute | solution.py:21
  36.9 4.1 %collective-permute-start.10 = (bf16[256,896]{1,0:T(8,128)(2,1)S(1)}, bf16[256,896]{1,0:T(8,128)(2,1)S(1)}, u32[]{:S(2)}, u32[]{:S(2)}) collective-permute-start(bf16[256,896]{1,0:T(8,128)(2,1)S(1)} %pad_maximum_fusion.2.refs_2_.refs_8_), channel_id=1, source_target_pairs={{0,3},{1,0},{2,1},{3,2},{4,7},{5,4},{6,5},{7,6},{8,11},{9,8},{10,9... | collective-permute-start | bytes 1376264 | tf_op jit(solution)/shard_map/ppermute | solution.py:16
  43.0 4.6 %collective-permute-start.6 = (bf16[256,896]{1,0:T(8,128)(2,1)S(1)}, bf16[256,896]{1,0:T(8,128)(2,1)}, u32[]{:S(2)}, u32[]{:S(2)}) collective-permute-start(bf16[256,896]{1,0:T(8,128)(2,1)S(1)} %pad_maximum_fusion.1.refs_2_.refs_4_), channel_id=1, source_target_pairs={{0,3},{1,0},{2,1},{3,2},{4,7},{5,4},{6,5},{7,6},{8,11},{9,8},{10,9... | collective-permute-start | bytes 1376264 | tf_op jit(solution)/shard_map/ppermute | solution.py:16
  47.7 4.2 %collective-permute-done.11.refs_5_.refs_11_ = bf16[256,896]{1,0:T(8,128)(2,1)S(1)} collective-permute-done((bf16[256,896]{1,0:T(8,128)(2,1)S(1)}, bf16[256,896]{1,0:T(8,128)(2,1)S(1)}, u32[]{:S(2)}, u32[]{:S(2)}) %collective-permute-start.11) | collective-permute-done | bytes 458784 | tf_op jit(solution)/shard_map/ppermute | solution.py:16
  51.9 10.4 %all-gather.3.cloned.1.call-done = bf16[32,128,128]{2,1,0:T(8,128)(2,1)} async-done(((bf16[2,128,128]{2,1,0:T(8,128)(2,1)}), bf16[32,128,128]{2,1,0:T(8,128)(2,1)}) %all-gather.3.cloned.1.call-update) | async-done | bytes 1048592 | tf_op jit(solution)/shard_map/all_gather | solution.py:100
  65.5 6.1 %all-to-all-start.2 = ((bf16[8,32,896]{2,1,0:T(8,128)(2,1)}), bf16[8,32,896]{2,1,0:T(8,128)(2,1)}, u32[]{:S(2)}, u32[]{:S(2)}) async-start(bf16[8,32,896]{2,1,0:T(8,128)(2,1)} %bitcast.9), calls=%async_computation.2 | async-start | bytes 917504 | tf_op jit(solution)/shard_map/all_to_all | solution.py:93
  72.7 5.2 %collective-permute-start = (bf16[128,896]{1,0:T(8,128)(2,1)S(1)}, bf16[128,896]{1,0:T(8,128)(2,1)S(1)}, u32[]{:S(2)}, u32[]{:S(2)}) collective-permute-start(bf16[128,896]{1,0:T(8,128)(2,1)S(1)} %get-tuple-element.5), channel_id=1, source_target_pairs={{0,4},{4,0},{1,5},{5,1},{2,6},{6,2},{3,7},{7,3},{8,12},{12,8},{9,1... | collective-permute-start | bytes 688136 | tf_op jit(solution)/shard_map/ppermute | solution.py:21
  78.0 4.8 %collective-permute-start.5 = (bf16[256,896]{1,0:T(8,128)(2,1)S(1)}, bf16[256,896]{1,0:T(8,128)(2,1)S(1)}, u32[]{:S(2)}, u32[]{:S(2)}) collective-permute-start(bf16[256,896]{1,0:T(8,128)(2,1)S(1)} %pad_maximum_fusion.1.refs_2_.refs_4_), channel_id=1, source_target_pairs={{0,1},{1,2},{2,3},{3,0},{4,5},{5,6},{6,7},{7,4},{8,9},{9,10},{10,1... | collective-permute-start | bytes 1376264 | tf_op jit(solution)/shard_map/ppermute | solution.py:16
  82.8 3.0 %collective-permute-start.7 = (bf16[256,896]{1,0:T(8,128)(2,1)}, bf16[256,896]{1,0:T(8,128)(2,1)S(1)}, u32[]{:S(2)}, u32[]{:S(2)}) collective-permute-start(bf16[256,896]{1,0:T(8,128)(2,1)} %collective-permute-done.6.refs_4_.refs_6_), channel_id=1, source_target_pairs={{0,3},{1,0},{2,1},{3,2},{4,7},{5,4},{6,5},{7,6},{8,11},{9,8},{10,9... | collective-permute-start | bytes 1376264 | tf_op jit(solution)/shard_map/ppermute | solution.py:16
  85.8 4.0 %collective-permute-start.1 = (bf16[256,896]{1,0:T(8,128)(2,1)S(1)}, bf16[256,896]{1,0:T(8,128)(2,1)}, u32[]{:S(2)}, u32[]{:S(2)}) collective-permute-start(bf16[256,896]{1,0:T(8,128)(2,1)S(1)} %pad_maximum_fusion.refs_2_.refs_0_), channel_id=1, source_target_pairs={{0,1},{1,2},{2,3},{3,0},{4,5},{5,6},{6,7},{7,4},{8,9},{9,10},{10,1... | collective-permute-start | bytes 1376264 | tf_op jit(solution)/shard_map/ppermute | solution.py:16
  89.9 4.1 %collective-permute-done.5.refs_3_.refs_5_ = bf16[256,896]{1,0:T(8,128)(2,1)S(1)} collective-permute-done((bf16[256,896]{1,0:T(8,128)(2,1)S(1)}, bf16[256,896]{1,0:T(8,128)(2,1)S(1)}, u32[]{:S(2)}, u32[]{:S(2)}) %collective-permute-start.5) | collective-permute-done | bytes 458784 | tf_op jit(solution)/shard_map/ppermute | solution.py:16
  99.9 6.4 %all-to-all-start.1 = ((bf16[8,32,896]{2,1,0:T(8,128)(2,1)}), bf16[8,32,896]{2,1,0:T(8,128)(2,1)}, u32[]{:S(2)}, u32[]{:S(2)}) async-start(bf16[8,32,896]{2,1,0:T(8,128)(2,1)} %bitcast.7), calls=%async_computation.1 | async-start | bytes 917504 | tf_op jit(solution)/shard_map/all_to_all | solution.py:93
  106.3 4.4 %collective-permute-start.2 = (bf16[256,896]{1,0:T(8,128)(2,1)S(1)}, bf16[256,896]{1,0:T(8,128)(2,1)S(1)}, u32[]{:S(2)}, u32[]{:S(2)}) collective-permute-start(bf16[256,896]{1,0:T(8,128)(2,1)S(1)} %pad_maximum_fusion.refs_2_.refs_0_), channel_id=1, source_target_pairs={{0,3},{1,0},{2,1},{3,2},{4,7},{5,4},{6,5},{7,6},{8,11},{9,8},{10,9... | collective-permute-start | bytes 1376264 | tf_op jit(solution)/shard_map/ppermute | solution.py:16
  112.7 5.5 %collective-permute-done.2.refs_4_.refs_2_ = bf16[256,896]{1,0:T(8,128)(2,1)S(1)} collective-permute-done((bf16[256,896]{1,0:T(8,128)(2,1)S(1)}, bf16[256,896]{1,0:T(8,128)(2,1)S(1)}, u32[]{:S(2)}, u32[]{:S(2)}) %collective-permute-start.2) | collective-permute-done | bytes 458784 | tf_op jit(solution)/shard_map/ppermute | solution.py:16
  118.3 5.3 %collective-permute-done.3.refs_5_.refs_3_ = bf16[256,896]{1,0:T(8,128)(2,1)S(1)} collective-permute-done((bf16[256,896]{1,0:T(8,128)(2,1)}, bf16[256,896]{1,0:T(8,128)(2,1)S(1)}, u32[]{:S(2)}, u32[]{:S(2)}) %collective-permute-start.3) | collective-permute-done | bytes 458784 | tf_op jit(solution)/shard_map/ppermute | solution.py:16
  123.5 2.6 %shard_map.68 = bf16[256,896]{1,0:T(8,128)(2,1)} custom-call(s32[2]{0:T(128)S(1)} %pad_add_fusion.refs_0_.place, bf16[16,2,128,128]{3,2,1,0:T(8,128)(2,1)S(1)} %bitcast.52, bf16[256,896]{1,0:T(8,128)(2,1)S(1)} %pad_maximum_fusion.refs_2_.refs_0_, bf16[256,896]{1,0:T(8,128)(2,1)} %collective-permute-done.1.refs_3_.refs_1_, ...), custom_call_target="tpu_custom_call" | custom-call | flops 469762048 | bytes 3000000 | tf_op jit(solution)/shard_map/pallas_call | solution.py:49
  127.6 6.4 %all-to-all-start = ((bf16[8,32,896]{2,1,0:T(8,128)(2,1)}), bf16[8,32,896]{2,1,0:T(8,128)(2,1)S(1)}, u32[]{:S(2)}, u32[]{:S(2)}) async-start(bf16[8,32,896]{2,1,0:T(8,128)(2,1)} %bitcast.5), calls=%async_computation | async-start | bytes 917504 | tf_op jit(solution)/shard_map/all_to_all | solution.py:93
  136.2 8.8 %all-to-all-done = bf16[8,32,896]{2,1,0:T(8,128)(2,1)S(1)} async-done(((bf16[8,32,896]{2,1,0:T(8,128)(2,1)}), bf16[8,32,896]{2,1,0:T(8,128)(2,1)S(1)}, u32[]{:S(2)}, u32[]{:S(2)}) %all-to-all-start) | async-done | bytes 458784 | tf_op jit(solution)/shard_map/all_to_all | solution.py:93
  145.4 35.1 %all_to_all.25.acts = bf16[8,3,32,896]{3,2,1,0:T(8,128)(2,1)S(1)} all-to-all(bf16[8,3,32,896]{3,2,1,0:T(8,128)(2,1)S(1)} %broadcast_in_dim.2), channel_id=1, replica_groups=mesh['y'=8,'zl'=4,'core'=2,'zh'=2,'x'=4] {'y'}, dimensions={0} | all-to-all | bytes 2752512 | tf_op jit(solution)/shard_map/all_to_all | solution.py:113
  180.5 3.0 %shard_map.71 = bf16[16,2,128,128]{3,2,1,0:T(8,128)(2,1)S(1)} custom-call(s32[2]{0:T(128)S(1)} %pad_add_fusion.refs_0_.place, bf16[8,3,32,896]{3,2,1,0:T(8,128)(2,1)S(1)} %all_to_all.25.acts, bf16[256,896]{1,0:T(8,128)(2,1)S(1)} %pad_maximum_fusion.refs_2_.refs_0_, bf16[256,896]{1,0:T(8,128)(2,1)} %collective-permute-done.1.refs_3_.refs_1_, ...), custom_call_target="tpu_custom_call" | custom-call | flops 1409286144 | bytes 8000000 | tf_op jit(solution)/shard_map/pallas_call | solution.py:81
  183.5 36.9 %all_to_all.26 = bf16[16,2,128,128]{3,2,1,0:T(8,128)(2,1)S(1)} all-to-all(bf16[16,2,128,128]{3,2,1,0:T(8,128)(2,1)S(1)} %shard_map.71), channel_id=1, replica_groups=mesh['y'=8,'zl'=4,'core'=2,'zh'=2,'x'=4] {'zh','zl','core'}, dimensions={0} | all-to-all | bytes 2097152 | tf_op jit(solution)/shard_map/all_to_all | solution.py:114
  (57 shorter events, 21.9 us)
Async XLA Ops:
  7.2 22.6 %copy-start.12 = (bf16[128,1792]{1,0:T(8,128)(2,1)S(1)}, bf16[128,1792]{1,0:T(8,128)(2,1)}, u32[]{:S(2)}) copy-start(bf16[128,1792]{1,0:T(8,128)(2,1)} %param.7) | copy-start | bytes 1376260
  7.2 55.1 %all-gather.3.cloned.1.call-start = ((), (), s32[]{:S(2)}) async-start(), calls=%async_computation.5 | async-start | bytes 1114112 | tf_op jit(solution)/shard_map/all_gather | solution.py:100
  9.8 16.6 %collective-permute-start.8 = (bf16[128,896]{1,0:T(8,128)(2,1)S(1)}, bf16[128,896]{1,0:T(8,128)(2,1)S(1)}, u32[]{:S(2)}, u32[]{:S(2)}) collective-permute-start(bf16[128,896]{1,0:T(8,128)(2,1)S(1)} %get-tuple-element.7), channel_id=1, source_target_pairs={{0,4},{4,0},{1,5},{5,1},{2,6},{6,2},{3,7},{7,3},{8,12},{12,8},{9,1... | collective-permute-start | bytes 688136 | tf_op jit(solution)/shard_map/ppermute | solution.py:21
  26.4 14.6 %collective-permute-start.9 = (bf16[256,896]{1,0:T(8,128)(2,1)S(1)}, bf16[256,896]{1,0:T(8,128)(2,1)S(1)}, u32[]{:S(2)}, u32[]{:S(2)}) collective-permute-start(bf16[256,896]{1,0:T(8,128)(2,1)S(1)} %pad_maximum_fusion.2.refs_2_.refs_8_), channel_id=1, source_target_pairs={{0,1},{1,2},{2,3},{3,0},{4,5},{5,6},{6,7},{7,4},{8,9},{9,10},{10,1... | collective-permute-start | bytes 1376264 | tf_op jit(solution)/shard_map/ppermute | solution.py:16
  29.8 13.1 %collective-permute-start.4 = (bf16[128,896]{1,0:T(8,128)(2,1)S(1)}, bf16[128,896]{1,0:T(8,128)(2,1)S(1)}, u32[]{:S(2)}, u32[]{:S(2)}) collective-permute-start(bf16[128,896]{1,0:T(8,128)(2,1)S(1)} %get-tuple-element.3), channel_id=1, source_target_pairs={{0,4},{4,0},{1,5},{5,1},{2,6},{6,2},{3,7},{7,3},{8,12},{12,8},{9,1... | collective-permute-start | bytes 688136 | tf_op jit(solution)/shard_map/ppermute | solution.py:21
  36.9 10.7 %collective-permute-start.10 = (bf16[256,896]{1,0:T(8,128)(2,1)S(1)}, bf16[256,896]{1,0:T(8,128)(2,1)S(1)}, u32[]{:S(2)}, u32[]{:S(2)}) collective-permute-start(bf16[256,896]{1,0:T(8,128)(2,1)S(1)} %pad_maximum_fusion.2.refs_2_.refs_8_), channel_id=1, source_target_pairs={{0,3},{1,0},{2,1},{3,2},{4,7},{5,4},{6,5},{7,6},{8,11},{9,8},{10,9... | collective-permute-start | bytes 1376264 | tf_op jit(solution)/shard_map/ppermute | solution.py:16
  41.0 10.8 %collective-permute-start.11 = (bf16[256,896]{1,0:T(8,128)(2,1)S(1)}, bf16[256,896]{1,0:T(8,128)(2,1)S(1)}, u32[]{:S(2)}, u32[]{:S(2)}) collective-permute-start(bf16[256,896]{1,0:T(8,128)(2,1)S(1)} %collective-permute-done.9.refs_3_.refs_9_), channel_id=1, source_target_pairs={{0,1},{1,2},{2,3},{3,0},{4,5},{5,6},{6,7},{7,4},{8,9},{9,10},{10,1... | collective-permute-start | bytes 1376264 | tf_op jit(solution)/shard_map/ppermute | solution.py:16
  43.0 39.8 %collective-permute-start.6 = (bf16[256,896]{1,0:T(8,128)(2,1)S(1)}, bf16[256,896]{1,0:T(8,128)(2,1)}, u32[]{:S(2)}, u32[]{:S(2)}) collective-permute-start(bf16[256,896]{1,0:T(8,128)(2,1)S(1)} %pad_maximum_fusion.1.refs_2_.refs_4_), channel_id=1, source_target_pairs={{0,3},{1,0},{2,1},{3,2},{4,7},{5,4},{6,5},{7,6},{8,11},{9,8},{10,9... | collective-permute-start | bytes 1376264 | tf_op jit(solution)/shard_map/ppermute | solution.py:16
  51.9 13.7 %copy-start.2 = (bf16[256,896]{1,0:T(8,128)(2,1)}, bf16[256,896]{1,0:T(8,128)(2,1)S(1)}, u32[]{:S(2)}) copy-start(bf16[256,896]{1,0:T(8,128)(2,1)S(1)} %collective-permute-done.11.refs_5_.refs_11_) | copy-start | bytes 1376260
  65.5 30.3 %copy-start.1 = (bf16[32,128,128]{2,1,0:T(8,128)(2,1)S(1)}, bf16[32,128,128]{2,1,0:T(8,128)(2,1)}, u32[]{:S(2)}) copy-start(bf16[32,128,128]{2,1,0:T(8,128)(2,1)} %all-gather.3.cloned.1.call-done) | copy-start | bytes 3145732
  65.5 34.4 %all-to-all-start.2 = ((bf16[8,32,896]{2,1,0:T(8,128)(2,1)}), bf16[8,32,896]{2,1,0:T(8,128)(2,1)}, u32[]{:S(2)}, u32[]{:S(2)}) async-start(bf16[8,32,896]{2,1,0:T(8,128)(2,1)} %bitcast.9), calls=%async_computation.2 | async-start | bytes 917504 | tf_op jit(solution)/shard_map/all_to_all | solution.py:93
  72.7 13.1 %collective-permute-start = (bf16[128,896]{1,0:T(8,128)(2,1)S(1)}, bf16[128,896]{1,0:T(8,128)(2,1)S(1)}, u32[]{:S(2)}, u32[]{:S(2)}) collective-permute-start(bf16[128,896]{1,0:T(8,128)(2,1)S(1)} %get-tuple-element.5), channel_id=1, source_target_pairs={{0,4},{4,0},{1,5},{5,1},{2,6},{6,2},{3,7},{7,3},{8,12},{12,8},{9,1... | collective-permute-start | bytes 688136 | tf_op jit(solution)/shard_map/ppermute | solution.py:21
  78.0 15.9 %collective-permute-start.5 = (bf16[256,896]{1,0:T(8,128)(2,1)S(1)}, bf16[256,896]{1,0:T(8,128)(2,1)S(1)}, u32[]{:S(2)}, u32[]{:S(2)}) collective-permute-start(bf16[256,896]{1,0:T(8,128)(2,1)S(1)} %pad_maximum_fusion.1.refs_2_.refs_4_), channel_id=1, source_target_pairs={{0,1},{1,2},{2,3},{3,0},{4,5},{5,6},{6,7},{7,4},{8,9},{9,10},{10,1... | collective-permute-start | bytes 1376264 | tf_op jit(solution)/shard_map/ppermute | solution.py:16
  82.8 13.0 %collective-permute-start.7 = (bf16[256,896]{1,0:T(8,128)(2,1)}, bf16[256,896]{1,0:T(8,128)(2,1)S(1)}, u32[]{:S(2)}, u32[]{:S(2)}) collective-permute-start(bf16[256,896]{1,0:T(8,128)(2,1)} %collective-permute-done.6.refs_4_.refs_6_), channel_id=1, source_target_pairs={{0,3},{1,0},{2,1},{3,2},{4,7},{5,4},{6,5},{7,6},{8,11},{9,8},{10,9... | collective-permute-start | bytes 1376264 | tf_op jit(solution)/shard_map/ppermute | solution.py:16
  85.8 24.9 %collective-permute-start.1 = (bf16[256,896]{1,0:T(8,128)(2,1)S(1)}, bf16[256,896]{1,0:T(8,128)(2,1)}, u32[]{:S(2)}, u32[]{:S(2)}) collective-permute-start(bf16[256,896]{1,0:T(8,128)(2,1)S(1)} %pad_maximum_fusion.refs_2_.refs_0_), channel_id=1, source_target_pairs={{0,1},{1,2},{2,3},{3,0},{4,5},{5,6},{6,7},{7,4},{8,9},{9,10},{10,1... | collective-permute-start | bytes 1376264 | tf_op jit(solution)/shard_map/ppermute | solution.py:16
  99.9 27.7 %all-to-all-start.1 = ((bf16[8,32,896]{2,1,0:T(8,128)(2,1)}), bf16[8,32,896]{2,1,0:T(8,128)(2,1)}, u32[]{:S(2)}, u32[]{:S(2)}) async-start(bf16[8,32,896]{2,1,0:T(8,128)(2,1)} %bitcast.7), calls=%async_computation.1 | async-start | bytes 917504 | tf_op jit(solution)/shard_map/all_to_all | solution.py:93
  106.3 11.9 %collective-permute-start.2 = (bf16[256,896]{1,0:T(8,128)(2,1)S(1)}, bf16[256,896]{1,0:T(8,128)(2,1)S(1)}, u32[]{:S(2)}, u32[]{:S(2)}) collective-permute-start(bf16[256,896]{1,0:T(8,128)(2,1)S(1)} %pad_maximum_fusion.refs_2_.refs_0_), channel_id=1, source_target_pairs={{0,3},{1,0},{2,1},{3,2},{4,7},{5,4},{6,5},{7,6},{8,11},{9,8},{10,9... | collective-permute-start | bytes 1376264 | tf_op jit(solution)/shard_map/ppermute | solution.py:16
  110.8 12.7 %collective-permute-start.3 = (bf16[256,896]{1,0:T(8,128)(2,1)}, bf16[256,896]{1,0:T(8,128)(2,1)S(1)}, u32[]{:S(2)}, u32[]{:S(2)}) collective-permute-start(bf16[256,896]{1,0:T(8,128)(2,1)} %collective-permute-done.1.refs_3_.refs_1_), channel_id=1, source_target_pairs={{0,1},{1,2},{2,3},{3,0},{4,5},{5,6},{6,7},{7,4},{8,9},{9,10},{10,1... | collective-permute-start | bytes 1376264 | tf_op jit(solution)/shard_map/ppermute | solution.py:16
  127.6 17.4 %all-to-all-start = ((bf16[8,32,896]{2,1,0:T(8,128)(2,1)}), bf16[8,32,896]{2,1,0:T(8,128)(2,1)S(1)}, u32[]{:S(2)}, u32[]{:S(2)}) async-start(bf16[8,32,896]{2,1,0:T(8,128)(2,1)} %bitcast.5), calls=%async_computation | async-start | bytes 917504 | tf_op jit(solution)/shard_map/all_to_all | solution.py:93
  145.3 35.2 %copy-start.3 = (bf16[256,896]{1,0:T(8,128)(2,1)S(1)}, bf16[256,896]{1,0:T(8,128)(2,1)}, u32[]{:S(2)}) copy-start(bf16[256,896]{1,0:T(8,128)(2,1)} %copy-done.2) | copy-start | bytes 1376260
  145.3 35.2 %copy-start.5 = (bf16[256,896]{1,0:T(8,128)(2,1)S(1)}, bf16[256,896]{1,0:T(8,128)(2,1)}, u32[]{:S(2)}) copy-start(bf16[256,896]{1,0:T(8,128)(2,1)} %copy-done.4) | copy-start | bytes 1376260
  145.3 35.2 %copy-start.7 = (bf16[256,896]{1,0:T(8,128)(2,1)S(1)}, bf16[256,896]{1,0:T(8,128)(2,1)}, u32[]{:S(2)}) copy-start(bf16[256,896]{1,0:T(8,128)(2,1)} %copy-done.6) | copy-start | bytes 1376260
  145.4 35.2 %copy-start.9 = (bf16[256,896]{1,0:T(8,128)(2,1)S(1)}, bf16[256,896]{1,0:T(8,128)(2,1)}, u32[]{:S(2)}) copy-start(bf16[256,896]{1,0:T(8,128)(2,1)} %copy-done.8) | copy-start | bytes 1376260
  145.4 35.2 %copy-start.11 = (bf16[256,896]{1,0:T(8,128)(2,1)S(1)}, bf16[256,896]{1,0:T(8,128)(2,1)}, u32[]{:S(2)}) copy-start(bf16[256,896]{1,0:T(8,128)(2,1)} %copy-done.10) | copy-start | bytes 1376260
  (5 other events, 4.3 us)
Sparse Core Ops, SparseCore 0:
  10.1 52.0 all-gather.2

commit v3 on v1

v3 whole, which is shorter than its diff:
```python
import jax
import jax.numpy as jnp
from jax import lax
from jax.experimental import pallas as pl
from jax.experimental.pallas import tpu as pltpu
from jax.sharding import Mesh, PartitionSpec as P

AXES = ("y", "zl", "core", "zh", "x")
RING = ("zh", "zl", "core")
NT = (((1,), (1,)), ((), ()))
F32, BF16 = jnp.float32, jnp.bfloat16
STEPS = (0, 3, 1, 2)
GATE, DOWN, UP = 0, 1, 2
SMEM = pl.BlockSpec(memory_space=pltpu.SMEM)


def whole(*shape):
    return pl.BlockSpec(shape, lambda i: (0,) * len(shape))


def call(kernel, out_shapes, in_specs, flops, moved):
    return pl.pallas_call(
        kernel,
        grid=(1,),
        out_shape=[jax.ShapeDtypeStruct(s, BF16) for s in out_shapes],
        in_specs=[SMEM, *in_specs],
        out_specs=[whole(*s) for s in out_shapes],
        cost_estimate=pl.CostEstimate(flops=flops, bytes_accessed=moved, transcendentals=0),
        compiler_params=pltpu.CompilerParams(vmem_limit_bytes=32 << 20),
    )


def shift(values, step):
    return lax.ppermute(values, "x", [(i, (i + step) % 4) for i in range(4)])


def exchange(values, axis):
    return lax.ppermute(values, axis, [(0, 1), (1, 0)])


def split_kernel(place, gate, down, up, keep, send_gate, send_two):
    low = place[1] == 0
    for k, weight in enumerate((gate, down, up)):
        left, right = weight[:, :896], weight[:, 896:]
        keep[k] = jnp.where(low, left, right)
        away = jnp.where(low, right, left)
        if k == GATE:
            send_gate[0] = away
        else:
            send_two[k - 1] = away


def feature(place, own, x):
    return ((place[1] + (0 if own else 1)) % 2) * 4 + x


def act_tile(place, near, other, which, t, f):
    k = 4 * t + f // 2
    return jnp.where(f % 2 == place[2], near[k, which], other[k, which])


def fill(place, near, other, which, wide):
    for t in (0, 1):
        for slot in range(4):
            rows = pl.ds(128 * t, 128)
            wide[rows, pl.ds(128 * slot, 128)] = act_tile(place, near, other, which, t, feature(place, True, slot))
            x = (place[0] + STEPS[slot]) % 4
            wide[rows, pl.ds(512 + 128 * slot, 128)] = act_tile(place, near, other, which, t, feature(place, False, x))


def contract(wide, kept, moved):
    total = jnp.dot(wide[:, :512], kept.reshape(512, 896), preferred_element_type=F32)
    first, second = jnp.concatenate(moved[:2], axis=0), jnp.concatenate(moved[2:], axis=0)
    total = total + jnp.dot(wide[:, 512:768], first, preferred_element_type=F32)
    return total + jnp.dot(wide[:, 768:], second, preferred_element_type=F32)


def gate_kernel(place, near, other, kept, m0, m1, m2, m3, out, wide):
    fill(place, near, other, 0, wide)
    total = contract(wide, kept[:, 0], [m[0] for m in (m0, m1, m2, m3)])
    out[...] = total.astype(BF16).reshape(8, 32, 896)


def two_kernel(place, near, other, kept, m0, m1, m2, far_down, far_up, out, wide):
    for k, (which, far) in enumerate(((1, far_down), (0, far_up))):
        fill(place, near, other, which, wide)
        total = contract(wide, kept[:, k + 1], [m0[k], m1[k], m2[k], far[0]])
        out[:, k] = total.astype(BF16).reshape(8, 32, 896)


def partial_sums(kernel, n, place, operands):
    shape = (8, 32, 896) if n == 1 else (8, 2, 32, 896)
    return pl.pallas_call(
        kernel,
        grid=(1,),
        out_shape=jax.ShapeDtypeStruct(shape, BF16),
        in_specs=[SMEM] + [whole(*v.shape) for v in operands],
        out_specs=whole(*shape),
        scratch_shapes=[pltpu.VMEM((256, 1024), BF16)],
        cost_estimate=pl.CostEstimate(flops=n * 2 * 256 * 1024 * 896, bytes_accessed=n * 3000000, transcendentals=0),
        compiler_params=pltpu.CompilerParams(vmem_limit_bytes=32 << 20),
    )(place, *operands)


def output_kernel(place, acts, kept, g0, g1, g2, g3, m0, m1, m2, far_down, far_up, out):
    hidden, gate_grad, up_grad = (acts[:, k].reshape(256, 896) for k in range(3))

    def store(mixed, grad, slot, f):
        cols = slice(128 * slot, 128 * slot + 128)
        for t in (0, 1):
            rows = slice(128 * t, 128 * t + 128)
            out[8 * t + f, 0] = mixed[rows, cols].astype(BF16)
            out[8 * t + f, 1] = grad[rows, cols].astype(BF16)

    def terms(gate, down, up):
        mixed = lax.dot_general(hidden, down, NT, preferred_element_type=F32)
        grad = lax.dot_general(gate_grad, gate, NT, preferred_element_type=F32)
        return mixed, grad + lax.dot_general(up_grad, up, NT, preferred_element_type=F32)

    for pair in (0, 1):
        blocks = [kept[2 * pair : 2 * pair + 2, k].reshape(256, 896) for k in (GATE, DOWN, UP)]
        mixed, grad = terms(*blocks)
        for slot in (0, 1):
            store(mixed, grad, slot, feature(place, True, 2 * pair + slot))
    gates = [g[0] for g in (g0, g1, g2, g3)]
    downs = [m0[0], m1[0], m2[0], far_down[0]]
    ups = [m0[1], m1[1], m2[1], far_up[0]]
    for pair in (0, 1):
        blocks = [jnp.concatenate(v[2 * pair : 2 * pair + 2], axis=0) for v in (gates, downs, ups)]
        mixed, grad = terms(*blocks)
        for slot in (0, 1):
            x = (place[0] + STEPS[2 * pair + slot]) % 4
            store(mixed, grad, slot, feature(place, False, x))


def on_device(tokens, gate_weight, up_weight, down_weight, grad_mixed):
    place = jnp.stack([lax.axis_index("x"), lax.axis_index("zh"), lax.axis_index("core")])
    keep, send_gate, send_two = call(
        split_kernel, [(3, 128, 896), (1, 128, 896), (2, 128, 896)], [whole(128, 1792)] * 3, 0, 3000000
    )(place, gate_weight, down_weight, up_weight)
    kept = lax.all_gather(keep, "x", axis=0)
    gate = exchange(send_gate, "zh")
    two = exchange(send_two, "zh")

    acts = jnp.broadcast_to(jnp.stack([tokens, grad_mixed])[None], (8, 2, 128, 128))
    near = lax.all_to_all(acts, ("zh", "zl"), 0, 0, tiled=True)
    other = exchange(near, "core")

    gate_left, gate_right = shift(gate, 1), shift(gate, -1)
    gates = (gate, gate_left, gate_right, shift(gate_left, 1))
    gate_parts = lax.all_to_all(partial_sums(gate_kernel, 1, place, (near, other, kept, *gates)), "y", 0, 0, tiled=True)

    two_left, two_right = shift(two, 1), shift(two, -1)
    twos = (two, two_left, two_right, shift(two_left[:1], 1), shift(two_right[1:], -1))
    two_parts = lax.all_to_all(partial_sums(two_kernel, 2, place, (near, other, kept, *twos)), "y", 0, 0, tiled=True)

    gate_value = jnp.sum(gate_parts.astype(F32), axis=0)
    hidden_grad, up_value = (jnp.sum(two_parts[:, k].astype(F32), axis=0) for k in (0, 1))
    sig = jax.nn.sigmoid(gate_value)
    silu = gate_value * sig
    hidden = (silu * up_value).astype(BF16)
    gate_grad = (hidden_grad * up_value * sig * (1.0 + gate_value * (1.0 - sig))).astype(BF16)
    up_grad = (hidden_grad * silu).astype(BF16)
    rows = jnp.stack([hidden, gate_grad, up_grad])
    rows = lax.all_to_all(jnp.broadcast_to(rows[None], (8, 3, 32, 896)), "y", 0, 0, tiled=True)
    operands = (rows, kept, *gates, *twos)
    (terms,) = call(
        output_kernel, [(16, 2, 128, 128)], [whole(*v.shape) for v in operands], 6 * 256 * 1024 * 896, 8000000
    )(place, *operands)
    terms = lax.all_to_all(terms, RING, 0, 0, tiled=True)
    both = jnp.sum(terms.astype(F32), axis=0).astype(BF16)
    return both[0], both[1]


def solution(mesh):
    fine = Mesh(mesh.devices.reshape(8, 4, 2, 2, 4), AXES)
    acts = P(("zh", "x"), ("y", "zl", "core"))
    weights = P(("y", "zh", "x"), ("zl", "core"))
    return jax.shard_map(
        on_device,
        mesh=fine,
        in_specs=(acts, weights, weights, weights, acts),
        out_specs=(acts, acts),
        check_vma=False,
    )
```

time: 281 us -> 237 us (0.84)
  starting transfers between devices: 121 us -> 57.1 us
  blocking collectives: 13.6 us -> 75.9 us
  local copies, waits for them, and re-layouts: 43.9 us -> 17.5 us
  waiting for transfers between devices: 79.1 us -> 60 us
  matrix products: 9.73 us -> 0 us
  Pallas kernels: 0 us -> 8.19 us
  between operations: 8.96 us -> 14.4 us
    all_to_all x1 -> x2, blocking collectives: 13.6 us -> 75.9 us  [the longest x1 42.6 us: on_device(): terms = lax.all_to_all(terms, RING, 0, 0, tiled=True)]
    all_to_all x11 -> x3, starting transfers between devices: 81.6 us -> 23.7 us  [the longest x1 10.9 us: on_device(): near = lax.all_to_all(acts, ('zh', 'zl'), 0, 0, tiled=True)]
    all_to_all x11 -> x3, waiting for transfers between devices: 78.3 us -> 31.3 us  [the longest x1 21.6 us: on_device(): lax.all_to_all(partial_sums(two_kernel, 2, place, (near, other, kept, *tw...]
    ppermute x12 -> x7, starting transfers between devices: 39.2 us -> 19 us  [shift(): return lax.ppermute(values, 'x', [(i, (i + step) % 4) for i in range(4)])]
    ppermute x12 -> x7, waiting for transfers between devices: 0.78 us -> 20.5 us  [shift(): return lax.ppermute(values, 'x', [(i, (i + step) % 4) for i in range(4)])]
    ppermute x0 -> x3, starting transfers between devices: none -> 14.4 us  [exchange(): return lax.ppermute(values, axis, [(0, 1), (1, 0)])]
    dot_general x6 -> x0, matrix products: 9.73 us -> none  [the longest x1 2.99 us: on_device(): hidden_grad = combine(jnp.dot(wide_grad, down, preferred_element_type=F32))]
    slice x6 -> x2, local copies, waits for them, and re-layouts: 8.61 us -> 0.04 us  [the longest x1 0.02 us: on_device(): two_left[:1]]
  transfers between devices with their start and end apart: 23 -> 14, of which waited for: 9 -> 9; matrix products, arithmetic and copies ran while one was open for 18% -> 1% of each run, Pallas kernels for 0% -> 2%
where the time goes in v3:
time: 237 us; the launch traced here: 236 us
  blocking collectives  75.9 us (32%)
  waiting for transfers between devices  60 us (25%)
  starting transfers between devices  57.1 us (24%)
  local copies, waits for them, and re-layouts  17.5 us (7%)
  between operations  14.4 us (6%)
  Pallas kernels  8.19 us (3%)
  other arithmetic  2.74 us (1%)
    all_to_all x1, blocking collectives, on_device(): terms = lax.all_to_all(terms, RING, 0, 0, tiled=True)  42.6 us
    all_to_all x1, blocking collectives, on_device(): lax.all_to_all(jnp.broadcast_to(rows[None], (8, 3, 32, 896)), 'y', 0, 0,...  33.3 us
    all_to_all x1, waiting for transfers between devices, on_device(): lax.all_to_all(partial_sums(two_kernel, 2, place, (near, other, kept, *tw...  21.6 us
    ppermute x7, waiting for transfers between devices, shift(): return lax.ppermute(values, 'x', [(i, (i + step) % 4) for i in range(4)])  20.5 us
    ppermute x7, starting transfers between devices, shift(): return lax.ppermute(values, 'x', [(i, (i + step) % 4) for i in range(4)])  19 us
    unnamed x58, local copies, waits for them, and re-layouts  15.8 us
    ppermute x3, starting transfers between devices, exchange(): return lax.ppermute(values, axis, [(0, 1), (1, 0)])  14.4 us
    all_to_all x1, starting transfers between devices, on_device(): near = lax.all_to_all(acts, ('zh', 'zl'), 0, 0, tiled=True)  10.9 us
  transfers between devices with their start and end apart: 14, of which 9 were waited for; matrix products, arithmetic and copies ran while one was open for 1% of the time, Pallas kernels for 2%

profile of v3, /device:TPU:1, one launch (start us, length us, event | category | flops | bytes accessed | tf_op | source)
XLA Modules:
  0.0 235.8 jit_solution(9524104811407367066)
XLA Ops:
  13.0 10.9 %all-to-all-start = ((bf16[8,2,128,128]{3,2,1,0:T(8,128)(2,1)}), bf16[8,2,128,128]{3,2,1,0:T(8,128)(2,1)S(1)}, u32[]{:S(2)}, u32[]{:S(2)}) async-start(bf16[8,2,128,128]{3,2,1,0:T(8,128)(2,1)} %broadcast_in_dim.4), calls=%async_computation | async-start | bytes 1048576 | tf_op jit(solution)/shard_map/all_to_all | solution.py:146
  23.9 7.3 %collective-permute-start.1 = (bf16[1,128,896]{2,1,0:T(8,128)(2,1)S(1)}, bf16[1,128,896]{2,1,0:T(8,128)(2,1)S(1)}, u32[]{:S(2)}, u32[]{:S(2)}) collective-permute-start(bf16[1,128,896]{2,1,0:T(8,128)(2,1)S(1)} %get-tuple-element.6), channel_id=1, source_target_pairs={{0,4},{4,0},{1,5},{5,1},{2,6},{6,2},{3,7},{7,3},{8,12},{12,8},{9,1... | collective-permute-start | bytes 688136 | tf_op jit(solution)/shard_map/ppermute | solution.py:38
  31.1 9.7 %all-to-all-done.near = bf16[8,2,128,128]{3,2,1,0:T(8,128)(2,1)S(1)} async-done(((bf16[8,2,128,128]{3,2,1,0:T(8,128)(2,1)}), bf16[8,2,128,128]{3,2,1,0:T(8,128)(2,1)S(1)}, u32[]{:S(2)}, u32[]{:S(2)}) %all-to-all-start) | async-done | bytes 524320 | tf_op jit(solution)/shard_map/all_to_all | solution.py:146
  40.9 2.5 %collective-permute-start = (bf16[8,2,128,128]{3,2,1,0:T(8,128)(2,1)S(1)}, bf16[8,2,128,128]{3,2,1,0:T(8,128)(2,1)S(1)}, u32[]{:S(2)}, u32[]{:S(2)}) collective-permute-start(bf16[8,2,128,128]{3,2,1,0:T(8,128)(2,1)S(1)} %all-to-all-done.near), channel_id=1, source_target_pairs={{0,8},{8,0},{1,9},{9,1},{2,10},{10,2},{3,11},{11,3},{4,12},{12,4},... | collective-permute-start | bytes 1572872 | tf_op jit(solution)/shard_map/ppermute | solution.py:38
  43.4 8.2 %collective-permute-done.1.m0.g0 = bf16[1,128,896]{2,1,0:T(8,128)(2,1)S(1)} collective-permute-done((bf16[1,128,896]{2,1,0:T(8,128)(2,1)S(1)}, bf16[1,128,896]{2,1,0:T(8,128)(2,1)S(1)}, u32[]{:S(2)}, u32[]{:S(2)}) %collective-permute-start.1) | collective-permute-done | bytes 229408 | tf_op jit(solution)/shard_map/ppermute | solution.py:38
  51.6 3.1 %collective-permute-start.2 = (bf16[1,128,896]{2,1,0:T(8,128)(2,1)S(1)}, bf16[1,128,896]{2,1,0:T(8,128)(2,1)S(1)}, u32[]{:S(2)}, u32[]{:S(2)}) collective-permute-start(bf16[1,128,896]{2,1,0:T(8,128)(2,1)S(1)} %collective-permute-done.1.m0.g0), channel_id=1, source_target_pairs={{0,1},{1,2},{2,3},{3,0},{4,5},{5,6},{6,7},{7,4},{8,9},{9,10},{10,1... | collective-permute-start | bytes 688136 | tf_op jit(solution)/shard_map/ppermute | solution.py:34
  54.8 4.6 %collective-permute-start.5 = (bf16[2,128,896]{2,1,0:T(8,128)(2,1)}, bf16[2,128,896]{2,1,0:T(8,128)(2,1)}, u32[]{:S(2)}, u32[]{:S(2)}) collective-permute-start(bf16[2,128,896]{2,1,0:T(8,128)(2,1)} %get-tuple-element.7), channel_id=1, source_target_pairs={{0,4},{4,0},{1,5},{5,1},{2,6},{6,2},{3,7},{7,3},{8,12},{12,8},{9,1... | collective-permute-start | bytes 1376264 | tf_op jit(solution)/shard_map/ppermute | solution.py:38
  59.4 3.4 %collective-permute-start.3 = (bf16[1,128,896]{2,1,0:T(8,128)(2,1)S(1)}, bf16[1,128,896]{2,1,0:T(8,128)(2,1)S(1)}, u32[]{:S(2)}, u32[]{:S(2)}) collective-permute-start(bf16[1,128,896]{2,1,0:T(8,128)(2,1)S(1)} %collective-permute-done.1.m0.g0), channel_id=1, source_target_pairs={{0,3},{1,0},{2,1},{3,2},{4,7},{5,4},{6,5},{7,6},{8,11},{9,8},{10,9... | collective-permute-start | bytes 688136 | tf_op jit(solution)/shard_map/ppermute | solution.py:34
  63.8 1.9 collective-permute-start.4
  68.6 4.8 %collective-permute-done.4.m3.g3 = bf16[1,128,896]{2,1,0:T(8,128)(2,1)S(1)} collective-permute-done((bf16[1,128,896]{2,1,0:T(8,128)(2,1)S(1)}, bf16[1,128,896]{2,1,0:T(8,128)(2,1)S(1)}, u32[]{:S(2)}, u32[]{:S(2)}) %collective-permute-start.4) | collective-permute-done | bytes 229408 | tf_op jit(solution)/shard_map/ppermute | solution.py:34
  74.9 1.8 copy-done
  82.6 6.5 %all-to-all-start.1 = ((bf16[8,32,896]{2,1,0:T(8,128)(2,1)}), bf16[8,32,896]{2,1,0:T(8,128)(2,1)}, u32[]{:S(2)}, u32[]{:S(2)}) async-start(bf16[8,32,896]{2,1,0:T(8,128)(2,1)} %copy-done.10), calls=%async_computation.1 | async-start | bytes 917504 | tf_op jit(solution)/shard_map/all_to_all | solution.py:151
  89.1 1.9 collective-permute-start.7
  91.0 3.4 %collective-permute-start.6 = (bf16[2,128,896]{2,1,0:T(8,128)(2,1)}, bf16[2,128,896]{2,1,0:T(8,128)(2,1)S(1)}, u32[]{:S(2)}, u32[]{:S(2)}) collective-permute-start(bf16[2,128,896]{2,1,0:T(8,128)(2,1)} %collective-permute-done.5.m0), channel_id=1, source_target_pairs={{0,1},{1,2},{2,3},{3,0},{4,5},{5,6},{6,7},{7,4},{8,9},{9,10},{10,1... | collective-permute-start | bytes 1376264 | tf_op jit(solution)/shard_map/ppermute | solution.py:34
  94.4 7.2 %collective-permute-done.7.m2 = bf16[2,128,896]{2,1,0:T(8,128)(2,1)S(1)} collective-permute-done((bf16[2,128,896]{2,1,0:T(8,128)(2,1)}, bf16[2,128,896]{2,1,0:T(8,128)(2,1)S(1)}, u32[]{:S(2)}, u32[]{:S(2)}) %collective-permute-start.7) | collective-permute-done | bytes 458784 | tf_op jit(solution)/shard_map/ppermute | solution.py:34
  101.5 3.3 %collective-permute-start.9 = (bf16[1,128,896]{2,1,0:T(8,128)(2,1)S(1)}, bf16[1,128,896]{2,1,0:T(8,128)(2,1)S(1)}, u32[]{:S(2)}, u32[]{:S(2)}) collective-permute-start(bf16[1,128,896]{2,1,0:T(8,128)(2,1)S(1)} %slice.25), channel_id=1, source_target_pairs={{0,3},{1,0},{2,1},{3,2},{4,7},{5,4},{6,5},{7,6},{8,11},{9,8},{10,9... | collective-permute-start | bytes 688136 | tf_op jit(solution)/shard_map/ppermute | solution.py:34
  104.9 2.0 collective-permute-start.8
  108.3 4.6 %collective-permute-done.8.far_down = bf16[1,128,896]{2,1,0:T(8,128)(2,1)S(1)} collective-permute-done((bf16[1,128,896]{2,1,0:T(8,128)(2,1)S(1)}, bf16[1,128,896]{2,1,0:T(8,128)(2,1)S(1)}, u32[]{:S(2)}, u32[]{:S(2)}) %collective-permute-start.8) | collective-permute-done | bytes 229408 | tf_op jit(solution)/shard_map/ppermute | solution.py:34
  113.9 2.4 %shard_map.70 = bf16[8,2,32,896]{3,2,1,0:T(8,128)(2,1)S(1)} custom-call(s32[3]{0:T(128)S(1)} %pad_add_fusion.place, bf16[8,2,128,128]{3,2,1,0:T(8,128)(2,1)S(1)} %all-to-all-done.near, bf16[8,2,128,128]{3,2,1,0:T(8,128)(2,1)S(1)} %copy-done.9, bf16[4,3,128,896]{3,2,1,0:T(8,128)(2,1)S(1)} %bitcast.49, bf16[2,128,896]{2,1,0:T(8,128)(2,1)} %collective-permute-done.5.m0, ...), custom_call_target="tpu_custom_call" | custom-call | flops 939524096 | bytes 6000000 | tf_op jit(solution)/shard_map/pallas_call | solution.py:93
  118.7 6.4 %all-to-all-start.2 = ((bf16[8,2,32,896]{3,2,1,0:T(8,128)(2,1)}), bf16[8,2,32,896]{3,2,1,0:T(8,128)(2,1)}, u32[]{:S(2)}, u32[]{:S(2)}) async-start(bf16[8,2,32,896]{3,2,1,0:T(8,128)(2,1)} %copy-done.2), calls=%async_computation.2 | async-start | bytes 1835008 | tf_op jit(solution)/shard_map/all_to_all | solution.py:155
  126.2 21.6 %all-to-all-done.2 = bf16[8,2,32,896]{3,2,1,0:T(8,128)(2,1)} async-done(((bf16[8,2,32,896]{3,2,1,0:T(8,128)(2,1)}), bf16[8,2,32,896]{3,2,1,0:T(8,128)(2,1)}, u32[]{:S(2)}, u32[]{:S(2)}) %all-to-all-start.2) | async-done | bytes 917536 | tf_op jit(solution)/shard_map/all_to_all | solution.py:155
  149.4 33.3 %all_to_all.25.acts = bf16[8,3,32,896]{3,2,1,0:T(8,128)(2,1)S(1)} all-to-all(bf16[8,3,32,896]{3,2,1,0:T(8,128)(2,1)S(1)} %broadcast_in_dim.5), channel_id=1, replica_groups=mesh['y'=8,'zl'=4,'core'=2,'zh'=2,'x'=4] {'y'}, dimensions={0} | all-to-all | bytes 2752512 | tf_op jit(solution)/shard_map/all_to_all | solution.py:165
  182.7 2.8 %shard_map.71 = bf16[16,2,128,128]{3,2,1,0:T(8,128)(2,1)S(1)} custom-call(s32[3]{0:T(128)S(1)} %pad_add_fusion.place, bf16[8,3,32,896]{3,2,1,0:T(8,128)(2,1)S(1)} %all_to_all.25.acts, bf16[4,3,128,896]{3,2,1,0:T(8,128)(2,1)S(1)} %bitcast.50, bf16[1,128,896]{2,1,0:T(8,128)(2,1)S(1)} %collective-permute-done.1.m0.g0, bf16[1,128,896]{2,1,0:T(8,128)(2,1)S(1)} %copy-done.13, ...), custom_call_target="tpu_custom_call" | custom-call | flops 1409286144 | bytes 8000000 | tf_op jit(solution)/shard_map/pallas_call | solution.py:167
  185.6 42.6 %all_to_all.26 = bf16[16,2,128,128]{3,2,1,0:T(8,128)(2,1)S(1)} all-to-all(bf16[16,2,128,128]{3,2,1,0:T(8,128)(2,1)S(1)} %shard_map.71), channel_id=1, replica_groups=mesh['y'=8,'zl'=4,'core'=2,'zh'=2,'x'=4] {'zh','zl','core'}, dimensions={0} | all-to-all | bytes 2097152 | tf_op jit(solution)/shard_map/all_to_all | solution.py:170
  (81 shorter events, 25.3 us)
Async XLA Ops:
  7.2 67.8 %all-gather.3.cloned.1.call-start = ((), (), s32[]{:S(2)}) async-start(), calls=%async_computation.5 | async-start | bytes 3440640 | tf_op jit(solution)/shard_map/all_gather | solution.py:141
  13.0 27.9 %all-to-all-start = ((bf16[8,2,128,128]{3,2,1,0:T(8,128)(2,1)}), bf16[8,2,128,128]{3,2,1,0:T(8,128)(2,1)S(1)}, u32[]{:S(2)}, u32[]{:S(2)}) async-start(bf16[8,2,128,128]{3,2,1,0:T(8,128)(2,1)} %broadcast_in_dim.4), calls=%async_computation | async-start | bytes 1048576 | tf_op jit(solution)/shard_map/all_to_all | solution.py:146
  23.9 27.8 %collective-permute-start.1 = (bf16[1,128,896]{2,1,0:T(8,128)(2,1)S(1)}, bf16[1,128,896]{2,1,0:T(8,128)(2,1)S(1)}, u32[]{:S(2)}, u32[]{:S(2)}) collective-permute-start(bf16[1,128,896]{2,1,0:T(8,128)(2,1)S(1)} %get-tuple-element.6), channel_id=1, source_target_pairs={{0,4},{4,0},{1,5},{5,1},{2,6},{6,2},{3,7},{7,3},{8,12},{12,8},{9,1... | collective-permute-start | bytes 688136 | tf_op jit(solution)/shard_map/ppermute | solution.py:38
  40.9 33.2 %collective-permute-start = (bf16[8,2,128,128]{3,2,1,0:T(8,128)(2,1)S(1)}, bf16[8,2,128,128]{3,2,1,0:T(8,128)(2,1)S(1)}, u32[]{:S(2)}, u32[]{:S(2)}) collective-permute-start(bf16[8,2,128,128]{3,2,1,0:T(8,128)(2,1)S(1)} %all-to-all-done.near), channel_id=1, source_target_pairs={{0,8},{8,0},{1,9},{9,1},{2,10},{10,2},{3,11},{11,3},{4,12},{12,4},... | collective-permute-start | bytes 1572872 | tf_op jit(solution)/shard_map/ppermute | solution.py:38
  51.6 12.1 %collective-permute-start.2 = (bf16[1,128,896]{2,1,0:T(8,128)(2,1)S(1)}, bf16[1,128,896]{2,1,0:T(8,128)(2,1)S(1)}, u32[]{:S(2)}, u32[]{:S(2)}) collective-permute-start(bf16[1,128,896]{2,1,0:T(8,128)(2,1)S(1)} %collective-permute-done.1.m0.g0), channel_id=1, source_target_pairs={{0,1},{1,2},{2,3},{3,0},{4,5},{5,6},{6,7},{7,4},{8,9},{9,10},{10,1... | collective-permute-start | bytes 688136 | tf_op jit(solution)/shard_map/ppermute | solution.py:34
  54.8 34.3 %collective-permute-start.5 = (bf16[2,128,896]{2,1,0:T(8,128)(2,1)}, bf16[2,128,896]{2,1,0:T(8,128)(2,1)}, u32[]{:S(2)}, u32[]{:S(2)}) collective-permute-start(bf16[2,128,896]{2,1,0:T(8,128)(2,1)} %get-tuple-element.7), channel_id=1, source_target_pairs={{0,4},{4,0},{1,5},{5,1},{2,6},{6,2},{3,7},{7,3},{8,12},{12,8},{9,1... | collective-permute-start | bytes 1376264 | tf_op jit(solution)/shard_map/ppermute | solution.py:38
  59.4 8.5 %collective-permute-start.3 = (bf16[1,128,896]{2,1,0:T(8,128)(2,1)S(1)}, bf16[1,128,896]{2,1,0:T(8,128)(2,1)S(1)}, u32[]{:S(2)}, u32[]{:S(2)}) collective-permute-start(bf16[1,128,896]{2,1,0:T(8,128)(2,1)S(1)} %collective-permute-done.1.m0.g0), channel_id=1, source_target_pairs={{0,3},{1,0},{2,1},{3,2},{4,7},{5,4},{6,5},{7,6},{8,11},{9,8},{10,9... | collective-permute-start | bytes 688136 | tf_op jit(solution)/shard_map/ppermute | solution.py:34
  63.8 9.6 %collective-permute-start.4 = (bf16[1,128,896]{2,1,0:T(8,128)(2,1)S(1)}, bf16[1,128,896]{2,1,0:T(8,128)(2,1)S(1)}, u32[]{:S(2)}, u32[]{:S(2)}) collective-permute-start(bf16[1,128,896]{2,1,0:T(8,128)(2,1)S(1)} %collective-permute-done.2.m1.g1), channel_id=1, source_target_pairs={{0,1},{1,2},{2,3},{3,0},{4,5},{5,6},{6,7},{7,4},{8,9},{9,10},{10,1... | collective-permute-start | bytes 688136 | tf_op jit(solution)/shard_map/ppermute | solution.py:34
  80.6 32.3 %copy-start.1 = (bf16[12,128,896]{2,1,0:T(8,128)(2,1)S(1)}, bf16[12,128,896]{2,1,0:T(8,128)(2,1)}, u32[]{:S(2)}) copy-start(bf16[12,128,896]{2,1,0:T(8,128)(2,1)} %all-gather.3.cloned.1.call-done) | copy-start | bytes 8257540
  82.6 36.2 %all-to-all-start.1 = ((bf16[8,32,896]{2,1,0:T(8,128)(2,1)}), bf16[8,32,896]{2,1,0:T(8,128)(2,1)}, u32[]{:S(2)}, u32[]{:S(2)}) async-start(bf16[8,32,896]{2,1,0:T(8,128)(2,1)} %copy-done.10), calls=%async_computation.1 | async-start | bytes 917504 | tf_op jit(solution)/shard_map/all_to_all | solution.py:151
  89.1 12.5 %collective-permute-start.7 = (bf16[2,128,896]{2,1,0:T(8,128)(2,1)}, bf16[2,128,896]{2,1,0:T(8,128)(2,1)S(1)}, u32[]{:S(2)}, u32[]{:S(2)}) collective-permute-start(bf16[2,128,896]{2,1,0:T(8,128)(2,1)} %collective-permute-done.5.m0), channel_id=1, source_target_pairs={{0,3},{1,0},{2,1},{3,2},{4,7},{5,4},{6,5},{7,6},{8,11},{9,8},{10,9... | collective-permute-start | bytes 1376264 | tf_op jit(solution)/shard_map/ppermute | solution.py:34
  91.0 13.9 %collective-permute-start.6 = (bf16[2,128,896]{2,1,0:T(8,128)(2,1)}, bf16[2,128,896]{2,1,0:T(8,128)(2,1)S(1)}, u32[]{:S(2)}, u32[]{:S(2)}) collective-permute-start(bf16[2,128,896]{2,1,0:T(8,128)(2,1)} %collective-permute-done.5.m0), channel_id=1, source_target_pairs={{0,1},{1,2},{2,3},{3,0},{4,5},{5,6},{6,7},{7,4},{8,9},{9,10},{10,1... | collective-permute-start | bytes 1376264 | tf_op jit(solution)/shard_map/ppermute | solution.py:34
  101.5 11.4 %copy-start.3 = (bf16[2,128,896]{2,1,0:T(8,128)(2,1)}, bf16[2,128,896]{2,1,0:T(8,128)(2,1)S(1)}, u32[]{:S(2)}) copy-start(bf16[2,128,896]{2,1,0:T(8,128)(2,1)S(1)} %collective-permute-done.7.m2) | copy-start | bytes 1376260
  101.5 6.8 %collective-permute-start.9 = (bf16[1,128,896]{2,1,0:T(8,128)(2,1)S(1)}, bf16[1,128,896]{2,1,0:T(8,128)(2,1)S(1)}, u32[]{:S(2)}, u32[]{:S(2)}) collective-permute-start(bf16[1,128,896]{2,1,0:T(8,128)(2,1)S(1)} %slice.25), channel_id=1, source_target_pairs={{0,3},{1,0},{2,1},{3,2},{4,7},{5,4},{6,5},{7,6},{8,11},{9,8},{10,9... | collective-permute-start | bytes 688136 | tf_op jit(solution)/shard_map/ppermute | solution.py:34
  104.9 8.0 %copy-start.5 = (bf16[2,128,896]{2,1,0:T(8,128)(2,1)}, bf16[2,128,896]{2,1,0:T(8,128)(2,1)S(1)}, u32[]{:S(2)}) copy-start(bf16[2,128,896]{2,1,0:T(8,128)(2,1)S(1)} %collective-permute-done.6.m1) | copy-start | bytes 1376260
  104.9 8.0 %collective-permute-start.8 = (bf16[1,128,896]{2,1,0:T(8,128)(2,1)S(1)}, bf16[1,128,896]{2,1,0:T(8,128)(2,1)S(1)}, u32[]{:S(2)}, u32[]{:S(2)}) collective-permute-start(bf16[1,128,896]{2,1,0:T(8,128)(2,1)S(1)} %slice.24), channel_id=1, source_target_pairs={{0,1},{1,2},{2,3},{3,0},{4,5},{5,6},{6,7},{7,4},{8,9},{9,10},{10,1... | collective-permute-start | bytes 688136 | tf_op jit(solution)/shard_map/ppermute | solution.py:34
  118.7 29.0 %all-to-all-start.2 = ((bf16[8,2,32,896]{3,2,1,0:T(8,128)(2,1)}), bf16[8,2,32,896]{3,2,1,0:T(8,128)(2,1)}, u32[]{:S(2)}, u32[]{:S(2)}) async-start(bf16[8,2,32,896]{3,2,1,0:T(8,128)(2,1)} %copy-done.2), calls=%async_computation.2 | async-start | bytes 1835008 | tf_op jit(solution)/shard_map/all_to_all | solution.py:155
  149.3 33.4 %copy-start.4 = (bf16[2,128,896]{2,1,0:T(8,128)(2,1)S(1)}, bf16[2,128,896]{2,1,0:T(8,128)(2,1)}, u32[]{:S(2)}) copy-start(bf16[2,128,896]{2,1,0:T(8,128)(2,1)} %copy-done.3) | copy-start | bytes 1376260
  149.3 33.4 %copy-start.6 = (bf16[2,128,896]{2,1,0:T(8,128)(2,1)S(1)}, bf16[2,128,896]{2,1,0:T(8,128)(2,1)}, u32[]{:S(2)}) copy-start(bf16[2,128,896]{2,1,0:T(8,128)(2,1)} %copy-done.5) | copy-start | bytes 1376260
  149.3 33.4 %copy-start.13 = (bf16[1,128,896]{2,1,0:T(8,128)(2,1)S(1)}, bf16[1,128,896]{2,1,0:T(8,128)(2,1)}, u32[]{:S(2)}) copy-start(bf16[1,128,896]{2,1,0:T(8,128)(2,1)} %copy-done.11) | copy-start | bytes 688132
  149.3 33.4 %copy-start.16 = (bf16[1,128,896]{2,1,0:T(8,128)(2,1)S(1)}, bf16[1,128,896]{2,1,0:T(8,128)(2,1)}, u32[]{:S(2)}) copy-start(bf16[1,128,896]{2,1,0:T(8,128)(2,1)} %copy-done.14) | copy-start | bytes 688132
  149.4 33.4 %copy-start.19 = (bf16[1,128,896]{2,1,0:T(8,128)(2,1)S(1)}, bf16[1,128,896]{2,1,0:T(8,128)(2,1)}, u32[]{:S(2)}) copy-start(bf16[1,128,896]{2,1,0:T(8,128)(2,1)} %copy-done.17) | copy-start | bytes 688132
  149.4 33.4 %copy-start.21 = (bf16[1,128,896]{2,1,0:T(8,128)(2,1)S(1)}, bf16[1,128,896]{2,1,0:T(8,128)(2,1)}, u32[]{:S(2)}) copy-start(bf16[1,128,896]{2,1,0:T(8,128)(2,1)} %copy-done.20) | copy-start | bytes 688132
  149.4 33.4 %copy-start.23 = (bf16[1,128,896]{2,1,0:T(8,128)(2,1)S(1)}, bf16[1,128,896]{2,1,0:T(8,128)(2,1)}, u32[]{:S(2)}) copy-start(bf16[1,128,896]{2,1,0:T(8,128)(2,1)} %copy-done.22) | copy-start | bytes 688132
  (19 other events, 19.2 us)
Sparse Core Ops, SparseCore 0:
  12.2 48.3 all-gather.2

commit v4 on v1

v4 whole, which is shorter than its diff:
```python
import jax
import jax.numpy as jnp
from jax import lax
from jax.experimental import pallas as pl
from jax.experimental.pallas import tpu as pltpu
from jax.sharding import Mesh, PartitionSpec as P

AXES = ("y", "zl", "core", "zh", "x")
NT = (((1,), (1,)), ((), ()))
F32, BF16 = jnp.float32, jnp.bfloat16
STEPS = (0, 3, 1, 2)
GATE, DOWN, UP = 0, 1, 2
WHICH = {GATE: 0, DOWN: 1, UP: 0}
HBM = pl.BlockSpec(memory_space=pltpu.HBM)
SMEM = pl.BlockSpec(memory_space=pltpu.SMEM)
BLOCK = (128, 896)


def call(kernel, outs, operands, scratch, flops, moved):
    return pl.pallas_call(
        kernel,
        out_shape=outs,
        in_specs=[SMEM] + [HBM] * (len(operands) - 1),
        out_specs=[HBM] * len(outs),
        scratch_shapes=scratch,
        cost_estimate=pl.CostEstimate(flops=flops, bytes_accessed=moved, transcendentals=0),
        compiler_params=pltpu.CompilerParams(vmem_limit_bytes=40 << 20),
    )(*operands)


def start(copies):
    for copy in copies:
        copy.start()
    return copies


def wait(copies):
    for copy in copies:
        copy.wait()


def shift(values, step):
    return lax.ppermute(values, "x", [(i, (i + step) % 4) for i in range(4)])


def exchange(values, axis):
    return lax.ppermute(values, axis, [(0, 1), (1, 0)])


def split_kernel(place, gate, down, up, keep, send_gate, send_down, send_up, sems):
    zh = place[1]
    low, high = pl.ds(0, 896), pl.ds(896, 896)

    def copies(mine, away):
        made = []
        for k, (weight, send) in enumerate(((gate, send_gate), (down, send_down), (up, send_up))):
            made.append(pltpu.make_async_copy(weight.at[:, mine], keep.at[k], sems.at[2 * k]))
            made.append(pltpu.make_async_copy(weight.at[:, away], send, sems.at[2 * k + 1]))
        return made

    @pl.when(zh == 0)
    def _():
        wait(start(copies(low, high)))

    @pl.when(zh == 1)
    def _():
        wait(start(copies(high, low)))


def acts_kernel(place, tokens, grad, out, sems):
    wait(start(
        [pltpu.make_async_copy(v, out.at[i, k], sems.at[2 * i + k]) for i in range(8) for k, v in enumerate((tokens, grad))]
    ))


def feature(place, own, x):
    return ((place[1] + (0 if own else 1)) % 2) * 4 + x


def came_from(place, slot):
    return (place[0] + STEPS[slot]) % 4


def load_weights(k, kept, moved, kept_v, moved_v, sems):
    made = [pltpu.make_async_copy(kept.at[:, k], kept_v.at[k], sems.at[5 * k])]
    for slot in range(4):
        made.append(pltpu.make_async_copy(moved[4 * k + slot], moved_v.at[k, slot], sems.at[5 * k + 1 + slot]))
    return made


def sums_kernel(place, near, other, kept, *refs):
    moved, out = refs[:12], refs[12]
    acts_v, kept_v, moved_v, wide, out_v, sems = refs[13:]
    acts = start(
        [pltpu.make_async_copy(near, acts_v.at[0], sems.at[15]), pltpu.make_async_copy(other, acts_v.at[1], sems.at[16])]
    )
    loads = [start(load_weights(k, kept, moved, kept_v, moved_v, sems)) for k in range(3)]
    wait(acts)
    for which in (0, 1):
        for t in (0, 1):
            for own in (True, False):
                for slot in range(4):
                    f = feature(place, own, slot if own else came_from(place, slot))
                    tile = acts_v[(f + place[2]) % 2, 4 * t + f // 2, which]
                    wide[which, pl.ds(128 * t, 128), pl.ds((0 if own else 512) + 128 * slot, 128)] = tile
    stores = []
    for k in range(3):
        wait(loads[k])
        which = WHICH[k]
        total = jnp.dot(wide[which, :, :512], kept_v[k].reshape(512, 896), preferred_element_type=F32)
        total = total + jnp.dot(wide[which, :, 512:], moved_v[k].reshape(512, 896), preferred_element_type=F32)
        out_v[k] = total.astype(BF16).reshape(8, 32, 896)
        stores += start([pltpu.make_async_copy(out_v.at[k], out.at[:, k], sems.at[17 + k])])
    wait(stores)


def output_kernel(place, acts, kept, *refs):
    moved, (mine, theirs) = refs[:12], refs[12:14]
    acts_v, kept_v, moved_v, out_v, sems = refs[14:]
    acts_in = start([pltpu.make_async_copy(acts.at[:, k], acts_v.at[k], sems.at[15 + k]) for k in range(3)])
    loads = [start(load_weights(k, kept, moved, kept_v, moved_v, sems)) for k in range(3)]
    wait(acts_in)
    hidden, gate_grad, up_grad = (acts_v[k].reshape(256, 896) for k in range(3))

    def store(terms, which, own):
        for slot in range(4):
            f = feature(place, own, slot if own else came_from(place, slot))
            for t in (0, 1):
                tile = terms[128 * t : 128 * t + 128, 128 * slot : 128 * slot + 128]
                out_v[(f + place[2]) % 2, 4 * t + f // 2, which] = tile

    def product(rows, blocks):
        return lax.dot_general(rows, blocks.reshape(512, 896), NT, preferred_element_type=F32)

    wait(loads[DOWN])
    store(product(hidden, kept_v[DOWN]), 0, True)
    store(product(hidden, moved_v[DOWN]), 0, False)
    wait(loads[GATE])
    wait(loads[UP])
    for own, held in ((True, kept_v), (False, moved_v)):
        store(product(gate_grad, held[GATE]) + product(up_grad, held[UP]), 1, own)
    wait(start(
        [pltpu.make_async_copy(out_v.at[0], mine, sems.at[18]), pltpu.make_async_copy(out_v.at[1], theirs, sems.at[19])]
    ))


def on_device(tokens, gate_weight, up_weight, down_weight, grad_mixed):
    place = jnp.stack([lax.axis_index("x"), lax.axis_index("zh"), lax.axis_index("core")])
    block = jax.ShapeDtypeStruct(BLOCK, BF16)
    keep, *sends = call(
        split_kernel,
        [jax.ShapeDtypeStruct((3, *BLOCK), BF16), block, block, block],
        (place, gate_weight, down_weight, up_weight),
        [pltpu.SemaphoreType.DMA((6,))], 0, 3000000,
    )
    kept = lax.all_gather(keep, "x", axis=0)
    arrived = [exchange(send, "zh") for send in sends]

    (acts,) = call(
        acts_kernel, [jax.ShapeDtypeStruct((8, 2, 128, 128), BF16)], (place, tokens, grad_mixed),
        [pltpu.SemaphoreType.DMA((16,))], 40000000000, 1000000,
    )
    near = lax.all_to_all(acts, ("zh", "zl"), 0, 0, tiled=True)
    other = exchange(near, "core")

    moved = []
    for k, block in enumerate(arrived):
        left, right = shift(block, 1), shift(block, -1)
        moved += [block, left, right, shift(right, -1) if k == DOWN else shift(left, 1)]

    weights_v = [pltpu.VMEM((3, 4, *BLOCK), BF16), pltpu.VMEM((3, 4, *BLOCK), BF16)]
    (parts,) = call(
        sums_kernel, [jax.ShapeDtypeStruct((8, 3, 32, 896), BF16)], (place, near, other, kept, *moved),
        [pltpu.VMEM((2, 8, 2, 128, 128), BF16), *weights_v, pltpu.VMEM((2, 256, 1024), BF16),
         pltpu.VMEM((3, 8, 32, 896), BF16), pltpu.SemaphoreType.DMA((20,))],
        6 * 256 * 1024 * 896, 8000000,
    )
    parts = lax.all_to_all(parts, "y", 0, 0, tiled=True)
    gate_value, hidden_grad, up_value = (jnp.sum(parts[:, k].astype(F32), axis=0) for k in range(3))
    sig = jax.nn.sigmoid(gate_value)
    silu = gate_value * sig
    hidden = (silu * up_value).astype(BF16)
    gate_grad = (hidden_grad * up_value * sig * (1.0 + gate_value * (1.0 - sig))).astype(BF16)
    up_grad = (hidden_grad * silu).astype(BF16)
    rows = jnp.stack([hidden, gate_grad, up_grad])
    rows = lax.all_to_all(jnp.broadcast_to(rows[None], (8, 3, 32, 896)), "y", 0, 0, tiled=True)
    terms = jax.ShapeDtypeStruct((8, 2, 128, 128), F32)
    mine, theirs = call(
        output_kernel, [terms, terms], (place, rows, kept, *moved),
        [pltpu.VMEM((3, 8, 32, 896), BF16), *weights_v, pltpu.VMEM((2, 8, 2, 128, 128), F32),
         pltpu.SemaphoreType.DMA((20,))],
        6 * 256 * 1024 * 896, 8000000,
    )
    terms = (mine + exchange(theirs, "core")).astype(BF16)
    terms = lax.all_to_all(terms, ("zh", "zl"), 0, 0, tiled=True)
    both = jnp.sum(terms.astype(F32), axis=0).astype(BF16)
    return both[0], both[1]


def solution(mesh):
    fine = Mesh(mesh.devices.reshape(8, 4, 2, 2, 4), AXES)
    acts = P(("zh", "x"), ("y", "zl", "core"))
    weights = P(("y", "zh", "x"), ("zl", "core"))
    return jax.shard_map(
        on_device,
        mesh=fine,
        in_specs=(acts, weights, weights, weights, acts),
        out_specs=(acts, acts),
        check_vma=False,
    )
```

time: 281 us -> 232 us (0.83)
  blocking collectives: 13.6 us -> 98.5 us
  waiting for transfers between devices: 79.1 us -> 25.3 us
  starting transfers between devices: 121 us -> 67.3 us
  local copies, waits for them, and re-layouts: 43.9 us -> 7.4 us
  Pallas kernels: 0 us -> 17.4 us
  matrix products: 9.73 us -> 0 us
  between operations: 8.96 us -> 14.3 us
    all_to_all x1 -> x3, blocking collectives: 13.6 us -> 98.5 us  [the longest x1 38.1 us: on_device(): parts = lax.all_to_all(parts, 'y', 0, 0, tiled=True)]
    all_to_all x11 -> x1, waiting for transfers between devices: 78.3 us -> 0.01 us  [on_device(): near = lax.all_to_all(acts, ('zh', 'zl'), 0, 0, tiled=True)]
    all_to_all x11 -> x1, starting transfers between devices: 81.6 us -> 10.9 us  [on_device(): near = lax.all_to_all(acts, ('zh', 'zl'), 0, 0, tiled=True)]
    ppermute x0 -> x5, starting transfers between devices: none -> 27.5 us  [exchange(): return lax.ppermute(values, axis, [(0, 1), (1, 0)])]
    ppermute x0 -> x5, waiting for transfers between devices: none -> 18.9 us  [exchange(): return lax.ppermute(values, axis, [(0, 1), (1, 0)])]
    pallas_call x0 -> x4, Pallas kernels: none -> 17.4 us  [call(): pl.pallas_call(kernel, out_shape=outs, in_specs=[SMEM] + [HBM] * (len(ope...]
    unnamed x45 -> x18, local copies, waits for them, and re-layouts: 18.2 us -> 6.67 us
    ppermute x12 -> x9, starting transfers between devices: 39.2 us -> 28.9 us  [shift(): return lax.ppermute(values, 'x', [(i, (i + step) % 4) for i in range(4)])]
  transfers between devices with their start and end apart: 23 -> 16, of which waited for: 9 -> 6; matrix products, arithmetic and copies ran while one was open for 18% -> 0% of each run, Pallas kernels for 0% -> 1%
where the time goes in v4:
time: 232 us; the launch traced here: 231 us
  blocking collectives  98.5 us (42%)
  starting transfers between devices  67.3 us (29%)
  waiting for transfers between devices  25.3 us (11%)
  Pallas kernels  17.4 us (7%)
  between operations  14.3 us (6%)
  local copies, waits for them, and re-layouts  7.4 us (3%)
    all_to_all x1, blocking collectives, on_device(): parts = lax.all_to_all(parts, 'y', 0, 0, tiled=True)  38.1 us
    all_to_all x1, blocking collectives, on_device(): lax.all_to_all(jnp.broadcast_to(rows[None], (8, 3, 32, 896)), 'y', 0, 0,...  34.7 us
    ppermute x9, starting transfers between devices, shift(): return lax.ppermute(values, 'x', [(i, (i + step) % 4) for i in range(4)])  28.9 us
    ppermute x5, starting transfers between devices, exchange(): return lax.ppermute(values, axis, [(0, 1), (1, 0)])  27.5 us
    all_to_all x1, blocking collectives, on_device(): terms = lax.all_to_all(terms, ('zh', 'zl'), 0, 0, tiled=True)  25.7 us
    ppermute x5, waiting for transfers between devices, exchange(): return lax.ppermute(values, axis, [(0, 1), (1, 0)])  18.9 us
    pallas_call x4, Pallas kernels, call(): pl.pallas_call(kernel, out_shape=outs, in_specs=[SMEM] + [HBM] * (len(ope...  17.4 us
    all_to_all x1, starting transfers between devices, on_device(): near = lax.all_to_all(acts, ('zh', 'zl'), 0, 0, tiled=True)  10.9 us
  transfers between devices with their start and end apart: 16, of which 6 were waited for; matrix products, arithmetic and copies ran while one was open for 0% of the time, Pallas kernels for 1%

profile of v4, /device:TPU:1, one launch (start us, length us, event | category | flops | bytes accessed | tf_op | source)
XLA Modules:
  0.0 230.8 jit_solution(17586322948748246332)
XLA Ops:
  13.3 10.9 %all-to-all-start = ((bf16[8,2,128,128]{3,2,1,0:T(8,128)(2,1)}), bf16[8,2,128,128]{3,2,1,0:T(8,128)(2,1)S(1)}, u32[]{:S(2)}, u32[]{:S(2)}) async-start(bf16[8,2,128,128]{3,2,1,0:T(8,128)(2,1)} %shard_map.68), calls=%async_computation | async-start | bytes 1048576 | tf_op jit(solution)/shard_map/all_to_all | solution.py:163
  24.2 7.3 %collective-permute-start.1 = (bf16[128,896]{1,0:T(8,128)(2,1)S(1)}, bf16[128,896]{1,0:T(8,128)(2,1)S(1)}, u32[]{:S(2)}, u32[]{:S(2)}) collective-permute-start(bf16[128,896]{1,0:T(8,128)(2,1)S(1)} %get-tuple-element.9), channel_id=1, source_target_pairs={{0,4},{4,0},{1,5},{5,1},{2,6},{6,2},{3,7},{7,3},{8,12},{12,8},{9,1... | collective-permute-start | bytes 688136 | tf_op jit(solution)/shard_map/ppermute | solution.py:47
  31.5 1.9 collective-permute-start.5
  33.4 7.3 %collective-permute-start.9 = (bf16[128,896]{1,0:T(8,128)(2,1)S(1)}, bf16[128,896]{1,0:T(8,128)(2,1)S(1)}, u32[]{:S(2)}, u32[]{:S(2)}) collective-permute-start(bf16[128,896]{1,0:T(8,128)(2,1)S(1)} %get-tuple-element.11), channel_id=1, source_target_pairs={{0,4},{4,0},{1,5},{5,1},{2,6},{6,2},{3,7},{7,3},{8,12},{12,8},{9,1... | collective-permute-start | bytes 688136 | tf_op jit(solution)/shard_map/ppermute | solution.py:47
  40.7 7.9 %collective-permute-done.1.refs_0_ = bf16[128,896]{1,0:T(8,128)(2,1)S(1)} collective-permute-done((bf16[128,896]{1,0:T(8,128)(2,1)S(1)}, bf16[128,896]{1,0:T(8,128)(2,1)S(1)}, u32[]{:S(2)}, u32[]{:S(2)}) %collective-permute-start.1) | collective-permute-done | bytes 229408 | tf_op jit(solution)/shard_map/ppermute | solution.py:47
  48.6 4.4 %collective-permute-start.3 = (bf16[128,896]{1,0:T(8,128)(2,1)S(1)}, bf16[128,896]{1,0:T(8,128)(2,1)S(1)}, u32[]{:S(2)}, u32[]{:S(2)}) collective-permute-start(bf16[128,896]{1,0:T(8,128)(2,1)S(1)} %collective-permute-done.1.refs_0_), channel_id=1, source_target_pairs={{0,3},{1,0},{2,1},{3,2},{4,7},{5,4},{6,5},{7,6},{8,11},{9,8},{10,9... | collective-permute-start | bytes 688136 | tf_op jit(solution)/shard_map/ppermute | solution.py:43
  53.0 3.4 %collective-permute-start = (bf16[8,2,128,128]{3,2,1,0:T(8,128)(2,1)S(1)}, bf16[8,2,128,128]{3,2,1,0:T(8,128)(2,1)S(1)}, u32[]{:S(2)}, u32[]{:S(2)}) collective-permute-start(bf16[8,2,128,128]{3,2,1,0:T(8,128)(2,1)S(1)} %all-to-all-done.near), channel_id=1, source_target_pairs={{0,8},{8,0},{1,9},{9,1},{2,10},{10,2},{3,11},{11,3},{4,12},{12,4},... | collective-permute-start | bytes 1572872 | tf_op jit(solution)/shard_map/ppermute | solution.py:47
  56.4 1.9 collective-permute-start.2
  58.4 4.6 %collective-permute-start.7 = (bf16[128,896]{1,0:T(8,128)(2,1)S(1)}, bf16[128,896]{1,0:T(8,128)(2,1)S(1)}, u32[]{:S(2)}, u32[]{:S(2)}) collective-permute-start(bf16[128,896]{1,0:T(8,128)(2,1)S(1)} %collective-permute-done.5.refs_4_), channel_id=1, source_target_pairs={{0,3},{1,0},{2,1},{3,2},{4,7},{5,4},{6,5},{7,6},{8,11},{9,8},{10,9... | collective-permute-start | bytes 688136 | tf_op jit(solution)/shard_map/ppermute | solution.py:43
  62.9 8.7 %collective-permute-done.9.refs_8_ = bf16[128,896]{1,0:T(8,128)(2,1)S(1)} collective-permute-done((bf16[128,896]{1,0:T(8,128)(2,1)S(1)}, bf16[128,896]{1,0:T(8,128)(2,1)S(1)}, u32[]{:S(2)}, u32[]{:S(2)}) %collective-permute-start.9) | collective-permute-done | bytes 229408 | tf_op jit(solution)/shard_map/ppermute | solution.py:47
  71.7 3.1 %collective-permute-start.6 = (bf16[128,896]{1,0:T(8,128)(2,1)S(1)}, bf16[128,896]{1,0:T(8,128)(2,1)S(1)}, u32[]{:S(2)}, u32[]{:S(2)}) collective-permute-start(bf16[128,896]{1,0:T(8,128)(2,1)S(1)} %collective-permute-done.5.refs_4_), channel_id=1, source_target_pairs={{0,1},{1,2},{2,3},{3,0},{4,5},{5,6},{6,7},{7,4},{8,9},{9,10},{10,1... | collective-permute-start | bytes 688136 | tf_op jit(solution)/shard_map/ppermute | solution.py:43
  74.8 3.1 %collective-permute-start.10 = (bf16[128,896]{1,0:T(8,128)(2,1)S(1)}, bf16[128,896]{1,0:T(8,128)(2,1)S(1)}, u32[]{:S(2)}, u32[]{:S(2)}) collective-permute-start(bf16[128,896]{1,0:T(8,128)(2,1)S(1)} %collective-permute-done.9.refs_8_), channel_id=1, source_target_pairs={{0,1},{1,2},{2,3},{3,0},{4,5},{5,6},{6,7},{7,4},{8,9},{9,10},{10,1... | collective-permute-start | bytes 688136 | tf_op jit(solution)/shard_map/ppermute | solution.py:43
  77.9 3.4 %collective-permute-start.11 = (bf16[128,896]{1,0:T(8,128)(2,1)S(1)}, bf16[128,896]{1,0:T(8,128)(2,1)S(1)}, u32[]{:S(2)}, u32[]{:S(2)}) collective-permute-start(bf16[128,896]{1,0:T(8,128)(2,1)S(1)} %collective-permute-done.9.refs_8_), channel_id=1, source_target_pairs={{0,3},{1,0},{2,1},{3,2},{4,7},{5,4},{6,5},{7,6},{8,11},{9,8},{10,9... | collective-permute-start | bytes 688136 | tf_op jit(solution)/shard_map/ppermute | solution.py:43
  81.3 1.9 collective-permute-start.4
  83.3 4.6 %collective-permute-start.8 = (bf16[128,896]{1,0:T(8,128)(2,1)S(1)}, bf16[128,896]{1,0:T(8,128)(2,1)S(1)}, u32[]{:S(2)}, u32[]{:S(2)}) collective-permute-start(bf16[128,896]{1,0:T(8,128)(2,1)S(1)} %collective-permute-done.7.refs_6_), channel_id=1, source_target_pairs={{0,3},{1,0},{2,1},{3,2},{4,7},{5,4},{6,5},{7,6},{8,11},{9,8},{10,9... | collective-permute-start | bytes 688136 | tf_op jit(solution)/shard_map/ppermute | solution.py:43
  87.8 1.9 collective-permute-start.12
  91.1 5.1 %collective-permute-done.12.refs_11_ = bf16[128,896]{1,0:T(8,128)(2,1)S(1)} collective-permute-done((bf16[128,896]{1,0:T(8,128)(2,1)S(1)}, bf16[128,896]{1,0:T(8,128)(2,1)S(1)}, u32[]{:S(2)}, u32[]{:S(2)}) %collective-permute-start.12) | collective-permute-done | bytes 229408 | tf_op jit(solution)/shard_map/ppermute | solution.py:43
  99.8 7.4 %shard_map.70 = bf16[8,3,32,896]{3,2,1,0:T(8,128)(2,1)S(1)} custom-call(s32[3]{0:T(128)S(1)} %pad_add_fusion.place, bf16[8,2,128,128]{3,2,1,0:T(8,128)(2,1)S(1)} %all-to-all-done.near, bf16[8,2,128,128]{3,2,1,0:T(8,128)(2,1)S(1)} %copy-done.3, bf16[4,3,128,896]{3,2,1,0:T(8,128)(2,1)S(1)} %bitcast.46, bf16[128,896]{1,0:T(8,128)(2,1)S(1)} %collective-permute-done.1.refs_0_, ...), custom_call_target="tpu_custom_call" | custom-call | flops 1409286144 | bytes 8000000 | tf_op jit(solution)/shard_map/pallas_call | solution.py:20
  107.2 38.1 %all_to_all.20 = bf16[8,3,32,896]{3,2,1,0:T(8,128)(2,1)S(1)} all-to-all(bf16[8,3,32,896]{3,2,1,0:T(8,128)(2,1)S(1)} %shard_map.70), channel_id=1, replica_groups=mesh['y'=8,'zl'=4,'core'=2,'zh'=2,'x'=4] {'y'}, dimensions={0} | all-to-all | bytes 2752512 | tf_op jit(solution)/shard_map/all_to_all | solution.py:178
  145.8 34.7 %all_to_all.21.acts = bf16[8,3,32,896]{3,2,1,0:T(8,128)(2,1)S(1)} all-to-all(bf16[8,3,32,896]{3,2,1,0:T(8,128)(2,1)S(1)} %broadcast_in_dim.2), channel_id=1, replica_groups=mesh['y'=8,'zl'=4,'core'=2,'zh'=2,'x'=4] {'y'}, dimensions={0} | all-to-all | bytes 2752512 | tf_op jit(solution)/shard_map/all_to_all | solution.py:186
  180.5 7.1 %shard_map.71 = (f32[8,2,128,128]{3,2,1,0:T(8,128)S(1)}, f32[8,2,128,128]{3,2,1,0:T(8,128)S(1)}) custom-call(s32[3]{0:T(128)S(1)} %pad_add_fusion.place, bf16[8,3,32,896]{3,2,1,0:T(8,128)(2,1)S(1)} %all_to_all.21.acts, bf16[4,3,128,896]{3,2,1,0:T(8,128)(2,1)S(1)} %bitcast.47, bf16[128,896]{1,0:T(8,128)(2,1)S(1)} %collective-permute-done.1.refs_0_, ...), custom_call_target="tpu_custom_call" | custom-call | flops 1409286144 | bytes 8000000 | tf_op jit(solution)/shard_map/pallas_call | solution.py:20
  187.6 7.6 %collective-permute-start.13 = (f32[8,2,128,128]{3,2,1,0:T(8,128)S(1)}, f32[8,2,128,128]{3,2,1,0:T(8,128)S(1)}, u32[]{:S(2)}, u32[]{:S(2)}) collective-permute-start(f32[8,2,128,128]{3,2,1,0:T(8,128)S(1)} %get-tuple-element.13), channel_id=1, source_target_pairs={{0,8},{8,0},{1,9},{9,1},{2,10},{10,2},{3,11},{11,3},{4,12},{12,4},... | collective-permute-start | bytes 3145736 | tf_op jit(solution)/shard_map/ppermute | solution.py:47
  195.2 2.3 collective-permute-done.13
  197.6 25.7 %all_to_all.22 = bf16[8,2,128,128]{3,2,1,0:T(8,128)(2,1)S(1)} all-to-all(bf16[8,2,128,128]{3,2,1,0:T(8,128)(2,1)S(1)} %add_convert_fusion), channel_id=1, replica_groups=mesh['y'=8,'zl'=4,'core'=2,'zh'=2,'x'=4] {'zh','zl'}, dimensions={0} | all-to-all | bytes 1048576 | tf_op jit(solution)/shard_map/all_to_all | solution.py:195
  (42 shorter events, 12.3 us)
Async XLA Ops:
  7.2 89.8 %all-gather.3.cloned.1.call-start = ((), (), s32[]{:S(2)}) async-start(), calls=%async_computation.4 | async-start | bytes 3440640 | tf_op jit(solution)/shard_map/all_gather | solution.py:156
  7.3 1.0 copy-start.4
  8.3 1.0 copy-start.5
  9.3 1.0 copy-start.6
  10.3 1.5 copy-start.7
  10.4 1.5 copy-start.8
  13.3 39.6 %all-to-all-start = ((bf16[8,2,128,128]{3,2,1,0:T(8,128)(2,1)}), bf16[8,2,128,128]{3,2,1,0:T(8,128)(2,1)S(1)}, u32[]{:S(2)}, u32[]{:S(2)}) async-start(bf16[8,2,128,128]{3,2,1,0:T(8,128)(2,1)} %shard_map.68), calls=%async_computation | async-start | bytes 1048576 | tf_op jit(solution)/shard_map/all_to_all | solution.py:163
  24.2 24.4 %collective-permute-start.1 = (bf16[128,896]{1,0:T(8,128)(2,1)S(1)}, bf16[128,896]{1,0:T(8,128)(2,1)S(1)}, u32[]{:S(2)}, u32[]{:S(2)}) collective-permute-start(bf16[128,896]{1,0:T(8,128)(2,1)S(1)} %get-tuple-element.9), channel_id=1, source_target_pairs={{0,4},{4,0},{1,5},{5,1},{2,6},{6,2},{3,7},{7,3},{8,12},{12,8},{9,1... | collective-permute-start | bytes 688136 | tf_op jit(solution)/shard_map/ppermute | solution.py:47
  31.5 26.9 %collective-permute-start.5 = (bf16[128,896]{1,0:T(8,128)(2,1)S(1)}, bf16[128,896]{1,0:T(8,128)(2,1)S(1)}, u32[]{:S(2)}, u32[]{:S(2)}) collective-permute-start(bf16[128,896]{1,0:T(8,128)(2,1)S(1)} %get-tuple-element.10), channel_id=1, source_target_pairs={{0,4},{4,0},{1,5},{5,1},{2,6},{6,2},{3,7},{7,3},{8,12},{12,8},{9,1... | collective-permute-start | bytes 688136 | tf_op jit(solution)/shard_map/ppermute | solution.py:47
  33.4 38.2 %collective-permute-start.9 = (bf16[128,896]{1,0:T(8,128)(2,1)S(1)}, bf16[128,896]{1,0:T(8,128)(2,1)S(1)}, u32[]{:S(2)}, u32[]{:S(2)}) collective-permute-start(bf16[128,896]{1,0:T(8,128)(2,1)S(1)} %get-tuple-element.11), channel_id=1, source_target_pairs={{0,4},{4,0},{1,5},{5,1},{2,6},{6,2},{3,7},{7,3},{8,12},{12,8},{9,1... | collective-permute-start | bytes 688136 | tf_op jit(solution)/shard_map/ppermute | solution.py:47
  48.6 26.2 %collective-permute-start.3 = (bf16[128,896]{1,0:T(8,128)(2,1)S(1)}, bf16[128,896]{1,0:T(8,128)(2,1)S(1)}, u32[]{:S(2)}, u32[]{:S(2)}) collective-permute-start(bf16[128,896]{1,0:T(8,128)(2,1)S(1)} %collective-permute-done.1.refs_0_), channel_id=1, source_target_pairs={{0,3},{1,0},{2,1},{3,2},{4,7},{5,4},{6,5},{7,6},{8,11},{9,8},{10,9... | collective-permute-start | bytes 688136 | tf_op jit(solution)/shard_map/ppermute | solution.py:43
  53.0 43.2 %collective-permute-start = (bf16[8,2,128,128]{3,2,1,0:T(8,128)(2,1)S(1)}, bf16[8,2,128,128]{3,2,1,0:T(8,128)(2,1)S(1)}, u32[]{:S(2)}, u32[]{:S(2)}) collective-permute-start(bf16[8,2,128,128]{3,2,1,0:T(8,128)(2,1)S(1)} %all-to-all-done.near), channel_id=1, source_target_pairs={{0,8},{8,0},{1,9},{9,1},{2,10},{10,2},{3,11},{11,3},{4,12},{12,4},... | collective-permute-start | bytes 1572872 | tf_op jit(solution)/shard_map/ppermute | solution.py:47
  56.4 21.5 %collective-permute-start.2 = (bf16[128,896]{1,0:T(8,128)(2,1)S(1)}, bf16[128,896]{1,0:T(8,128)(2,1)S(1)}, u32[]{:S(2)}, u32[]{:S(2)}) collective-permute-start(bf16[128,896]{1,0:T(8,128)(2,1)S(1)} %collective-permute-done.1.refs_0_), channel_id=1, source_target_pairs={{0,1},{1,2},{2,3},{3,0},{4,5},{5,6},{6,7},{7,4},{8,9},{9,10},{10,1... | collective-permute-start | bytes 688136 | tf_op jit(solution)/shard_map/ppermute | solution.py:43
  58.4 23.0 %collective-permute-start.7 = (bf16[128,896]{1,0:T(8,128)(2,1)S(1)}, bf16[128,896]{1,0:T(8,128)(2,1)S(1)}, u32[]{:S(2)}, u32[]{:S(2)}) collective-permute-start(bf16[128,896]{1,0:T(8,128)(2,1)S(1)} %collective-permute-done.5.refs_4_), channel_id=1, source_target_pairs={{0,3},{1,0},{2,1},{3,2},{4,7},{5,4},{6,5},{7,6},{8,11},{9,8},{10,9... | collective-permute-start | bytes 688136 | tf_op jit(solution)/shard_map/ppermute | solution.py:43
  71.7 11.6 %collective-permute-start.6 = (bf16[128,896]{1,0:T(8,128)(2,1)S(1)}, bf16[128,896]{1,0:T(8,128)(2,1)S(1)}, u32[]{:S(2)}, u32[]{:S(2)}) collective-permute-start(bf16[128,896]{1,0:T(8,128)(2,1)S(1)} %collective-permute-done.5.refs_4_), channel_id=1, source_target_pairs={{0,1},{1,2},{2,3},{3,0},{4,5},{5,6},{6,7},{7,4},{8,9},{9,10},{10,1... | collective-permute-start | bytes 688136 | tf_op jit(solution)/shard_map/ppermute | solution.py:43
  74.8 13.1 %collective-permute-start.10 = (bf16[128,896]{1,0:T(8,128)(2,1)S(1)}, bf16[128,896]{1,0:T(8,128)(2,1)S(1)}, u32[]{:S(2)}, u32[]{:S(2)}) collective-permute-start(bf16[128,896]{1,0:T(8,128)(2,1)S(1)} %collective-permute-done.9.refs_8_), channel_id=1, source_target_pairs={{0,1},{1,2},{2,3},{3,0},{4,5},{5,6},{6,7},{7,4},{8,9},{9,10},{10,1... | collective-permute-start | bytes 688136 | tf_op jit(solution)/shard_map/ppermute | solution.py:43
  77.9 11.9 %collective-permute-start.11 = (bf16[128,896]{1,0:T(8,128)(2,1)S(1)}, bf16[128,896]{1,0:T(8,128)(2,1)S(1)}, u32[]{:S(2)}, u32[]{:S(2)}) collective-permute-start(bf16[128,896]{1,0:T(8,128)(2,1)S(1)} %collective-permute-done.9.refs_8_), channel_id=1, source_target_pairs={{0,3},{1,0},{2,1},{3,2},{4,7},{5,4},{6,5},{7,6},{8,11},{9,8},{10,9... | collective-permute-start | bytes 688136 | tf_op jit(solution)/shard_map/ppermute | solution.py:43
  81.3 9.2 %collective-permute-start.4 = (bf16[128,896]{1,0:T(8,128)(2,1)S(1)}, bf16[128,896]{1,0:T(8,128)(2,1)S(1)}, u32[]{:S(2)}, u32[]{:S(2)}) collective-permute-start(bf16[128,896]{1,0:T(8,128)(2,1)S(1)} %collective-permute-done.2.refs_1_), channel_id=1, source_target_pairs={{0,1},{1,2},{2,3},{3,0},{4,5},{5,6},{6,7},{7,4},{8,9},{9,10},{10,1... | collective-permute-start | bytes 688136 | tf_op jit(solution)/shard_map/ppermute | solution.py:43
  83.3 7.8 %collective-permute-start.8 = (bf16[128,896]{1,0:T(8,128)(2,1)S(1)}, bf16[128,896]{1,0:T(8,128)(2,1)S(1)}, u32[]{:S(2)}, u32[]{:S(2)}) collective-permute-start(bf16[128,896]{1,0:T(8,128)(2,1)S(1)} %collective-permute-done.7.refs_6_), channel_id=1, source_target_pairs={{0,3},{1,0},{2,1},{3,2},{4,7},{5,4},{6,5},{7,6},{8,11},{9,8},{10,9... | collective-permute-start | bytes 688136 | tf_op jit(solution)/shard_map/ppermute | solution.py:43
  87.8 8.3 %collective-permute-start.12 = (bf16[128,896]{1,0:T(8,128)(2,1)S(1)}, bf16[128,896]{1,0:T(8,128)(2,1)S(1)}, u32[]{:S(2)}, u32[]{:S(2)}) collective-permute-start(bf16[128,896]{1,0:T(8,128)(2,1)S(1)} %collective-permute-done.10.refs_9_), channel_id=1, source_target_pairs={{0,1},{1,2},{2,3},{3,0},{4,5},{5,6},{6,7},{7,4},{8,9},{9,10},{10,1... | collective-permute-start | bytes 688136 | tf_op jit(solution)/shard_map/ppermute | solution.py:43
  96.9 1.8 copy-start
  98.7 1.0 copy-start.3
  145.8 34.7 %copy-start.1 = (bf16[12,128,896]{2,1,0:T(8,128)(2,1)S(1)}, bf16[12,128,896]{2,1,0:T(8,128)(2,1)}, u32[]{:S(2)}) copy-start(bf16[12,128,896]{2,1,0:T(8,128)(2,1)} %all-gather.3.cloned.1.call-done) | copy-start | bytes 8257540
  187.6 9.9 %collective-permute-start.13 = (f32[8,2,128,128]{3,2,1,0:T(8,128)S(1)}, f32[8,2,128,128]{3,2,1,0:T(8,128)S(1)}, u32[]{:S(2)}, u32[]{:S(2)}) collective-permute-start(f32[8,2,128,128]{3,2,1,0:T(8,128)S(1)} %get-tuple-element.13), channel_id=1, source_target_pairs={{0,8},{8,0},{1,9},{9,1},{2,10},{10,2},{3,11},{11,3},{4,12},{12,4},... | collective-permute-start | bytes 3145736 | tf_op jit(solution)/shard_map/ppermute | solution.py:47
  (1 other events, 0.8 us)
Sparse Core Ops, SparseCore 0:
  12.0 50.4 all-gather.2

commit v5 on v1

v5 whole, which is shorter than its diff:
```python
import jax
import jax.numpy as jnp
from jax import lax
from jax.experimental import pallas as pl
from jax.experimental.pallas import tpu as pltpu
from jax.sharding import Mesh, PartitionSpec as P

AXES = ("yh", "yl", "zu", "zv", "core", "zh", "x")
SIZES = (4, 2, 2, 2, 2, 2, 4)
SUMS = ("yh", "zh")
NEAR = ("yl", "zu", "zv")
NT = (((1,), (1,)), ((), ()))
F32, BF16 = jnp.float32, jnp.bfloat16
STEPS = (0, 3, 1, 2)
GATE, DOWN, UP = 0, 1, 2
WHICH = (0, 1, 0)
SMEM = pl.BlockSpec(memory_space=pltpu.SMEM)
VMEM = pl.BlockSpec(memory_space=pltpu.VMEM)
BLOCK = (128, 896)


def call(kernel, outs, operands, scratch, flops, moved):
    return pl.pallas_call(
        kernel,
        out_shape=outs,
        in_specs=[SMEM] + [VMEM] * (len(operands) - 1),
        out_specs=[VMEM] * len(outs),
        scratch_shapes=scratch,
        cost_estimate=pl.CostEstimate(flops=flops, bytes_accessed=moved, transcendentals=0),
        compiler_params=pltpu.CompilerParams(vmem_limit_bytes=24 << 20),
    )(*operands)


def shift(values, step):
    return lax.ppermute(values, "x", [(i, (i + step) % 4) for i in range(4)])


def exchange(values, axis):
    return lax.ppermute(values, axis, [(0, 1), (1, 0)])


def turn(values):
    return lax.ppermute(values, ("zu", "zh"), [(0, 0), (1, 2), (2, 1), (3, 3)])


def split_kernel(place, gate, down, up, keep, send_gate, send_down, send_up):
    low = place[1] == 0
    for k, (weight, send) in enumerate(((gate, send_gate), (down, send_down), (up, send_up))):
        left, right = weight[:, :896], weight[:, 896:]
        keep[k] = jnp.where(low, left, right)
        send[...] = jnp.where(low, right, left)


def acts_kernel(place, acts, out):
    for i in range(8):
        out[i] = acts[...]


def row_block(place, own, slot):
    if own:
        return place[1], slot
    return 1 - place[1], (place[0] + STEPS[slot]) % 4


def sums_kernel(place, near, other, kept, *refs):
    moved, out, wide = refs[:12], refs[12], refs[13]
    for own in (True, False):
        for slot in range(4):
            yl, x = row_block(place, own, slot)
            same = x % 2 == place[2]
            for t in (0, 1):
                i = 4 * yl + 2 * t + x // 2
                for which in (0, 1):
                    tile = jnp.where(same, near[i, which], other[i, which])
                    wide[which, pl.ds(128 * t, 128), pl.ds((0 if own else 512) + 128 * slot, 128)] = tile
    for k in range(3):
        acts = WHICH[k]
        total = jnp.dot(wide[acts, :, :512], kept[:, k].reshape(512, 896), preferred_element_type=F32)
        for pair in (0, 1):
            rows = jnp.concatenate([moved[4 * k + 2 * pair][...], moved[4 * k + 2 * pair + 1][...]], axis=0)
            cols = pl.ds(512 + 256 * pair, 256)
            total = total + jnp.dot(wide[acts, :, cols], rows, preferred_element_type=F32)
        out[:, k] = total.astype(BF16).reshape(8, 32, 896)


def output_kernel(place, acts, kept, *refs):
    moved, mine, theirs, held = refs[:12], refs[12], refs[13], refs[14]
    hidden, gate_grad, up_grad = (acts[:, k].reshape(256, 896) for k in range(3))

    def product(rows, block):
        return lax.dot_general(rows, block, NT, preferred_element_type=F32)

    for own in (True, False):
        for pair in (0, 1):
            if own:
                blocks = [kept[2 * pair : 2 * pair + 2, k].reshape(256, 896) for k in range(3)]
            else:
                blocks = [
                    jnp.concatenate([moved[4 * k + 2 * pair][...], moved[4 * k + 2 * pair + 1][...]], axis=0)
                    for k in range(3)
                ]
            mixed = product(hidden, blocks[DOWN])
            grad = product(gate_grad, blocks[GATE]) + product(up_grad, blocks[UP])
            for slot in (0, 1):
                yl, x = row_block(place, own, 2 * pair + slot)
                side = (x + place[2]) % 2
                for t in (0, 1):
                    part = (slice(128 * t, 128 * t + 128), slice(128 * slot, 128 * slot + 128))
                    held[side, 4 * yl + 2 * t + x // 2, 0] = mixed[part]
                    held[side, 4 * yl + 2 * t + x // 2, 1] = grad[part]
    mine[...] = held[0]
    theirs[...] = held[1]


def on_device(tokens, gate_weight, up_weight, down_weight, grad_mixed):
    place = jnp.stack([lax.axis_index("x"), lax.axis_index("yl"), lax.axis_index("core")])
    block = jax.ShapeDtypeStruct(BLOCK, BF16)
    keep, *sends = call(
        split_kernel,
        [jax.ShapeDtypeStruct((3, *BLOCK), BF16), block, block, block],
        (place, gate_weight, down_weight, up_weight), [], 0, 3000000,
    )
    kept = lax.all_gather(keep, "x", axis=0)
    arrived = [exchange(send, "yl") for send in sends]

    acts = turn(jnp.stack([tokens, grad_mixed]))
    (acts,) = call(
        acts_kernel, [jax.ShapeDtypeStruct((8, 2, 128, 128), BF16)], (place, acts), [], 40000000000, 1000000
    )
    near = lax.all_to_all(acts, NEAR, 0, 0, tiled=True)
    other = exchange(near, "core")

    moved = []
    for k, block in enumerate(arrived):
        left, right = shift(block, 1), shift(block, -1)
        moved += [block, left, right, shift(right, -1) if k == DOWN else shift(left, 1)]

    (parts,) = call(
        sums_kernel, [jax.ShapeDtypeStruct((8, 3, 32, 896), BF16)], (place, near, other, kept, *moved),
        [pltpu.VMEM((2, 256, 1024), BF16)], 6 * 256 * 1024 * 896, 8000000,
    )
    parts = lax.all_to_all(parts, SUMS, 0, 0, tiled=True)
    gate_value, hidden_grad, up_value = (jnp.sum(parts[:, k].astype(F32), axis=0) for k in range(3))
    sig = jax.nn.sigmoid(gate_value)
    silu = gate_value * sig
    hidden = (silu * up_value).astype(BF16)
    gate_grad = (hidden_grad * up_value * sig * (1.0 + gate_value * (1.0 - sig))).astype(BF16)
    up_grad = (hidden_grad * silu).astype(BF16)
    rows = jnp.stack([hidden, gate_grad, up_grad])
    rows = lax.all_to_all(jnp.broadcast_to(rows[None], (8, 3, 32, 896)), SUMS, 0, 0, tiled=True)
    terms = jax.ShapeDtypeStruct((8, 2, 128, 128), F32)
    mine, theirs = call(
        output_kernel, [terms, terms], (place, rows, kept, *moved),
        [pltpu.VMEM((2, 8, 2, 128, 128), F32)], 6 * 256 * 1024 * 896, 8000000,
    )
    terms = (mine + exchange(theirs, "core")).astype(BF16)
    terms = lax.all_to_all(terms, NEAR, 0, 0, tiled=True)
    both = turn(jnp.sum(terms.astype(F32), axis=0).astype(BF16))
    return both[0], both[1]


def solution(mesh):
    fine = Mesh(mesh.devices.reshape(SIZES), AXES)
    acts = P(("zh", "x"), ("yh", "yl", "zu", "zv", "core"))
    weights = P(("yh", "yl", "zh", "x"), ("zu", "zv", "core"))
    return jax.shard_map(
        on_device,
        mesh=fine,
        in_specs=(acts, weights, weights, weights, acts),
        out_specs=(acts, acts),
        check_vma=False,
    )
```

time: 281 us -> 227 us (0.81)
  the two profiles are of different devices: /device:TPU:1 before, /device:TPU:152 now
where the time goes in v5:
time: 227 us; the launch traced here: 226 us
  blocking collectives  110 us (48%)
  starting transfers between devices  54.6 us (24%)
  waiting for transfers between devices  30.8 us (14%)
  between operations  14.3 us (6%)
  Pallas kernels  7.81 us (3%)
  local copies, waits for them, and re-layouts  7.39 us (3%)
    all_to_all x1, blocking collectives, on_device(): lax.all_to_all(jnp.broadcast_to(rows[None], (8, 3, 32, 896)), SUMS, 0, 0,...  46.1 us
    all_to_all x1, blocking collectives, on_device(): parts = lax.all_to_all(parts, SUMS, 0, 0, tiled=True)  44.2 us
    ppermute x9, starting transfers between devices, shift(): return lax.ppermute(values, 'x', [(i, (i + step) % 4) for i in range(4)])  26.1 us
    all_to_all x1, blocking collectives, on_device(): terms = lax.all_to_all(terms, NEAR, 0, 0, tiled=True)  19.4 us
    ppermute x9, waiting for transfers between devices, shift(): return lax.ppermute(values, 'x', [(i, (i + step) % 4) for i in range(4)])  17.1 us
    ppermute x5, starting transfers between devices, exchange(): return lax.ppermute(values, axis, [(0, 1), (1, 0)])  12.1 us
    ppermute x2, starting transfers between devices, turn(): return lax.ppermute(values, ('zu', 'zh'), [(0, 0), (1, 2), (2, 1), (3, 3)])  10.3 us
    pallas_call x4, Pallas kernels, call(): pl.pallas_call(kernel, out_shape=outs, in_specs=[SMEM] + [VMEM] * (len(op...  7.81 us
  transfers between devices with their start and end apart: 18, of which 8 were waited for; matrix products, arithmetic and copies ran while one was open for 0% of the time, Pallas kernels for 1%

profile of v5, /device:TPU:152, one launch (start us, length us, event | category | flops | bytes accessed | tf_op | source)
XLA Modules:
  0.0 225.9 jit_solution(7975733693081728207)
XLA Ops:
  8.0 7.3 %collective-permute-start = (bf16[2,128,128]{2,1,0:T(8,128)(2,1)S(1)}, bf16[2,128,128]{2,1,0:T(8,128)(2,1)S(1)}, u32[]{:S(2)}, u32[]{:S(2)}) collective-permute-start(bf16[2,128,128]{2,1,0:T(8,128)(2,1)S(1)} %pad_maximum_fusion.1), channel_id=1, source_target_pairs={{0,0},{4,32},{32,4},{36,36},{1,1},{5,33},{33,5},{37,37},{2,2},{6,3... | collective-permute-start | bytes 196616 | tf_op jit(solution)/shard_map/ppermute | solution.py:43
  21.4 6.0 %all-to-all-start = ((bf16[8,2,128,128]{3,2,1,0:T(8,128)(2,1)}), bf16[8,2,128,128]{3,2,1,0:T(8,128)(2,1)S(1)}, u32[]{:S(2)}, u32[]{:S(2)}) async-start(bf16[8,2,128,128]{3,2,1,0:T(8,128)(2,1)} %shard_map.68), calls=%async_computation | async-start | bytes 1048576 | tf_op jit(solution)/shard_map/all_to_all | solution.py:130
  27.4 2.5 %collective-permute-start.2 = (bf16[128,896]{1,0:T(8,128)(2,1)S(1)}, bf16[128,896]{1,0:T(8,128)(2,1)S(1)}, u32[]{:S(2)}, u32[]{:S(2)}) collective-permute-start(bf16[128,896]{1,0:T(8,128)(2,1)S(1)} %get-tuple-element.9), channel_id=1, source_target_pairs={{0,64},{64,0},{1,65},{65,1},{2,66},{66,2},{3,67},{67,3},{4,68},{68... | collective-permute-start | bytes 688136 | tf_op jit(solution)/shard_map/ppermute | solution.py:39
  29.8 3.4 %collective-permute-start.6 = (bf16[128,896]{1,0:T(8,128)(2,1)S(1)}, bf16[128,896]{1,0:T(8,128)(2,1)S(1)}, u32[]{:S(2)}, u32[]{:S(2)}) collective-permute-start(bf16[128,896]{1,0:T(8,128)(2,1)S(1)} %get-tuple-element.10), channel_id=1, source_target_pairs={{0,64},{64,0},{1,65},{65,1},{2,66},{66,2},{3,67},{67,3},{4,68},{68... | collective-permute-start | bytes 688136 | tf_op jit(solution)/shard_map/ppermute | solution.py:39
  33.2 2.5 %collective-permute-start.10 = (bf16[128,896]{1,0:T(8,128)(2,1)S(1)}, bf16[128,896]{1,0:T(8,128)(2,1)S(1)}, u32[]{:S(2)}, u32[]{:S(2)}) collective-permute-start(bf16[128,896]{1,0:T(8,128)(2,1)S(1)} %get-tuple-element.11), channel_id=1, source_target_pairs={{0,64},{64,0},{1,65},{65,1},{2,66},{66,2},{3,67},{67,3},{4,68},{68... | collective-permute-start | bytes 688136 | tf_op jit(solution)/shard_map/ppermute | solution.py:39
  35.7 4.6 %collective-permute-done.2.refs_0_ = bf16[128,896]{1,0:T(8,128)(2,1)S(1)} collective-permute-done((bf16[128,896]{1,0:T(8,128)(2,1)S(1)}, bf16[128,896]{1,0:T(8,128)(2,1)S(1)}, u32[]{:S(2)}, u32[]{:S(2)}) %collective-permute-start.2) | collective-permute-done | bytes 229408 | tf_op jit(solution)/shard_map/ppermute | solution.py:39
  40.3 4.7 %collective-permute-start.4 = (bf16[128,896]{1,0:T(8,128)(2,1)S(1)}, bf16[128,896]{1,0:T(8,128)(2,1)S(1)}, u32[]{:S(2)}, u32[]{:S(2)}) collective-permute-start(bf16[128,896]{1,0:T(8,128)(2,1)S(1)} %collective-permute-done.2.refs_0_), channel_id=1, source_target_pairs={{0,3},{1,0},{2,1},{3,2},{4,7},{5,4},{6,5},{7,6},{8,11},{9,8},{10,9... | collective-permute-start | bytes 688136 | tf_op jit(solution)/shard_map/ppermute | solution.py:35
  44.9 1.9 collective-permute-start.1
  48.8 5.1 %collective-permute-start.8 = (bf16[128,896]{1,0:T(8,128)(2,1)S(1)}, bf16[128,896]{1,0:T(8,128)(2,1)S(1)}, u32[]{:S(2)}, u32[]{:S(2)}) collective-permute-start(bf16[128,896]{1,0:T(8,128)(2,1)S(1)} %collective-permute-done.6.refs_4_), channel_id=1, source_target_pairs={{0,3},{1,0},{2,1},{3,2},{4,7},{5,4},{6,5},{7,6},{8,11},{9,8},{10,9... | collective-permute-start | bytes 688136 | tf_op jit(solution)/shard_map/ppermute | solution.py:35
  55.9 2.0 collective-permute-start.11
  57.9 5.4 %collective-permute-done.3.refs_1_ = bf16[128,896]{1,0:T(8,128)(2,1)S(1)} collective-permute-done((bf16[128,896]{1,0:T(8,128)(2,1)S(1)}, bf16[128,896]{1,0:T(8,128)(2,1)S(1)}, u32[]{:S(2)}, u32[]{:S(2)}) %collective-permute-start.3) | collective-permute-done | bytes 229408 | tf_op jit(solution)/shard_map/ppermute | solution.py:35
  65.2 3.9 %collective-permute-start.5 = (bf16[128,896]{1,0:T(8,128)(2,1)S(1)}, bf16[128,896]{1,0:T(8,128)(2,1)S(1)}, u32[]{:S(2)}, u32[]{:S(2)}) collective-permute-start(bf16[128,896]{1,0:T(8,128)(2,1)S(1)} %collective-permute-done.3.refs_1_), channel_id=1, source_target_pairs={{0,1},{1,2},{2,3},{3,0},{4,5},{5,6},{6,7},{7,4},{8,9},{9,10},{10,1... | collective-permute-start | bytes 688136 | tf_op jit(solution)/shard_map/ppermute | solution.py:35
  70.3 2.7 %collective-permute-start.9 = (bf16[128,896]{1,0:T(8,128)(2,1)S(1)}, bf16[128,896]{1,0:T(8,128)(2,1)S(1)}, u32[]{:S(2)}, u32[]{:S(2)}) collective-permute-start(bf16[128,896]{1,0:T(8,128)(2,1)S(1)} %collective-permute-done.8.refs_6_), channel_id=1, source_target_pairs={{0,3},{1,0},{2,1},{3,2},{4,7},{5,4},{6,5},{7,6},{8,11},{9,8},{10,9... | collective-permute-start | bytes 688136 | tf_op jit(solution)/shard_map/ppermute | solution.py:35
  73.0 2.2 collective-permute-done.11.refs_9_
  77.1 2.8 %collective-permute-done.5.refs_3_ = bf16[128,896]{1,0:T(8,128)(2,1)S(1)} collective-permute-done((bf16[128,896]{1,0:T(8,128)(2,1)S(1)}, bf16[128,896]{1,0:T(8,128)(2,1)S(1)}, u32[]{:S(2)}, u32[]{:S(2)}) %collective-permute-start.5) | collective-permute-done | bytes 229408 | tf_op jit(solution)/shard_map/ppermute | solution.py:35
  80.0 5.6 %collective-permute-done.13.refs_11_ = bf16[128,896]{1,0:T(8,128)(2,1)S(1)} collective-permute-done((bf16[128,896]{1,0:T(8,128)(2,1)S(1)}, bf16[128,896]{1,0:T(8,128)(2,1)S(1)}, u32[]{:S(2)}, u32[]{:S(2)}) %collective-permute-start.13) | collective-permute-done | bytes 229408 | tf_op jit(solution)/shard_map/ppermute | solution.py:35
  89.2 2.4 %shard_map.70 = bf16[8,3,32,896]{3,2,1,0:T(8,128)(2,1)S(1)} custom-call(s32[3]{0:T(128)S(1)} %pad_add_fusion.place, bf16[8,2,128,128]{3,2,1,0:T(8,128)(2,1)S(1)} %all-to-all-done.near, bf16[8,2,128,128]{3,2,1,0:T(8,128)(2,1)S(1)} %copy-done.3, bf16[4,3,128,896]{3,2,1,0:T(8,128)(2,1)S(1)} %bitcast.48, bf16[128,896]{1,0:T(8,128)(2,1)S(1)} %collective-permute-done.2.refs_0_, ...), custom_call_target="tpu_custom_call" | custom-call | flops 1409286144 | bytes 8000000 | tf_op jit(solution)/shard_map/pallas_call | solution.py:23
  91.6 44.2 %all_to_all.20 = bf16[8,3,32,896]{3,2,1,0:T(8,128)(2,1)S(1)} all-to-all(bf16[8,3,32,896]{3,2,1,0:T(8,128)(2,1)S(1)} %shard_map.70), channel_id=1, replica_groups=mesh['yh'=4,'yl'=2,'zu'=2,'zv'=2,'core'=2,'zh'=2,'x'=4] {'yh','zh'}, dimensions={0} | all-to-all | bytes 2752512 | tf_op jit(solution)/shard_map/all_to_all | solution.py:142
  136.2 46.1 %all_to_all.21.acts = bf16[8,3,32,896]{3,2,1,0:T(8,128)(2,1)S(1)} all-to-all(bf16[8,3,32,896]{3,2,1,0:T(8,128)(2,1)S(1)} %broadcast_in_dim.2), channel_id=1, replica_groups=mesh['yh'=4,'yl'=2,'zu'=2,'zv'=2,'core'=2,'zh'=2,'x'=4] {'yh','zh'}, dimensions={0} | all-to-all | bytes 2752512 | tf_op jit(solution)/shard_map/all_to_all | solution.py:150
  182.3 2.5 %shard_map.71 = (f32[8,2,128,128]{3,2,1,0:T(8,128)S(1)}, f32[8,2,128,128]{3,2,1,0:T(8,128)S(1)}) custom-call(s32[3]{0:T(128)S(1)} %pad_add_fusion.place, bf16[8,3,32,896]{3,2,1,0:T(8,128)(2,1)S(1)} %all_to_all.21.acts, bf16[4,3,128,896]{3,2,1,0:T(8,128)(2,1)S(1)} %bitcast.49, bf16[128,896]{1,0:T(8,128)(2,1)S(1)} %collective-permute-done.2.refs_0_, ...), custom_call_target="tpu_custom_call" | custom-call | flops 1409286144 | bytes 8000000 | tf_op jit(solution)/shard_map/pallas_call | solution.py:23
  186.8 2.6 %collective-permute-done.14 = f32[8,2,128,128]{3,2,1,0:T(8,128)S(1)} collective-permute-done((f32[8,2,128,128]{3,2,1,0:T(8,128)S(1)}, f32[8,2,128,128]{3,2,1,0:T(8,128)S(1)}, u32[]{:S(2)}, u32[]{:S(2)}) %collective-permute-start.14) | collective-permute-done | bytes 1048608 | tf_op jit(solution)/shard_map/ppermute | solution.py:39
  189.5 19.4 %all_to_all.22 = bf16[8,2,128,128]{3,2,1,0:T(8,128)(2,1)S(1)} all-to-all(bf16[8,2,128,128]{3,2,1,0:T(8,128)(2,1)S(1)} %add_convert_fusion), channel_id=1, replica_groups=mesh['yh'=4,'yl'=2,'zu'=2,'zv'=2,'core'=2,'zh'=2,'x'=4] {'yl','zu','zv'}, dimensions={0} | all-to-all | bytes 1048576 | tf_op jit(solution)/shard_map/all_to_all | solution.py:157
  209.0 3.0 %collective-permute-start.15 = (bf16[2,128,128]{2,1,0:T(8,128)(2,1)S(1)}, bf16[2,128,128]{2,1,0:T(8,128)(2,1)S(1)}, u32[]{:S(2)}, u32[]{:S(2)}) collective-permute-start(bf16[2,128,128]{2,1,0:T(8,128)(2,1)S(1)} %reduce_sum.51), channel_id=1, source_target_pairs={{0,0},{4,32},{32,4},{36,36},{1,1},{5,33},{33,5},{37,37},{2,2},{6,3... | collective-permute-start | bytes 196616 | tf_op jit(solution)/shard_map/ppermute | solution.py:43
  212.0 6.4 %collective-permute-done.15 = bf16[2,128,128]{2,1,0:T(8,128)(2,1)S(1)} collective-permute-done((bf16[2,128,128]{2,1,0:T(8,128)(2,1)S(1)}, bf16[2,128,128]{2,1,0:T(8,128)(2,1)S(1)}, u32[]{:S(2)}, u32[]{:S(2)}) %collective-permute-start.15) | collective-permute-done | bytes 65568 | tf_op jit(solution)/shard_map/ppermute | solution.py:43
  (43 shorter events, 22.4 us)
Async XLA Ops:
  7.2 79.2 %all-gather.3.cloned.1.call-start = ((), (), s32[]{:S(2)}) async-start(), calls=%async_computation.4 | async-start | bytes 3440640 | tf_op jit(solution)/shard_map/all_gather | solution.py:123
  8.0 12.0 %collective-permute-start = (bf16[2,128,128]{2,1,0:T(8,128)(2,1)S(1)}, bf16[2,128,128]{2,1,0:T(8,128)(2,1)S(1)}, u32[]{:S(2)}, u32[]{:S(2)}) collective-permute-start(bf16[2,128,128]{2,1,0:T(8,128)(2,1)S(1)} %pad_maximum_fusion.1), channel_id=1, source_target_pairs={{0,0},{4,32},{32,4},{36,36},{1,1},{5,33},{33,5},{37,37},{2,2},{6,3... | collective-permute-start | bytes 196616 | tf_op jit(solution)/shard_map/ppermute | solution.py:43
  15.4 1.0 copy-start.4
  16.4 1.0 copy-start.5
  17.4 1.0 copy-start.6
  21.4 23.6 %all-to-all-start = ((bf16[8,2,128,128]{3,2,1,0:T(8,128)(2,1)}), bf16[8,2,128,128]{3,2,1,0:T(8,128)(2,1)S(1)}, u32[]{:S(2)}, u32[]{:S(2)}) async-start(bf16[8,2,128,128]{3,2,1,0:T(8,128)(2,1)} %shard_map.68), calls=%async_computation | async-start | bytes 1048576 | tf_op jit(solution)/shard_map/all_to_all | solution.py:130
  27.4 12.9 %collective-permute-start.2 = (bf16[128,896]{1,0:T(8,128)(2,1)S(1)}, bf16[128,896]{1,0:T(8,128)(2,1)S(1)}, u32[]{:S(2)}, u32[]{:S(2)}) collective-permute-start(bf16[128,896]{1,0:T(8,128)(2,1)S(1)} %get-tuple-element.9), channel_id=1, source_target_pairs={{0,64},{64,0},{1,65},{65,1},{2,66},{66,2},{3,67},{67,3},{4,68},{68... | collective-permute-start | bytes 688136 | tf_op jit(solution)/shard_map/ppermute | solution.py:39
  29.8 19.0 %collective-permute-start.6 = (bf16[128,896]{1,0:T(8,128)(2,1)S(1)}, bf16[128,896]{1,0:T(8,128)(2,1)S(1)}, u32[]{:S(2)}, u32[]{:S(2)}) collective-permute-start(bf16[128,896]{1,0:T(8,128)(2,1)S(1)} %get-tuple-element.10), channel_id=1, source_target_pairs={{0,64},{64,0},{1,65},{65,1},{2,66},{66,2},{3,67},{67,3},{4,68},{68... | collective-permute-start | bytes 688136 | tf_op jit(solution)/shard_map/ppermute | solution.py:39
  33.2 20.7 %collective-permute-start.10 = (bf16[128,896]{1,0:T(8,128)(2,1)S(1)}, bf16[128,896]{1,0:T(8,128)(2,1)S(1)}, u32[]{:S(2)}, u32[]{:S(2)}) collective-permute-start(bf16[128,896]{1,0:T(8,128)(2,1)S(1)} %get-tuple-element.11), channel_id=1, source_target_pairs={{0,64},{64,0},{1,65},{65,1},{2,66},{66,2},{3,67},{67,3},{4,68},{68... | collective-permute-start | bytes 688136 | tf_op jit(solution)/shard_map/ppermute | solution.py:39
  40.3 15.6 %collective-permute-start.4 = (bf16[128,896]{1,0:T(8,128)(2,1)S(1)}, bf16[128,896]{1,0:T(8,128)(2,1)S(1)}, u32[]{:S(2)}, u32[]{:S(2)}) collective-permute-start(bf16[128,896]{1,0:T(8,128)(2,1)S(1)} %collective-permute-done.2.refs_0_), channel_id=1, source_target_pairs={{0,3},{1,0},{2,1},{3,2},{4,7},{5,4},{6,5},{7,6},{8,11},{9,8},{10,9... | collective-permute-start | bytes 688136 | tf_op jit(solution)/shard_map/ppermute | solution.py:35
  44.9 40.7 %collective-permute-start.1 = (bf16[8,2,128,128]{3,2,1,0:T(8,128)(2,1)S(1)}, bf16[8,2,128,128]{3,2,1,0:T(8,128)(2,1)S(1)}, u32[]{:S(2)}, u32[]{:S(2)}) collective-permute-start(bf16[8,2,128,128]{3,2,1,0:T(8,128)(2,1)S(1)} %all-to-all-done.near), channel_id=1, source_target_pairs={{0,8},{8,0},{1,9},{9,1},{2,10},{10,2},{3,11},{11,3},{4,12},{12,4},... | collective-permute-start | bytes 1572872 | tf_op jit(solution)/shard_map/ppermute | solution.py:39
  46.9 16.5 %collective-permute-start.3 = (bf16[128,896]{1,0:T(8,128)(2,1)S(1)}, bf16[128,896]{1,0:T(8,128)(2,1)S(1)}, u32[]{:S(2)}, u32[]{:S(2)}) collective-permute-start(bf16[128,896]{1,0:T(8,128)(2,1)S(1)} %collective-permute-done.2.refs_0_), channel_id=1, source_target_pairs={{0,1},{1,2},{2,3},{3,0},{4,5},{5,6},{6,7},{7,4},{8,9},{9,10},{10,1... | collective-permute-start | bytes 688136 | tf_op jit(solution)/shard_map/ppermute | solution.py:35
  48.8 16.4 %collective-permute-start.8 = (bf16[128,896]{1,0:T(8,128)(2,1)S(1)}, bf16[128,896]{1,0:T(8,128)(2,1)S(1)}, u32[]{:S(2)}, u32[]{:S(2)}) collective-permute-start(bf16[128,896]{1,0:T(8,128)(2,1)S(1)} %collective-permute-done.6.refs_4_), channel_id=1, source_target_pairs={{0,3},{1,0},{2,1},{3,2},{4,7},{5,4},{6,5},{7,6},{8,11},{9,8},{10,9... | collective-permute-start | bytes 688136 | tf_op jit(solution)/shard_map/ppermute | solution.py:35
  54.0 16.3 %collective-permute-start.7 = (bf16[128,896]{1,0:T(8,128)(2,1)S(1)}, bf16[128,896]{1,0:T(8,128)(2,1)S(1)}, u32[]{:S(2)}, u32[]{:S(2)}) collective-permute-start(bf16[128,896]{1,0:T(8,128)(2,1)S(1)} %collective-permute-done.6.refs_4_), channel_id=1, source_target_pairs={{0,1},{1,2},{2,3},{3,0},{4,5},{5,6},{6,7},{7,4},{8,9},{9,10},{10,1... | collective-permute-start | bytes 688136 | tf_op jit(solution)/shard_map/ppermute | solution.py:35
  55.9 19.3 %collective-permute-start.11 = (bf16[128,896]{1,0:T(8,128)(2,1)S(1)}, bf16[128,896]{1,0:T(8,128)(2,1)S(1)}, u32[]{:S(2)}, u32[]{:S(2)}) collective-permute-start(bf16[128,896]{1,0:T(8,128)(2,1)S(1)} %collective-permute-done.10.refs_8_), channel_id=1, source_target_pairs={{0,1},{1,2},{2,3},{3,0},{4,5},{5,6},{6,7},{7,4},{8,9},{9,10},{10,1... | collective-permute-start | bytes 688136 | tf_op jit(solution)/shard_map/ppermute | solution.py:35
  63.3 13.8 %collective-permute-start.12 = (bf16[128,896]{1,0:T(8,128)(2,1)S(1)}, bf16[128,896]{1,0:T(8,128)(2,1)S(1)}, u32[]{:S(2)}, u32[]{:S(2)}) collective-permute-start(bf16[128,896]{1,0:T(8,128)(2,1)S(1)} %collective-permute-done.10.refs_8_), channel_id=1, source_target_pairs={{0,3},{1,0},{2,1},{3,2},{4,7},{5,4},{6,5},{7,6},{8,11},{9,8},{10,9... | collective-permute-start | bytes 688136 | tf_op jit(solution)/shard_map/ppermute | solution.py:35
  65.2 14.7 %collective-permute-start.5 = (bf16[128,896]{1,0:T(8,128)(2,1)S(1)}, bf16[128,896]{1,0:T(8,128)(2,1)S(1)}, u32[]{:S(2)}, u32[]{:S(2)}) collective-permute-start(bf16[128,896]{1,0:T(8,128)(2,1)S(1)} %collective-permute-done.3.refs_1_), channel_id=1, source_target_pairs={{0,1},{1,2},{2,3},{3,0},{4,5},{5,6},{6,7},{7,4},{8,9},{9,10},{10,1... | collective-permute-start | bytes 688136 | tf_op jit(solution)/shard_map/ppermute | solution.py:35
  70.3 9.7 %collective-permute-start.9 = (bf16[128,896]{1,0:T(8,128)(2,1)S(1)}, bf16[128,896]{1,0:T(8,128)(2,1)S(1)}, u32[]{:S(2)}, u32[]{:S(2)}) collective-permute-start(bf16[128,896]{1,0:T(8,128)(2,1)S(1)} %collective-permute-done.8.refs_6_), channel_id=1, source_target_pairs={{0,3},{1,0},{2,1},{3,2},{4,7},{5,4},{6,5},{7,6},{8,11},{9,8},{10,9... | collective-permute-start | bytes 688136 | tf_op jit(solution)/shard_map/ppermute | solution.py:35
  75.2 10.4 %collective-permute-start.13 = (bf16[128,896]{1,0:T(8,128)(2,1)S(1)}, bf16[128,896]{1,0:T(8,128)(2,1)S(1)}, u32[]{:S(2)}, u32[]{:S(2)}) collective-permute-start(bf16[128,896]{1,0:T(8,128)(2,1)S(1)} %collective-permute-done.11.refs_9_), channel_id=1, source_target_pairs={{0,1},{1,2},{2,3},{3,0},{4,5},{5,6},{6,7},{7,4},{8,9},{9,10},{10,1... | collective-permute-start | bytes 688136 | tf_op jit(solution)/shard_map/ppermute | solution.py:35
  86.4 1.8 copy-start
  88.2 1.0 copy-start.3
  136.2 46.1 %copy-start.1 = (bf16[12,128,896]{2,1,0:T(8,128)(2,1)S(1)}, bf16[12,128,896]{2,1,0:T(8,128)(2,1)}, u32[]{:S(2)}) copy-start(bf16[12,128,896]{2,1,0:T(8,128)(2,1)} %all-gather.3.cloned.1.call-done) | copy-start | bytes 8257540
  184.8 4.6 %collective-permute-start.14 = (f32[8,2,128,128]{3,2,1,0:T(8,128)S(1)}, f32[8,2,128,128]{3,2,1,0:T(8,128)S(1)}, u32[]{:S(2)}, u32[]{:S(2)}) collective-permute-start(f32[8,2,128,128]{3,2,1,0:T(8,128)S(1)} %get-tuple-element.13), channel_id=1, source_target_pairs={{0,8},{8,0},{1,9},{9,1},{2,10},{10,2},{3,11},{11,3},{4,12},{12,4},... | collective-permute-start | bytes 3145736 | tf_op jit(solution)/shard_map/ppermute | solution.py:39
  209.0 9.4 %collective-permute-start.15 = (bf16[2,128,128]{2,1,0:T(8,128)(2,1)S(1)}, bf16[2,128,128]{2,1,0:T(8,128)(2,1)S(1)}, u32[]{:S(2)}, u32[]{:S(2)}) collective-permute-start(bf16[2,128,128]{2,1,0:T(8,128)(2,1)S(1)} %reduce_sum.51), channel_id=1, source_target_pairs={{0,0},{4,32},{32,4},{36,36},{1,1},{5,33},{33,5},{37,37},{2,2},{6,3... | collective-permute-start | bytes 196616 | tf_op jit(solution)/shard_map/ppermute | solution.py:43
  (1 other events, 0.8 us)
Sparse Core Ops, SparseCore 0:
  20.1 51.2 all-gather.2

commit v6 on v5

v6 whole, which is shorter than its diff:
```python
import jax
import jax.numpy as jnp
from jax import lax
from jax.experimental import pallas as pl
from jax.experimental.pallas import tpu as pltpu
from jax.sharding import Mesh, PartitionSpec as P

AXES = ("yh", "yl", "zl", "core", "zh", "x")
SIZES = (4, 2, 4, 2, 2, 4)
RING = ("yl", "zl", "zh")
NT = (((1,), (1,)), ((), ()))
F32, BF16 = jnp.float32, jnp.bfloat16
STEPS = (0, 3, 1, 2)
GATE, DOWN, UP = 0, 1, 2
WHICH = (0, 1, 0)
SMEM = pl.BlockSpec(memory_space=pltpu.SMEM)
VMEM = pl.BlockSpec(memory_space=pltpu.VMEM)


def call(kernel, outs, operands, scratch, flops, moved):
    return pl.pallas_call(
        kernel,
        out_shape=outs,
        in_specs=[SMEM] + [VMEM] * (len(operands) - 1),
        out_specs=[VMEM] * len(outs),
        scratch_shapes=scratch,
        cost_estimate=pl.CostEstimate(flops=flops, bytes_accessed=moved, transcendentals=0),
        compiler_params=pltpu.CompilerParams(vmem_limit_bytes=24 << 20),
    )(*operands)


def shift(values, step):
    return lax.ppermute(values, "x", [(i, (i + step) % 4) for i in range(4)])


def exchange(values):
    return lax.ppermute(values, "core", [(0, 1), (1, 0)])


def turn(values):
    return lax.ppermute(values, ("yl", "core"), [(0, 0), (1, 2), (2, 1), (3, 3)])


def turn_across(values):
    pairs = [(4 * a + 2 * b + z, 4 * b + 2 * a + 1 - z) for a in (0, 1) for b in (0, 1) for z in (0, 1)]
    return lax.ppermute(values, ("yl", "core", "zh"), pairs)


def split_kernel(place, gate, down, up, keep, send):
    low = place[1] == 0
    for k, weight in enumerate((gate, down, up)):
        left, right = weight[:, :896], weight[:, 896:]
        rows = pl.ds(128 * k, 128)
        keep[rows] = jnp.where(low, left, right)
        send[rows] = jnp.where(low, right, left)


def acts_kernel(place, acts, out):
    for i in range(16):
        out[i] = acts[...]


def tile_index(place, own, slot, half):
    x = slot if own else (place[0] + STEPS[slot]) % 4
    zh = place[1] if own else 1 - place[1]
    t = place[2] if half == 0 else 1 - place[2]
    return 8 * (x % 2) + 2 * (2 * zh + x // 2) + t


def moved_rows(k, slot, block, left, right, far_low, far_high):
    if slot < 3:
        return (block, left, right)[slot][128 * k : 128 * k + 128]
    if k == 1:
        return jnp.concatenate([far_low[128:], far_high[:64]], axis=0)
    return far_low[:128] if k == 0 else far_high[64:]


def sums_kernel(place, acts, kept, *refs):
    moved, mine, theirs, wide = refs[:5], refs[5], refs[6], refs[7]
    for own in (True, False):
        for slot in range(4):
            for half in (0, 1):
                for which in (0, 1):
                    cols = pl.ds((0 if own else 512) + 128 * slot, 128)
                    wide[which, pl.ds(128 * half, 128), cols] = acts[tile_index(place, own, slot, half), which]
    for k in range(3):
        tokens = WHICH[k]
        rows = kept[:, pl.ds(128 * k, 128)].reshape(512, 896)
        total = jnp.dot(wide[tokens, :, :512], rows, preferred_element_type=F32)
        for pair in (0, 1):
            rows = jnp.concatenate([moved_rows(k, 2 * pair + i, *moved) for i in (0, 1)], axis=0)
            total = total + jnp.dot(wide[tokens, :, pl.ds(512 + 256 * pair, 256)], rows, preferred_element_type=F32)
        mine[:, k] = total[:128].reshape(4, 32, 896)
        theirs[:, k] = total[128:].reshape(4, 32, 896)


def output_kernel(place, near, other, kept, *refs):
    moved, out = refs[:5], refs[5]
    hidden, gate_grad, up_grad = (
        jnp.concatenate([near[:, k].reshape(128, 896), other[:, k].reshape(128, 896)], axis=0) for k in range(3)
    )

    def product(rows, block):
        return lax.dot_general(rows, block, NT, preferred_element_type=F32)

    for own in (True, False):
        for pair in (0, 1):
            if own:
                blocks = [kept[2 * pair : 2 * pair + 2, pl.ds(128 * k, 128)].reshape(256, 896) for k in range(3)]
            else:
                blocks = [
                    jnp.concatenate([moved_rows(k, 2 * pair + i, *moved) for i in (0, 1)], axis=0) for k in range(3)
                ]
            mixed = product(hidden, blocks[DOWN])
            grad = product(gate_grad, blocks[GATE]) + product(up_grad, blocks[UP])
            for slot in (0, 1):
                for half in (0, 1):
                    part = (slice(128 * half, 128 * half + 128), slice(128 * slot, 128 * slot + 128))
                    i = tile_index(place, own, 2 * pair + slot, half)
                    out[i, 0] = mixed[part].astype(BF16)
                    out[i, 1] = grad[part].astype(BF16)


def on_device(tokens, gate_weight, up_weight, down_weight, grad_mixed):
    place = jnp.stack([lax.axis_index("x"), lax.axis_index("zh"), lax.axis_index("core")])
    half = jax.ShapeDtypeStruct((384, 896), BF16)
    keep, send = call(split_kernel, [half, half], (place, gate_weight, down_weight, up_weight), [], 0, 3000000)
    block = turn_across(send)
    kept = lax.all_gather(turn(keep), "x", axis=0)

    acts = turn(jnp.stack([tokens, grad_mixed]))
    (acts,) = call(
        acts_kernel, [jax.ShapeDtypeStruct((16, 2, 128, 128), BF16)], (place, acts), [], 20000000000, 1000000
    )
    acts, _ = lax.optimization_barrier((acts, block))
    acts = lax.all_to_all(acts, RING, 0, 0, tiled=True)

    left, right = shift(block, 1), shift(block, -1)
    moved = (block, left, right, shift(left[:192], 1), shift(right[192:], -1))

    sums = jax.ShapeDtypeStruct((4, 3, 32, 896), F32)
    mine, theirs = call(
        sums_kernel, [sums, sums], (place, acts, kept, *moved), [pltpu.VMEM((2, 256, 1024), BF16)],
        6 * 256 * 1024 * 896, 8000000,
    )
    parts = lax.all_to_all((mine + exchange(theirs)).astype(BF16), "yh", 0, 0, tiled=True)
    gate_value, hidden_grad, up_value = (jnp.sum(parts[:, k].astype(F32), axis=0) for k in range(3))
    sig = jax.nn.sigmoid(gate_value)
    silu = gate_value * sig
    hidden = (silu * up_value).astype(BF16)
    gate_grad = (hidden_grad * up_value * sig * (1.0 + gate_value * (1.0 - sig))).astype(BF16)
    up_grad = (hidden_grad * silu).astype(BF16)
    rows = jnp.stack([hidden, gate_grad, up_grad])
    rows = lax.all_to_all(jnp.broadcast_to(rows[None], (4, 3, 32, 896)), "yh", 0, 0, tiled=True)
    (terms,) = call(
        output_kernel, [jax.ShapeDtypeStruct((16, 2, 128, 128), BF16)], (place, rows, exchange(rows), kept, *moved),
        [], 6 * 256 * 1024 * 896, 8000000,
    )
    terms = lax.all_to_all(terms, RING, 0, 0, tiled=True)
    both = turn(jnp.sum(terms.astype(F32), axis=0).astype(BF16))
    return both[0], both[1]


def solution(mesh):
    fine = Mesh(mesh.devices.reshape(SIZES), AXES)
    acts = P(("zh", "x"), ("yh", "yl", "zl", "core"))
    weights = P(("yh", "yl", "zh", "x"), ("zl", "core"))
    return jax.shard_map(
        on_device,
        mesh=fine,
        in_specs=(acts, weights, weights, weights, acts),
        out_specs=(acts, acts),
        check_vma=False,
    )
```

time: 227 us -> 214 us (0.943)
  the two profiles are of different devices: /device:TPU:152 before, /device:TPU:1 now
where the time goes in v6:
time: 214 us
  blocking collectives  71.1 us (33%)
  starting transfers between devices  60.6 us (28%)
  waiting for transfers between devices  51.9 us (24%)
  between operations  14.3 us (7%)
  local copies, waits for them, and re-layouts  8.17 us (4%)
  Pallas kernels  7.04 us (3%)
    all_to_all x1, blocking collectives, on_device(): terms = lax.all_to_all(terms, RING, 0, 0, tiled=True)  33.2 us
    ppermute x4, waiting for transfers between devices, shift(): return lax.ppermute(values, 'x', [(i, (i + step) % 4) for i in range(4)])  22.1 us
    all_to_all x1, blocking collectives, on_device(): lax.all_to_all((mine + exchange(theirs)).astype(BF16), 'yh', 0, 0, tiled=...  20.9 us
    all_to_all x1, blocking collectives, on_device(): lax.all_to_all(jnp.broadcast_to(rows[None], (4, 3, 32, 896)), 'yh', 0, 0,...  17 us
    ppermute x2, starting transfers between devices, exchange(): return lax.ppermute(values, 'core', [(0, 1), (1, 0)])  16.4 us
    ppermute x1, waiting for transfers between devices, turn_across(): return lax.ppermute(values, ('yl', 'core', 'zh'), pairs)  14.8 us
    ppermute x3, starting transfers between devices, turn(): lax.ppermute(values, ('yl', 'core'), [(0, 0), (1, 2), (2, 1), (3, 3)])  13.2 us
    ppermute x4, starting transfers between devices, shift(): return lax.ppermute(values, 'x', [(i, (i + step) % 4) for i in range(4)])  11.6 us
  transfers between devices with their start and end apart: 12, of which 8 were waited for; matrix products, arithmetic and copies ran while one was open for 0% of the time, Pallas kernels for 1%

profile of v6, /device:TPU:1, one launch (start us, length us, event | category | flops | bytes accessed | tf_op | source)
XLA Modules:
  0.0 213.6 jit_solution(2817290429932771641)
XLA Ops:
  11.0 4.6 %collective-permute-start.2 = (bf16[384,896]{1,0:T(8,128)(2,1)S(1)}, bf16[384,896]{1,0:T(8,128)(2,1)S(1)}, u32[]{:S(2)}, u32[]{:S(2)}) collective-permute-start(bf16[384,896]{1,0:T(8,128)(2,1)S(1)} %get-tuple-element.9), channel_id=1, source_target_pairs={{0,0},{8,64},{64,8},{72,72},{1,1},{9,65},{65,9},{73,73},{2,2},{10,... | collective-permute-start | bytes 2064392 | tf_op jit(solution)/shard_map/ppermute | solution.py:41
  15.6 8.6 %collective-permute-done.2 = bf16[384,896]{1,0:T(8,128)(2,1)S(1)} collective-permute-done((bf16[384,896]{1,0:T(8,128)(2,1)S(1)}, bf16[384,896]{1,0:T(8,128)(2,1)S(1)}, u32[]{:S(2)}, u32[]{:S(2)}) %collective-permute-start.2) | collective-permute-done | bytes 688160 | tf_op jit(solution)/shard_map/ppermute | solution.py:41
  25.1 3.6 %collective-permute-start = (bf16[2,128,128]{2,1,0:T(8,128)(2,1)S(1)}, bf16[2,128,128]{2,1,0:T(8,128)(2,1)S(1)}, u32[]{:S(2)}, u32[]{:S(2)}) collective-permute-start(bf16[2,128,128]{2,1,0:T(8,128)(2,1)S(1)} %pad_maximum_fusion.1), channel_id=1, source_target_pairs={{0,0},{8,64},{64,8},{72,72},{1,1},{9,65},{65,9},{73,73},{2,2},{10,... | collective-permute-start | bytes 196616 | tf_op jit(solution)/shard_map/ppermute | solution.py:41
  28.8 10.7 %collective-permute-start.1 = (bf16[384,896]{1,0:T(8,128)(2,1)S(1)}, bf16[384,896]{1,0:T(8,128)(2,1)S(1)}, u32[]{:S(2)}, u32[]{:S(2)}) collective-permute-start(bf16[384,896]{1,0:T(8,128)(2,1)S(1)} %get-tuple-element.7), channel_id=1, source_target_pairs={{0,4},{4,0},{8,68},{12,64},{64,12},{68,8},{72,76},{76,72},{1,5},{5... | collective-permute-start | bytes 2064392 | tf_op jit(solution)/shard_map/ppermute | solution.py:46
  41.1 14.8 %collective-permute-done.1.refs_0_ = bf16[384,896]{1,0:T(8,128)(2,1)S(1)} collective-permute-done((bf16[384,896]{1,0:T(8,128)(2,1)S(1)}, bf16[384,896]{1,0:T(8,128)(2,1)S(1)}, u32[]{:S(2)}, u32[]{:S(2)}) %collective-permute-start.1) | collective-permute-done | bytes 688160 | tf_op jit(solution)/shard_map/ppermute | solution.py:46
  55.9 8.6 %all-to-all-start = ((bf16[16,2,128,128]{3,2,1,0:T(8,128)(2,1)}), bf16[16,2,128,128]{3,2,1,0:T(8,128)(2,1)S(1)}, u32[]{:S(2)}, u32[]{:S(2)}) async-start(bf16[16,2,128,128]{3,2,1,0:T(8,128)(2,1)} %shard_map.68), calls=%async_computation | async-start | bytes 2097152 | tf_op jit(solution)/shard_map/all_to_all | solution.py:136
  64.5 4.4 %collective-permute-start.4 = (bf16[384,896]{1,0:T(8,128)(2,1)S(1)}, bf16[384,896]{1,0:T(8,128)(2,1)S(1)}, u32[]{:S(2)}, u32[]{:S(2)}) collective-permute-start(bf16[384,896]{1,0:T(8,128)(2,1)S(1)} %collective-permute-done.1.refs_0_), channel_id=1, source_target_pairs={{0,3},{1,0},{2,1},{3,2},{4,7},{5,4},{6,5},{7,6},{8,11},{9,8},{10,9... | collective-permute-start | bytes 2064392 | tf_op jit(solution)/shard_map/ppermute | solution.py:33
  68.9 1.9 collective-permute-start.3
  70.8 13.8 %collective-permute-done.4.refs_2_ = bf16[384,896]{1,0:T(8,128)(2,1)S(1)} collective-permute-done((bf16[384,896]{1,0:T(8,128)(2,1)S(1)}, bf16[384,896]{1,0:T(8,128)(2,1)S(1)}, u32[]{:S(2)}, u32[]{:S(2)}) %collective-permute-start.4) | collective-permute-done | bytes 688160 | tf_op jit(solution)/shard_map/ppermute | solution.py:33
  84.7 3.2 %collective-permute-start.6 = (bf16[192,896]{1,0:T(8,128)(2,1)S(1)}, bf16[192,896]{1,0:T(8,128)(2,1)S(1)}, u32[]{:S(2)}, u32[]{:S(2)}) collective-permute-start(bf16[192,896]{1,0:T(8,128)(2,1)S(1)} %slice.29), channel_id=1, source_target_pairs={{0,3},{1,0},{2,1},{3,2},{4,7},{5,4},{6,5},{7,6},{8,11},{9,8},{10,9... | collective-permute-start | bytes 1032200 | tf_op jit(solution)/shard_map/ppermute | solution.py:33
  87.9 2.1 collective-permute-start.5
  90.0 5.4 %collective-permute-done.6.refs_4_ = bf16[192,896]{1,0:T(8,128)(2,1)S(1)} collective-permute-done((bf16[192,896]{1,0:T(8,128)(2,1)S(1)}, bf16[192,896]{1,0:T(8,128)(2,1)S(1)}, u32[]{:S(2)}, u32[]{:S(2)}) %collective-permute-start.6) | collective-permute-done | bytes 344096 | tf_op jit(solution)/shard_map/ppermute | solution.py:33
  95.4 2.8 %collective-permute-done.5.refs_3_ = bf16[192,896]{1,0:T(8,128)(2,1)S(1)} collective-permute-done((bf16[192,896]{1,0:T(8,128)(2,1)S(1)}, bf16[192,896]{1,0:T(8,128)(2,1)S(1)}, u32[]{:S(2)}, u32[]{:S(2)}) %collective-permute-start.5) | collective-permute-done | bytes 344096 | tf_op jit(solution)/shard_map/ppermute | solution.py:33
  99.0 1.8 copy-done
  101.8 2.4 %shard_map.70 = (f32[4,3,32,896]{3,2,1,0:T(8,128)S(1)}, f32[4,3,32,896]{3,2,1,0:T(8,128)S(1)}) custom-call(s32[3]{0:T(128)S(1)} %pad_add_fusion.place, bf16[16,2,128,128]{3,2,1,0:T(8,128)(2,1)S(1)} %all-to-all-done.acts, bf16[4,384,896]{2,1,0:T(8,128)(2,1)S(1)} %bitcast.48, bf16[384,896]{1,0:T(8,128)(2,1)S(1)} %collective-permute-done.1.refs_0_, ...), custom_call_target="tpu_custom_call" | custom-call | flops 1409286144 | bytes 8000000 | tf_op jit(solution)/shard_map/pallas_call | solution.py:21
  104.1 5.1 %collective-permute-start.7 = (f32[4,3,32,896]{3,2,1,0:T(8,128)S(1)}, f32[4,3,32,896]{3,2,1,0:T(8,128)S(1)}, u32[]{:S(2)}, u32[]{:S(2)}) collective-permute-start(f32[4,3,32,896]{3,2,1,0:T(8,128)S(1)} %get-tuple-element.11), channel_id=1, source_target_pairs={{0,8},{8,0},{1,9},{9,1},{2,10},{10,2},{3,11},{11,3},{4,12},{12,4},... | collective-permute-start | bytes 4128776 | tf_op jit(solution)/shard_map/ppermute | solution.py:37
  109.3 2.7 %collective-permute-done.7 = f32[4,3,32,896]{3,2,1,0:T(8,128)S(1)} collective-permute-done((f32[4,3,32,896]{3,2,1,0:T(8,128)S(1)}, f32[4,3,32,896]{3,2,1,0:T(8,128)S(1)}, u32[]{:S(2)}, u32[]{:S(2)}) %collective-permute-start.7) | collective-permute-done | bytes 1376288 | tf_op jit(solution)/shard_map/ppermute | solution.py:37
  112.2 20.9 %all_to_all.20 = bf16[4,3,32,896]{3,2,1,0:T(8,128)(2,1)S(1)} all-to-all(bf16[4,3,32,896]{3,2,1,0:T(8,128)(2,1)S(1)} %add_convert_fusion), channel_id=1, replica_groups=mesh['yh'=4,'yl'=2,'zl'=4,'core'=2,'zh'=2,'x'=4] {'yh'}, dimensions={0} | all-to-all | bytes 1376256 | tf_op jit(solution)/shard_map/all_to_all | solution.py:146
  133.4 17.0 %all_to_all.21.near = bf16[4,3,32,896]{3,2,1,0:T(8,128)(2,1)S(1)} all-to-all(bf16[4,3,32,896]{3,2,1,0:T(8,128)(2,1)S(1)} %broadcast_in_dim.2), channel_id=1, replica_groups=mesh['yh'=4,'yl'=2,'zl'=4,'core'=2,'zh'=2,'x'=4] {'yh'}, dimensions={0} | all-to-all | bytes 1376256 | tf_op jit(solution)/shard_map/all_to_all | solution.py:154
  150.3 11.3 %collective-permute-start.8 = (bf16[4,3,32,896]{3,2,1,0:T(8,128)(2,1)S(1)}, bf16[4,3,32,896]{3,2,1,0:T(8,128)(2,1)S(1)}, u32[]{:S(2)}, u32[]{:S(2)}) collective-permute-start(bf16[4,3,32,896]{3,2,1,0:T(8,128)(2,1)S(1)} %all_to_all.21.near), channel_id=1, source_target_pairs={{0,8},{8,0},{1,9},{9,1},{2,10},{10,2},{3,11},{11,3},{4,12},{12,4},... | collective-permute-start | bytes 2064392 | tf_op jit(solution)/shard_map/ppermute | solution.py:37
  163.4 2.4 %shard_map.71 = bf16[16,2,128,128]{3,2,1,0:T(8,128)(2,1)S(1)} custom-call(s32[3]{0:T(128)S(1)} %pad_add_fusion.place, bf16[4,3,32,896]{3,2,1,0:T(8,128)(2,1)S(1)} %all_to_all.21.near, bf16[4,3,32,896]{3,2,1,0:T(8,128)(2,1)S(1)} %collective-permute-done.8.other, bf16[4,384,896]{2,1,0:T(8,128)(2,1)S(1)} %bitcast.49, ...), custom_call_target="tpu_custom_call" | custom-call | flops 1409286144 | bytes 8000000 | tf_op jit(solution)/shard_map/pallas_call | solution.py:21
  165.8 33.2 %all_to_all.22 = bf16[16,2,128,128]{3,2,1,0:T(8,128)(2,1)S(1)} all-to-all(bf16[16,2,128,128]{3,2,1,0:T(8,128)(2,1)S(1)} %shard_map.71), channel_id=1, replica_groups=mesh['yh'=4,'yl'=2,'zl'=4,'core'=2,'zh'=2,'x'=4] {'yl','zl','zh'}, dimensions={0} | all-to-all | bytes 2097152 | tf_op jit(solution)/shard_map/all_to_all | solution.py:159
  199.1 5.0 %collective-permute-start.9 = (bf16[2,128,128]{2,1,0:T(8,128)(2,1)S(1)}, bf16[2,128,128]{2,1,0:T(8,128)(2,1)S(1)}, u32[]{:S(2)}, u32[]{:S(2)}) collective-permute-start(bf16[2,128,128]{2,1,0:T(8,128)(2,1)S(1)} %reduce_sum.51), channel_id=1, source_target_pairs={{0,0},{8,64},{64,8},{72,72},{1,1},{9,65},{65,9},{73,73},{2,2},{10,... | collective-permute-start | bytes 196616 | tf_op jit(solution)/shard_map/ppermute | solution.py:41
  204.2 1.9 collective-permute-done.9
  (41 shorter events, 11.1 us)
Async XLA Ops:
  7.2 91.8 %all-gather.3.cloned.1.call-start = ((), (), s32[]{:S(2)}) async-start(), calls=%async_computation.4 | async-start | bytes 3440640 | tf_op jit(solution)/shard_map/all_gather | solution.py:129
  7.3 1.0 copy-start.5
  8.3 1.0 copy-start.6
  9.3 1.0 copy-start.7
  10.3 14.8 %copy-start.9 = (bf16[128,128]{1,0:T(8,128)(2,1)S(1)}, bf16[128,128]{1,0:T(8,128)(2,1)}, u32[]{:S(2)}) copy-start(bf16[128,128]{1,0:T(8,128)(2,1)} %param.9) | copy-start | bytes 98308
  10.4 14.8 %copy-start.10 = (bf16[128,128]{1,0:T(8,128)(2,1)S(1)}, bf16[128,128]{1,0:T(8,128)(2,1)}, u32[]{:S(2)}) copy-start(bf16[128,128]{1,0:T(8,128)(2,1)} %param.5) | copy-start | bytes 98308
  11.0 13.2 %collective-permute-start.2 = (bf16[384,896]{1,0:T(8,128)(2,1)S(1)}, bf16[384,896]{1,0:T(8,128)(2,1)S(1)}, u32[]{:S(2)}, u32[]{:S(2)}) collective-permute-start(bf16[384,896]{1,0:T(8,128)(2,1)S(1)} %get-tuple-element.9), channel_id=1, source_target_pairs={{0,0},{8,64},{64,8},{72,72},{1,1},{9,65},{65,9},{73,73},{2,2},{10,... | collective-permute-start | bytes 2064392 | tf_op jit(solution)/shard_map/ppermute | solution.py:41
  24.2 0.9 copy-start.8
  25.1 14.3 %collective-permute-start = (bf16[2,128,128]{2,1,0:T(8,128)(2,1)S(1)}, bf16[2,128,128]{2,1,0:T(8,128)(2,1)S(1)}, u32[]{:S(2)}, u32[]{:S(2)}) collective-permute-start(bf16[2,128,128]{2,1,0:T(8,128)(2,1)S(1)} %pad_maximum_fusion.1), channel_id=1, source_target_pairs={{0,0},{8,64},{64,8},{72,72},{1,1},{9,65},{65,9},{73,73},{2,2},{10,... | collective-permute-start | bytes 196616 | tf_op jit(solution)/shard_map/ppermute | solution.py:41
  28.8 27.1 %collective-permute-start.1 = (bf16[384,896]{1,0:T(8,128)(2,1)S(1)}, bf16[384,896]{1,0:T(8,128)(2,1)S(1)}, u32[]{:S(2)}, u32[]{:S(2)}) collective-permute-start(bf16[384,896]{1,0:T(8,128)(2,1)S(1)} %get-tuple-element.7), channel_id=1, source_target_pairs={{0,4},{4,0},{8,68},{12,64},{64,12},{68,8},{72,76},{76,72},{1,5},{5... | collective-permute-start | bytes 2064392 | tf_op jit(solution)/shard_map/ppermute | solution.py:46
  55.9 43.1 %all-to-all-start = ((bf16[16,2,128,128]{3,2,1,0:T(8,128)(2,1)}), bf16[16,2,128,128]{3,2,1,0:T(8,128)(2,1)S(1)}, u32[]{:S(2)}, u32[]{:S(2)}) async-start(bf16[16,2,128,128]{3,2,1,0:T(8,128)(2,1)} %shard_map.68), calls=%async_computation | async-start | bytes 2097152 | tf_op jit(solution)/shard_map/all_to_all | solution.py:136
  64.5 20.2 %collective-permute-start.4 = (bf16[384,896]{1,0:T(8,128)(2,1)S(1)}, bf16[384,896]{1,0:T(8,128)(2,1)S(1)}, u32[]{:S(2)}, u32[]{:S(2)}) collective-permute-start(bf16[384,896]{1,0:T(8,128)(2,1)S(1)} %collective-permute-done.1.refs_0_), channel_id=1, source_target_pairs={{0,3},{1,0},{2,1},{3,2},{4,7},{5,4},{6,5},{7,6},{8,11},{9,8},{10,9... | collective-permute-start | bytes 2064392 | tf_op jit(solution)/shard_map/ppermute | solution.py:33
  68.9 19.0 %collective-permute-start.3 = (bf16[384,896]{1,0:T(8,128)(2,1)S(1)}, bf16[384,896]{1,0:T(8,128)(2,1)S(1)}, u32[]{:S(2)}, u32[]{:S(2)}) collective-permute-start(bf16[384,896]{1,0:T(8,128)(2,1)S(1)} %collective-permute-done.1.refs_0_), channel_id=1, source_target_pairs={{0,1},{1,2},{2,3},{3,0},{4,5},{5,6},{6,7},{7,4},{8,9},{9,10},{10,1... | collective-permute-start | bytes 2064392 | tf_op jit(solution)/shard_map/ppermute | solution.py:33
  84.7 10.7 %collective-permute-start.6 = (bf16[192,896]{1,0:T(8,128)(2,1)S(1)}, bf16[192,896]{1,0:T(8,128)(2,1)S(1)}, u32[]{:S(2)}, u32[]{:S(2)}) collective-permute-start(bf16[192,896]{1,0:T(8,128)(2,1)S(1)} %slice.29), channel_id=1, source_target_pairs={{0,3},{1,0},{2,1},{3,2},{4,7},{5,4},{6,5},{7,6},{8,11},{9,8},{10,9... | collective-permute-start | bytes 1032200 | tf_op jit(solution)/shard_map/ppermute | solution.py:33
  87.9 10.4 %collective-permute-start.5 = (bf16[192,896]{1,0:T(8,128)(2,1)S(1)}, bf16[192,896]{1,0:T(8,128)(2,1)S(1)}, u32[]{:S(2)}, u32[]{:S(2)}) collective-permute-start(bf16[192,896]{1,0:T(8,128)(2,1)S(1)} %slice.28), channel_id=1, source_target_pairs={{0,1},{1,2},{2,3},{3,0},{4,5},{5,6},{6,7},{7,4},{8,9},{9,10},{10,1... | collective-permute-start | bytes 1032200 | tf_op jit(solution)/shard_map/ppermute | solution.py:33
  98.3 0.7 copy-start.2
  99.0 1.8 copy-start
  100.8 1.0 copy-start.3
  104.1 7.9 %collective-permute-start.7 = (f32[4,3,32,896]{3,2,1,0:T(8,128)S(1)}, f32[4,3,32,896]{3,2,1,0:T(8,128)S(1)}, u32[]{:S(2)}, u32[]{:S(2)}) collective-permute-start(f32[4,3,32,896]{3,2,1,0:T(8,128)S(1)} %get-tuple-element.11), channel_id=1, source_target_pairs={{0,8},{8,0},{1,9},{9,1},{2,10},{10,2},{3,11},{11,3},{4,12},{12,4},... | collective-permute-start | bytes 4128776 | tf_op jit(solution)/shard_map/ppermute | solution.py:37
  133.2 30.2 %copy-start.1 = (bf16[1536,896]{1,0:T(8,128)(2,1)S(1)}, bf16[1536,896]{1,0:T(8,128)(2,1)}, u32[]{:S(2)}) copy-start(bf16[1536,896]{1,0:T(8,128)(2,1)} %all-gather.3.cloned.1.call-done) | copy-start | bytes 8257540
  133.3 30.1 %copy-start.4 = (bf16[192,896]{1,0:T(8,128)(2,1)S(1)}, bf16[192,896]{1,0:T(8,128)(2,1)}, u32[]{:S(2)}) copy-start(bf16[192,896]{1,0:T(8,128)(2,1)} %copy-done.2) | copy-start | bytes 1032196
  150.3 13.1 %collective-permute-start.8 = (bf16[4,3,32,896]{3,2,1,0:T(8,128)(2,1)S(1)}, bf16[4,3,32,896]{3,2,1,0:T(8,128)(2,1)S(1)}, u32[]{:S(2)}, u32[]{:S(2)}) collective-permute-start(bf16[4,3,32,896]{3,2,1,0:T(8,128)(2,1)S(1)} %all_to_all.21.near), channel_id=1, source_target_pairs={{0,8},{8,0},{1,9},{9,1},{2,10},{10,2},{3,11},{11,3},{4,12},{12,4},... | collective-permute-start | bytes 2064392 | tf_op jit(solution)/shard_map/ppermute | solution.py:37
  199.1 7.0 %collective-permute-start.9 = (bf16[2,128,128]{2,1,0:T(8,128)(2,1)S(1)}, bf16[2,128,128]{2,1,0:T(8,128)(2,1)S(1)}, u32[]{:S(2)}, u32[]{:S(2)}) collective-permute-start(bf16[2,128,128]{2,1,0:T(8,128)(2,1)S(1)} %reduce_sum.51), channel_id=1, source_target_pairs={{0,0},{8,64},{64,8},{72,72},{1,1},{9,65},{65,9},{73,73},{2,2},{10,... | collective-permute-start | bytes 196616 | tf_op jit(solution)/shard_map/ppermute | solution.py:41
Sparse Core Ops, SparseCore 0:
  25.2 45.9 all-gather.2

commit v7 on v5

v7 whole, which is shorter than its diff:
```python
import jax
import jax.numpy as jnp
from jax import lax
from jax.experimental import pallas as pl
from jax.experimental.pallas import tpu as pltpu
from jax.sharding import Mesh, PartitionSpec as P

AXES = ("y", "zl", "core", "zh", "x")
SIZES = (8, 4, 2, 2, 4)
RING = ("zh", "zl")
NT = (((1,), (1,)), ((), ()))
F32, BF16 = jnp.float32, jnp.bfloat16
STEPS = (0, 3, 1, 2)
GATE, DOWN, UP = 0, 1, 2
WHICH = (0, 1, 0)
SMEM = pl.BlockSpec(memory_space=pltpu.SMEM)
VMEM = pl.BlockSpec(memory_space=pltpu.VMEM)


def call(kernel, outs, operands, scratch, flops, moved):
    return pl.pallas_call(
        kernel,
        out_shape=outs,
        in_specs=[SMEM] + [VMEM] * (len(operands) - 1),
        out_specs=[VMEM] * len(outs),
        scratch_shapes=scratch,
        cost_estimate=pl.CostEstimate(flops=flops, bytes_accessed=moved, transcendentals=0),
        compiler_params=pltpu.CompilerParams(vmem_limit_bytes=12 << 20),
    )(*operands)


def shift(values, step):
    return lax.ppermute(values, "x", [(i, (i + step) % 4) for i in range(4)])


def exchange(values, axis):
    return lax.ppermute(values, axis, [(0, 1), (1, 0)])


def split_kernel(place, gate, down, up, keep, send):
    low = place[1] == 0
    for k, weight in enumerate((gate, down, up)):
        left, right = weight[:, :896], weight[:, 896:]
        rows = pl.ds(128 * k, 128)
        keep[rows] = jnp.where(low, left, right)
        send[rows] = jnp.where(low, right, left)


def table_kernel(place, out):
    for other_zh in (0, 1):
        for slot in range(4):
            zh = 1 - place[1] if other_zh else place[1]
            out[4 * other_zh + slot] = 4 * zh + (place[0] + STEPS[slot]) % 4
    out[8] = place[2]


def own_kernel(place, keep, block, out):
    for k in range(3):
        out[0, k] = keep[128 * k : 128 * k + 128]
        out[1, k] = block[128 * k : 128 * k + 128]


def spread_kernel(place, tokens, grad, out):
    for i in range(8):
        out[i, 0] = tokens[...]
        out[i, 1] = grad[...]


def rows_of(k, other_zh, pair, own, kept, moved):
    came, rows = (moved if other_zh else kept), slice(128 * k, 128 * k + 128)
    if pair:
        return jnp.concatenate([came[1][rows], came[2][rows]], axis=0)
    return jnp.concatenate([own[other_zh, k], came[0][rows]], axis=0)


def sums_kernel(table, near, other, own, *refs):
    kept, moved, out, wide = refs[:3], refs[3:6], refs[6], refs[7]
    for other_zh in (0, 1):
        for slot in range(4):
            f = table[4 * other_zh + slot]
            same = f % 2 == table[8]
            for t in (0, 1):
                for which in (0, 1):
                    tile = jnp.where(same, near[4 * t + f // 2, which], other[4 * t + f // 2, which])
                    wide[which, pl.ds(128 * t, 128), pl.ds(512 * other_zh + 128 * slot, 128)] = tile
    for k in range(3):
        total = None
        for other_zh in (0, 1):
            for pair in (0, 1):
                rows = rows_of(k, other_zh, pair, own, kept, moved)
                cols = pl.ds(512 * other_zh + 256 * pair, 256)
                term = jnp.dot(wide[WHICH[k], :, cols], rows, preferred_element_type=F32)
                total = term if total is None else total + term
        out[:, k] = total.astype(BF16).reshape(8, 32, 896)


def output_kernel(table, acts, own, *refs):
    kept, moved, mine, theirs, held = refs[:3], refs[3:6], refs[6], refs[7], refs[8]
    hidden, gate_grad, up_grad = (acts[:, k].reshape(256, 896) for k in range(3))

    def product(rows, block):
        return lax.dot_general(rows, block, NT, preferred_element_type=F32)

    for other_zh in (0, 1):
        for pair in (0, 1):
            gate, down, up = (rows_of(k, other_zh, pair, own, kept, moved) for k in range(3))
            mixed = product(hidden, down)
            grad = product(gate_grad, gate) + product(up_grad, up)
            for slot in (0, 1):
                f = table[4 * other_zh + 2 * pair + slot]
                side = (f + table[8]) % 2
                for t in (0, 1):
                    part = (slice(128 * t, 128 * t + 128), slice(128 * slot, 128 * slot + 128))
                    held[side, 4 * t + f // 2, 0] = mixed[part]
                    held[side, 4 * t + f // 2, 1] = grad[part]
    mine[...] = held[0]
    theirs[...] = held[1]


def on_device(tokens, gate_weight, up_weight, down_weight, grad_mixed):
    place = jnp.stack([lax.axis_index("x"), lax.axis_index("zh"), lax.axis_index("core")])
    half = jax.ShapeDtypeStruct((384, 896), BF16)
    keep, send = call(split_kernel, [half, half], (place, gate_weight, down_weight, up_weight), [], 0, 3000000)
    block = exchange(send, "zh")
    kept = (shift(keep, 1), shift(keep, -1), shift(keep, 2))
    (own,) = call(
        own_kernel, [jax.ShapeDtypeStruct((2, 3, 128, 896), BF16)], (place, keep, block), [], 30000000000, 2800000
    )
    block, own, kept, tokens = lax.optimization_barrier((block, own, kept, tokens))
    weights = (own, *kept, shift(block, 1), shift(block, -1), shift(block, 2))
    (acts,) = call(
        spread_kernel, [jax.ShapeDtypeStruct((8, 2, 128, 128), BF16)], (place, tokens, grad_mixed), [], 30000000000, 1000000
    )
    table = pl.pallas_call(
        table_kernel,
        out_shape=jax.ShapeDtypeStruct((9,), jnp.int32),
        in_specs=[SMEM],
        out_specs=SMEM,
        cost_estimate=pl.CostEstimate(flops=30000000000, bytes_accessed=64, transcendentals=0),
    )(place)
    near, table = lax.optimization_barrier((lax.all_to_all(acts, RING, 0, 0, tiled=True), table))

    (parts,) = call(
        sums_kernel, [jax.ShapeDtypeStruct((8, 3, 32, 896), BF16)],
        (table, near, exchange(near, "core"), *weights), [pltpu.VMEM((2, 256, 1024), BF16)],
        6 * 256 * 1024 * 896, 8000000,
    )
    parts = lax.all_to_all(parts, "y", 0, 0, tiled=True)
    gate_value, hidden_grad, up_value = (jnp.sum(parts[:, k].astype(F32), axis=0) for k in range(3))
    sig = jax.nn.sigmoid(gate_value)
    silu = gate_value * sig
    hidden = (silu * up_value).astype(BF16)
    gate_grad = (hidden_grad * up_value * sig * (1.0 + gate_value * (1.0 - sig))).astype(BF16)
    up_grad = (hidden_grad * silu).astype(BF16)
    rows = jnp.stack([hidden, gate_grad, up_grad])
    rows = lax.all_to_all(jnp.broadcast_to(rows[None], (8, 3, 32, 896)), "y", 0, 0, tiled=True)
    terms = jax.ShapeDtypeStruct((8, 2, 128, 128), F32)
    mine, theirs = call(
        output_kernel, [terms, terms], (table, rows, *weights), [pltpu.VMEM((2, 8, 2, 128, 128), F32)],
        6 * 256 * 1024 * 896, 8000000,
    )
    terms = (mine + exchange(theirs, "core")).astype(BF16)
    terms = lax.all_to_all(terms, RING, 0, 0, tiled=True)
    both = jnp.sum(terms.astype(F32), axis=0).astype(BF16)
    return both[0], both[1]


def solution(mesh):
    fine = Mesh(mesh.devices.reshape(SIZES), AXES)
    acts = P(("zh", "x"), ("y", "zl", "core"))
    weights = P(("y", "zh", "x"), ("zl", "core"))
    return jax.shard_map(
        on_device,
        mesh=fine,
        in_specs=(acts, weights, weights, weights, acts),
        out_specs=(acts, acts),
        check_vma=False,
    )
```

time: 227 us -> 205 us (0.903)
  the two profiles are of different devices: /device:TPU:152 before, /device:TPU:1 now
where the time goes in v7:
time: 205 us; the launch traced here: 204 us
  blocking collectives  98.5 us (48%)
  starting transfers between devices  44.7 us (22%)
  waiting for transfers between devices  43.2 us (21%)
  Pallas kernels  10.6 us (5%)
  local copies, waits for them, and re-layouts  5.24 us (3%)
    all_to_all x1, blocking collectives, on_device(): parts = lax.all_to_all(parts, 'y', 0, 0, tiled=True)  41.9 us
    all_to_all x1, blocking collectives, on_device(): lax.all_to_all(jnp.broadcast_to(rows[None], (8, 3, 32, 896)), 'y', 0, 0,...  36.3 us
    ppermute x3, starting transfers between devices, exchange(): return lax.ppermute(values, axis, [(0, 1), (1, 0)])  20.5 us
    all_to_all x1, blocking collectives, on_device(): terms = lax.all_to_all(terms, RING, 0, 0, tiled=True)  20.4 us
    ppermute x6, waiting for transfers between devices, shift(): return lax.ppermute(values, 'x', [(i, (i + step) % 4) for i in range(4)])  20 us
    ppermute x6, starting transfers between devices, shift(): return lax.ppermute(values, 'x', [(i, (i + step) % 4) for i in range(4)])  19.9 us
    all_to_all x1, waiting for transfers between devices, on_device(): lax.all_to_all(acts, RING, 0, 0, tiled=True)  14.9 us
    pallas_call x5, Pallas kernels, call(): pl.pallas_call(kernel, out_shape=outs, in_specs=[SMEM] + [VMEM] * (len(op...  9.44 us
  transfers between devices with their start and end apart: 10, of which 7 were waited for; matrix products, arithmetic and copies ran while one was open for 0% of the time, Pallas kernels for 1%

profile of v7, /device:TPU:1, one launch (start us, length us, event | category | flops | bytes accessed | tf_op | source)
XLA Modules:
  0.0 203.7 jit_solution(7947153326481999427)
XLA Ops:
  0.7 1.0 copy-done.1
  4.4 11.5 %collective-permute-start = (bf16[384,896]{1,0:T(8,128)(2,1)S(1)}, bf16[384,896]{1,0:T(8,128)(2,1)}, u32[]{:S(2)}, u32[]{:S(2)}) collective-permute-start(bf16[384,896]{1,0:T(8,128)(2,1)S(1)} %get-tuple-element.14), channel_id=1, source_target_pairs={{0,4},{4,0},{1,5},{5,1},{2,6},{6,2},{3,7},{7,3},{8,12},{12,8},{9,1... | collective-permute-start | bytes 2064392 | tf_op jit(solution)/shard_map/ppermute | solution.py:37
  15.9 4.7 %collective-permute-start.3 = (bf16[384,896]{1,0:T(8,128)(2,1)S(1)}, bf16[384,896]{1,0:T(8,128)(2,1)S(1)}, u32[]{:S(2)}, u32[]{:S(2)}) collective-permute-start(bf16[384,896]{1,0:T(8,128)(2,1)S(1)} %get-tuple-element.15.keep), channel_id=1, source_target_pairs={{0,2},{1,3},{2,0},{3,1},{4,6},{5,7},{6,4},{7,5},{8,10},{9,11},{10,... | collective-permute-start | bytes 2064392 | tf_op jit(solution)/shard_map/ppermute | solution.py:33
  20.6 2.8 %collective-permute-start.2 = (bf16[384,896]{1,0:T(8,128)(2,1)S(1)}, bf16[384,896]{1,0:T(8,128)(2,1)S(1)}, u32[]{:S(2)}, u32[]{:S(2)}) collective-permute-start(bf16[384,896]{1,0:T(8,128)(2,1)S(1)} %get-tuple-element.15.keep), channel_id=1, source_target_pairs={{0,3},{1,0},{2,1},{3,2},{4,7},{5,4},{6,5},{7,6},{8,11},{9,8},{10,9... | collective-permute-start | bytes 2064392 | tf_op jit(solution)/shard_map/ppermute | solution.py:33
  23.4 2.5 %collective-permute-start.1 = (bf16[384,896]{1,0:T(8,128)(2,1)S(1)}, bf16[384,896]{1,0:T(8,128)(2,1)S(1)}, u32[]{:S(2)}, u32[]{:S(2)}) collective-permute-start(bf16[384,896]{1,0:T(8,128)(2,1)S(1)} %get-tuple-element.15.keep), channel_id=1, source_target_pairs={{0,1},{1,2},{2,3},{3,0},{4,5},{5,6},{6,7},{7,4},{8,9},{9,10},{10,1... | collective-permute-start | bytes 2064392 | tf_op jit(solution)/shard_map/ppermute | solution.py:33
  25.9 4.3 %collective-permute-done.block = bf16[384,896]{1,0:T(8,128)(2,1)} collective-permute-done((bf16[384,896]{1,0:T(8,128)(2,1)S(1)}, bf16[384,896]{1,0:T(8,128)(2,1)}, u32[]{:S(2)}, u32[]{:S(2)}) %collective-permute-start) | collective-permute-done | bytes 688160 | tf_op jit(solution)/shard_map/ppermute | solution.py:37
  30.2 1.2 shard_map.69.own
  31.4 3.9 %collective-permute-done.3.refs_2_ = bf16[384,896]{1,0:T(8,128)(2,1)S(1)} collective-permute-done((bf16[384,896]{1,0:T(8,128)(2,1)S(1)}, bf16[384,896]{1,0:T(8,128)(2,1)S(1)}, u32[]{:S(2)}, u32[]{:S(2)}) %collective-permute-start.3) | collective-permute-done | bytes 688160 | tf_op jit(solution)/shard_map/ppermute | solution.py:33
  35.4 15.1 %collective-permute-done.2.refs_1_ = bf16[384,896]{1,0:T(8,128)(2,1)S(1)} collective-permute-done((bf16[384,896]{1,0:T(8,128)(2,1)S(1)}, bf16[384,896]{1,0:T(8,128)(2,1)S(1)}, u32[]{:S(2)}, u32[]{:S(2)}) %collective-permute-start.2) | collective-permute-done | bytes 688160 | tf_op jit(solution)/shard_map/ppermute | solution.py:33
  51.4 4.6 %collective-permute-start.7 = (bf16[384,896]{1,0:T(8,128)(2,1)}, bf16[384,896]{1,0:T(8,128)(2,1)}, u32[]{:S(2)}, u32[]{:S(2)}) collective-permute-start(bf16[384,896]{1,0:T(8,128)(2,1)} %collective-permute-done.block), channel_id=1, source_target_pairs={{0,2},{1,3},{2,0},{3,1},{4,6},{5,7},{6,4},{7,5},{8,10},{9,11},{10,... | collective-permute-start | bytes 2064392 | tf_op jit(solution)/shard_map/ppermute | solution.py:33
  56.1 2.8 %collective-permute-start.6 = (bf16[384,896]{1,0:T(8,128)(2,1)}, bf16[384,896]{1,0:T(8,128)(2,1)}, u32[]{:S(2)}, u32[]{:S(2)}) collective-permute-start(bf16[384,896]{1,0:T(8,128)(2,1)} %collective-permute-done.block), channel_id=1, source_target_pairs={{0,3},{1,0},{2,1},{3,2},{4,7},{5,4},{6,5},{7,6},{8,11},{9,8},{10,9... | collective-permute-start | bytes 2064392 | tf_op jit(solution)/shard_map/ppermute | solution.py:33
  58.9 2.5 %collective-permute-start.5 = (bf16[384,896]{1,0:T(8,128)(2,1)}, bf16[384,896]{1,0:T(8,128)(2,1)}, u32[]{:S(2)}, u32[]{:S(2)}) collective-permute-start(bf16[384,896]{1,0:T(8,128)(2,1)} %collective-permute-done.block), channel_id=1, source_target_pairs={{0,1},{1,2},{2,3},{3,0},{4,5},{5,6},{6,7},{7,4},{8,9},{9,10},{10,1... | collective-permute-start | bytes 2064392 | tf_op jit(solution)/shard_map/ppermute | solution.py:33
  62.8 4.3 %all-to-all-start = ((bf16[8,2,128,128]{3,2,1,0:T(8,128)(2,1)}), bf16[8,2,128,128]{3,2,1,0:T(8,128)(2,1)}, u32[]{:S(2)}, u32[]{:S(2)}) async-start(bf16[8,2,128,128]{3,2,1,0:T(8,128)(2,1)} %copy-done), calls=%async_computation | async-start | bytes 1048576 | tf_op jit(solution)/shard_map/all_to_all | solution.py:141
  67.1 1.2 shard_map.71.table
  68.3 14.9 %all-to-all-done.near = bf16[8,2,128,128]{3,2,1,0:T(8,128)(2,1)} async-done(((bf16[8,2,128,128]{3,2,1,0:T(8,128)(2,1)}), bf16[8,2,128,128]{3,2,1,0:T(8,128)(2,1)}, u32[]{:S(2)}, u32[]{:S(2)}) %all-to-all-start) | async-done | bytes 524320 | tf_op jit(solution)/shard_map/all_to_all | solution.py:141
  83.2 4.3 %collective-permute-start.4 = (bf16[8,2,128,128]{3,2,1,0:T(8,128)(2,1)}, bf16[8,2,128,128]{3,2,1,0:T(8,128)(2,1)S(1)}, u32[]{:S(2)}, u32[]{:S(2)}) collective-permute-start(bf16[8,2,128,128]{3,2,1,0:T(8,128)(2,1)} %all-to-all-done.near), channel_id=1, source_target_pairs={{0,8},{8,0},{1,9},{9,1},{2,10},{10,2},{3,11},{11,3},{4,12},{12,4},... | collective-permute-start | bytes 1572872 | tf_op jit(solution)/shard_map/ppermute | solution.py:37
  87.6 1.7 collective-permute-done.4.other
  89.9 3.5 %shard_map.72 = bf16[8,3,32,896]{3,2,1,0:T(8,128)(2,1)S(1)} custom-call(s32[9]{0:T(128)S(1)} %copy-done.5, bf16[8,2,128,128]{3,2,1,0:T(8,128)(2,1)} %all-to-all-done.near, bf16[8,2,128,128]{3,2,1,0:T(8,128)(2,1)S(1)} %collective-permute-done.4.other, bf16[2,3,128,896]{3,2,1,0:T(8,128)(2,1)S(1)} %shard_map.69.own, ...), custom_call_target="tpu_custom_call" | custom-call | flops 1409286144 | bytes 8000000 | tf_op jit(solution)/shard_map/pallas_call | solution.py:21
  93.4 41.9 %all_to_all.20 = bf16[8,3,32,896]{3,2,1,0:T(8,128)(2,1)S(1)} all-to-all(bf16[8,3,32,896]{3,2,1,0:T(8,128)(2,1)S(1)} %shard_map.72), channel_id=1, replica_groups=mesh['y'=8,'zl'=4,'core'=2,'zh'=2,'x'=4] {'y'}, dimensions={0} | all-to-all | bytes 2752512 | tf_op jit(solution)/shard_map/all_to_all | solution.py:148
  135.8 36.3 %all_to_all.21.acts = bf16[8,3,32,896]{3,2,1,0:T(8,128)(2,1)S(1)} all-to-all(bf16[8,3,32,896]{3,2,1,0:T(8,128)(2,1)S(1)} %broadcast_in_dim.2), channel_id=1, replica_groups=mesh['y'=8,'zl'=4,'core'=2,'zh'=2,'x'=4] {'y'}, dimensions={0} | all-to-all | bytes 2752512 | tf_op jit(solution)/shard_map/all_to_all | solution.py:156
  172.0 3.5 %shard_map.73 = (f32[8,2,128,128]{3,2,1,0:T(8,128)S(1)}, f32[8,2,128,128]{3,2,1,0:T(8,128)S(1)}) custom-call(s32[9]{0:T(128)S(1)} %copy-done.6, bf16[8,3,32,896]{3,2,1,0:T(8,128)(2,1)S(1)} %all_to_all.21.acts, bf16[2,3,128,896]{3,2,1,0:T(8,128)(2,1)S(1)} %shard_map.69.own, bf16[384,896]{1,0:T(8,128)(2,1)S(1)} %collective-permute-done.1.refs_0_, ...), custom_call_target="tpu_custom_call" | custom-call | flops 1409286144 | bytes 8000000 | tf_op jit(solution)/shard_map/pallas_call | solution.py:21
  175.5 4.7 %collective-permute-start.8 = (f32[8,2,128,128]{3,2,1,0:T(8,128)S(1)}, f32[8,2,128,128]{3,2,1,0:T(8,128)S(1)}, u32[]{:S(2)}, u32[]{:S(2)}) collective-permute-start(f32[8,2,128,128]{3,2,1,0:T(8,128)S(1)} %get-tuple-element.25), channel_id=1, source_target_pairs={{0,8},{8,0},{1,9},{9,1},{2,10},{10,2},{3,11},{11,3},{4,12},{12,4},... | collective-permute-start | bytes 3145736 | tf_op jit(solution)/shard_map/ppermute | solution.py:37
  180.3 2.3 %collective-permute-done.8 = f32[8,2,128,128]{3,2,1,0:T(8,128)S(1)} collective-permute-done((f32[8,2,128,128]{3,2,1,0:T(8,128)S(1)}, f32[8,2,128,128]{3,2,1,0:T(8,128)S(1)}, u32[]{:S(2)}, u32[]{:S(2)}) %collective-permute-start.8) | collective-permute-done | bytes 1048608 | tf_op jit(solution)/shard_map/ppermute | solution.py:37
  182.7 20.4 %all_to_all.22 = bf16[8,2,128,128]{3,2,1,0:T(8,128)(2,1)S(1)} all-to-all(bf16[8,2,128,128]{3,2,1,0:T(8,128)(2,1)S(1)} %add_convert_fusion), channel_id=1, replica_groups=mesh['y'=8,'zl'=4,'core'=2,'zh'=2,'x'=4] {'zh','zl'}, dimensions={0} | all-to-all | bytes 1048576 | tf_op jit(solution)/shard_map/all_to_all | solution.py:163
  (31 shorter events, 7.0 us)
Async XLA Ops:
  0.7 1.0 copy-start.1
  1.7 1.0 copy-start.2
  2.8 1.0 copy-start.3
  3.8 57.6 %copy-start.4 = (s32[3]{0:T(128)}, s32[3]{0:T(128)S(1)}, u32[]{:S(2)}) copy-start(s32[3]{0:T(128)S(1)} %pad_add_fusion.place) | copy-start | bytes 40
  4.4 25.8 %collective-permute-start = (bf16[384,896]{1,0:T(8,128)(2,1)S(1)}, bf16[384,896]{1,0:T(8,128)(2,1)}, u32[]{:S(2)}, u32[]{:S(2)}) collective-permute-start(bf16[384,896]{1,0:T(8,128)(2,1)S(1)} %get-tuple-element.14), channel_id=1, source_target_pairs={{0,4},{4,0},{1,5},{5,1},{2,6},{6,2},{3,7},{7,3},{8,12},{12,8},{9,1... | collective-permute-start | bytes 2064392 | tf_op jit(solution)/shard_map/ppermute | solution.py:37
  15.9 45.5 %copy-start.7 = (bf16[128,128]{1,0:T(8,128)(2,1)S(1)}, bf16[128,128]{1,0:T(8,128)(2,1)}, u32[]{:S(2)}) copy-start(bf16[128,128]{1,0:T(8,128)(2,1)} %tokens) | copy-start | bytes 98308
  15.9 45.5 %copy-start.8 = (bf16[128,128]{1,0:T(8,128)(2,1)S(1)}, bf16[128,128]{1,0:T(8,128)(2,1)}, u32[]{:S(2)}) copy-start(bf16[128,128]{1,0:T(8,128)(2,1)} %grad.1) | copy-start | bytes 98308
  15.9 19.4 %collective-permute-start.3 = (bf16[384,896]{1,0:T(8,128)(2,1)S(1)}, bf16[384,896]{1,0:T(8,128)(2,1)S(1)}, u32[]{:S(2)}, u32[]{:S(2)}) collective-permute-start(bf16[384,896]{1,0:T(8,128)(2,1)S(1)} %get-tuple-element.15.keep), channel_id=1, source_target_pairs={{0,2},{1,3},{2,0},{3,1},{4,6},{5,7},{6,4},{7,5},{8,10},{9,11},{10,... | collective-permute-start | bytes 2064392 | tf_op jit(solution)/shard_map/ppermute | solution.py:33
  20.6 29.9 %collective-permute-start.2 = (bf16[384,896]{1,0:T(8,128)(2,1)S(1)}, bf16[384,896]{1,0:T(8,128)(2,1)S(1)}, u32[]{:S(2)}, u32[]{:S(2)}) collective-permute-start(bf16[384,896]{1,0:T(8,128)(2,1)S(1)} %get-tuple-element.15.keep), channel_id=1, source_target_pairs={{0,3},{1,0},{2,1},{3,2},{4,7},{5,4},{6,5},{7,6},{8,11},{9,8},{10,9... | collective-permute-start | bytes 2064392 | tf_op jit(solution)/shard_map/ppermute | solution.py:33
  23.4 28.1 %collective-permute-start.1 = (bf16[384,896]{1,0:T(8,128)(2,1)S(1)}, bf16[384,896]{1,0:T(8,128)(2,1)S(1)}, u32[]{:S(2)}, u32[]{:S(2)}) collective-permute-start(bf16[384,896]{1,0:T(8,128)(2,1)S(1)} %get-tuple-element.15.keep), channel_id=1, source_target_pairs={{0,1},{1,2},{2,3},{3,0},{4,5},{5,6},{6,7},{7,4},{8,9},{9,10},{10,1... | collective-permute-start | bytes 2064392 | tf_op jit(solution)/shard_map/ppermute | solution.py:33
  51.4 36.1 %collective-permute-start.7 = (bf16[384,896]{1,0:T(8,128)(2,1)}, bf16[384,896]{1,0:T(8,128)(2,1)}, u32[]{:S(2)}, u32[]{:S(2)}) collective-permute-start(bf16[384,896]{1,0:T(8,128)(2,1)} %collective-permute-done.block), channel_id=1, source_target_pairs={{0,2},{1,3},{2,0},{3,1},{4,6},{5,7},{6,4},{7,5},{8,10},{9,11},{10,... | collective-permute-start | bytes 2064392 | tf_op jit(solution)/shard_map/ppermute | solution.py:33
  56.1 31.5 %collective-permute-start.6 = (bf16[384,896]{1,0:T(8,128)(2,1)}, bf16[384,896]{1,0:T(8,128)(2,1)}, u32[]{:S(2)}, u32[]{:S(2)}) collective-permute-start(bf16[384,896]{1,0:T(8,128)(2,1)} %collective-permute-done.block), channel_id=1, source_target_pairs={{0,3},{1,0},{2,1},{3,2},{4,7},{5,4},{6,5},{7,6},{8,11},{9,8},{10,9... | collective-permute-start | bytes 2064392 | tf_op jit(solution)/shard_map/ppermute | solution.py:33
  58.9 28.7 %collective-permute-start.5 = (bf16[384,896]{1,0:T(8,128)(2,1)}, bf16[384,896]{1,0:T(8,128)(2,1)}, u32[]{:S(2)}, u32[]{:S(2)}) collective-permute-start(bf16[384,896]{1,0:T(8,128)(2,1)} %collective-permute-done.block), channel_id=1, source_target_pairs={{0,1},{1,2},{2,3},{3,0},{4,5},{5,6},{6,7},{7,4},{8,9},{9,10},{10,1... | collective-permute-start | bytes 2064392 | tf_op jit(solution)/shard_map/ppermute | solution.py:33
  62.0 0.8 copy-start
  62.8 20.4 %all-to-all-start = ((bf16[8,2,128,128]{3,2,1,0:T(8,128)(2,1)}), bf16[8,2,128,128]{3,2,1,0:T(8,128)(2,1)}, u32[]{:S(2)}, u32[]{:S(2)}) async-start(bf16[8,2,128,128]{3,2,1,0:T(8,128)(2,1)} %copy-done), calls=%async_computation | async-start | bytes 1048576 | tf_op jit(solution)/shard_map/all_to_all | solution.py:141
  83.2 6.1 %collective-permute-start.4 = (bf16[8,2,128,128]{3,2,1,0:T(8,128)(2,1)}, bf16[8,2,128,128]{3,2,1,0:T(8,128)(2,1)S(1)}, u32[]{:S(2)}, u32[]{:S(2)}) collective-permute-start(bf16[8,2,128,128]{3,2,1,0:T(8,128)(2,1)} %all-to-all-done.near), channel_id=1, source_target_pairs={{0,8},{8,0},{1,9},{9,1},{2,10},{10,2},{3,11},{11,3},{4,12},{12,4},... | collective-permute-start | bytes 1572872 | tf_op jit(solution)/shard_map/ppermute | solution.py:37
  89.3 0.7 copy-start.5
  135.7 36.3 %copy-start.6 = (s32[9]{0:T(128)S(1)}, s32[9]{0:T(128)}, u32[]{:S(2)}) copy-start(s32[9]{0:T(128)} %shard_map.71.table) | copy-start | bytes 112
  175.5 7.0 %collective-permute-start.8 = (f32[8,2,128,128]{3,2,1,0:T(8,128)S(1)}, f32[8,2,128,128]{3,2,1,0:T(8,128)S(1)}, u32[]{:S(2)}, u32[]{:S(2)}) collective-permute-start(f32[8,2,128,128]{3,2,1,0:T(8,128)S(1)} %get-tuple-element.25), channel_id=1, source_target_pairs={{0,8},{8,0},{1,9},{9,1},{2,10},{10,2},{3,11},{11,3},{4,12},{12,4},... | collective-permute-start | bytes 3145736 | tf_op jit(solution)/shard_map/ppermute | solution.py:37

commit v8 on v7

--- a/solution.py
+++ b/solution.py
@@ -54,10 +54,14 @@
     out[8] = place[2]
 
 
-def own_kernel(place, keep, block, out):
-    for k in range(3):
-        out[0, k] = keep[128 * k : 128 * k + 128]
-        out[1, k] = block[128 * k : 128 * k + 128]
+def pack_kernel(place, b0, b1, b2, b3, out):
+    for slot, block in enumerate((b0, b1, b2, b3)):
+        for k in range(3):
+            out[k, 128 * slot : 128 * slot + 128] = block[128 * k : 128 * k + 128]
+
+
+def hold_kernel(place, block, out):
+    out[...] = block[...]
 
 
 def spread_kernel(place, tokens, grad, out):
@@ -66,15 +70,7 @@
         out[i, 1] = grad[...]
 
 
-def rows_of(k, other_zh, pair, own, kept, moved):
-    came, rows = (moved if other_zh else kept), slice(128 * k, 128 * k + 128)
-    if pair:
-        return jnp.concatenate([came[1][rows], came[2][rows]], axis=0)
-    return jnp.concatenate([own[other_zh, k], came[0][rows]], axis=0)
-
-
-def sums_kernel(table, near, other, own, *refs):
-    kept, moved, out, wide = refs[:3], refs[3:6], refs[6], refs[7]
+def sums_kernel(table, near, other, kept, moved, out, wide):
     for other_zh in (0, 1):
         for slot in range(4):
             f = table[4 * other_zh + slot]
@@ -84,35 +80,27 @@
                     tile = jnp.where(same, near[4 * t + f // 2, which], other[4 * t + f // 2, which])
                     wide[which, pl.ds(128 * t, 128), pl.ds(512 * other_zh + 128 * slot, 128)] = tile
     for k in range(3):
-        total = None
-        for other_zh in (0, 1):
-            for pair in (0, 1):
-                rows = rows_of(k, other_zh, pair, own, kept, moved)
-                cols = pl.ds(512 * other_zh + 256 * pair, 256)
-                term = jnp.dot(wide[WHICH[k], :, cols], rows, preferred_element_type=F32)
-                total = term if total is None else total + term
+        total = jnp.dot(wide[WHICH[k], :, :512], kept[k], preferred_element_type=F32)
+        total = total + jnp.dot(wide[WHICH[k], :, 512:], moved[k], preferred_element_type=F32)
         out[:, k] = total.astype(BF16).reshape(8, 32, 896)
 
 
-def output_kernel(table, acts, own, *refs):
-    kept, moved, mine, theirs, held = refs[:3], refs[3:6], refs[6], refs[7], refs[8]
+def output_kernel(table, acts, kept, moved, mine, theirs, held):
     hidden, gate_grad, up_grad = (acts[:, k].reshape(256, 896) for k in range(3))
 
     def product(rows, block):
         return lax.dot_general(rows, block, NT, preferred_element_type=F32)
 
-    for other_zh in (0, 1):
-        for pair in (0, 1):
-            gate, down, up = (rows_of(k, other_zh, pair, own, kept, moved) for k in range(3))
-            mixed = product(hidden, down)
-            grad = product(gate_grad, gate) + product(up_grad, up)
-            for slot in (0, 1):
-                f = table[4 * other_zh + 2 * pair + slot]
-                side = (f + table[8]) % 2
-                for t in (0, 1):
-                    part = (slice(128 * t, 128 * t + 128), slice(128 * slot, 128 * slot + 128))
-                    held[side, 4 * t + f // 2, 0] = mixed[part]
-                    held[side, 4 * t + f // 2, 1] = grad[part]
+    for other_zh, rows in enumerate((kept, moved)):
+        mixed = product(hidden, rows[DOWN])
+        grad = product(gate_grad, rows[GATE]) + product(up_grad, rows[UP])
+        for slot in range(4):
+            f = table[4 * other_zh + slot]
+            side = (f + table[8]) % 2
+            for t in (0, 1):
+                part = (slice(128 * t, 128 * t + 128), slice(128 * slot, 128 * slot + 128))
+                held[side, 4 * t + f // 2, 0] = mixed[part]
+                held[side, 4 * t + f // 2, 1] = grad[part]
     mine[...] = held[0]
     theirs[...] = held[1]
 
@@ -123,11 +111,13 @@
     keep, send = call(split_kernel, [half, half], (place, gate_weight, down_weight, up_weight), [], 0, 3000000)
     block = exchange(send, "zh")
     kept = (shift(keep, 1), shift(keep, -1), shift(keep, 2))
-    (own,) = call(
-        own_kernel, [jax.ShapeDtypeStruct((2, 3, 128, 896), BF16)], (place, keep, block), [], 30000000000, 2800000
-    )
-    block, own, kept, tokens = lax.optimization_barrier((block, own, kept, tokens))
-    weights = (own, *kept, shift(block, 1), shift(block, -1), shift(block, 2))
+    packed = jax.ShapeDtypeStruct((3, 512, 896), BF16)
+    (first,) = call(pack_kernel, [packed], (place, keep, *kept), [], 0, 0)
+    (hold,) = call(hold_kernel, [half], (place, block), [], 30000000000, 1400000)
+    block, first, tokens = lax.optimization_barrier((hold, first, tokens))
+    moved = (block, shift(block, 1), shift(block, -1), shift(block, 2))
+    (second,) = call(pack_kernel, [packed], (place, *moved), [], 0, 0)
+    weights = (first, second)
     (acts,) = call(
         spread_kernel, [jax.ShapeDtypeStruct((8, 2, 128, 128), BF16)], (place, tokens, grad_mixed), [], 30000000000, 1000000
     )

time: 205 us -> 201 us (0.980)
  waiting for transfers between devices: 43.2 us -> 38.5 us
  blocking collectives: 98.5 us -> 94.9 us
  starting transfers between devices: 44.7 us -> 47.8 us
    ppermute x3, starting transfers between devices: 20.5 us -> 23.5 us  [exchange(): return lax.ppermute(values, axis, [(0, 1), (1, 0)])]
    all_to_all x1, waiting for transfers between devices: 14.9 us -> 12.9 us  [on_device(): lax.all_to_all(acts, RING, 0, 0, tiled=True)]
    pallas_call x5 -> x7, Pallas kernels: 9.44 us -> 10.3 us  [call(): pl.pallas_call(kernel, out_shape=outs, in_specs=[SMEM] + [VMEM] * (len(op...]
  transfers between devices with their start and end apart: 10 -> 10, of which waited for: 7 -> 6; matrix products, arithmetic and copies ran while one was open for 0% -> 0% of each run, Pallas kernels for 1% -> 3%
where the time goes in v8:
time: 201 us; the launch traced here: 199 us
  blocking collectives  94.9 us (47%)
  starting transfers between devices  47.8 us (24%)
  waiting for transfers between devices  38.5 us (19%)
  Pallas kernels  11.7 us (6%)
  local copies, waits for them, and re-layouts  4.6 us (2%)
    all_to_all x1, blocking collectives, on_device(): parts = lax.all_to_all(parts, 'y', 0, 0, tiled=True)  40 us
    all_to_all x1, blocking collectives, on_device(): lax.all_to_all(jnp.broadcast_to(rows[None], (8, 3, 32, 896)), 'y', 0, 0,...  35.5 us
    ppermute x3, starting transfers between devices, exchange(): return lax.ppermute(values, axis, [(0, 1), (1, 0)])  23.5 us
    ppermute x6, starting transfers between devices, shift(): return lax.ppermute(values, 'x', [(i, (i + step) % 4) for i in range(4)])  19.9 us
    all_to_all x1, blocking collectives, on_device(): terms = lax.all_to_all(terms, RING, 0, 0, tiled=True)  19.5 us
    ppermute x6, waiting for transfers between devices, shift(): return lax.ppermute(values, 'x', [(i, (i + step) % 4) for i in range(4)])  19.1 us
    all_to_all x1, waiting for transfers between devices, on_device(): lax.all_to_all(acts, RING, 0, 0, tiled=True)  12.9 us
    pallas_call x7, Pallas kernels, call(): pl.pallas_call(kernel, out_shape=outs, in_specs=[SMEM] + [VMEM] * (len(op...  10.3 us
  transfers between devices with their start and end apart: 10, of which 6 were waited for; matrix products, arithmetic and copies ran while one was open for 0% of the time, Pallas kernels for 3%

profile of v8, /device:TPU:1, one launch (start us, length us, event | category | flops | bytes accessed | tf_op | source)
XLA Modules:
  0.0 199.0 jit_solution(1098892154693258985)
XLA Ops:
  4.4 11.5 %collective-permute-start = (bf16[384,896]{1,0:T(8,128)(2,1)S(1)}, bf16[384,896]{1,0:T(8,128)(2,1)S(1)}, u32[]{:S(2)}, u32[]{:S(2)}) collective-permute-start(bf16[384,896]{1,0:T(8,128)(2,1)S(1)} %get-tuple-element.11), channel_id=1, source_target_pairs={{0,4},{4,0},{1,5},{5,1},{2,6},{6,2},{3,7},{7,3},{8,12},{12,8},{9,1... | collective-permute-start | bytes 2064392 | tf_op jit(solution)/shard_map/ppermute | solution.py:37
  15.9 3.1 %collective-permute-start.1 = (bf16[384,896]{1,0:T(8,128)(2,1)S(1)}, bf16[384,896]{1,0:T(8,128)(2,1)S(1)}, u32[]{:S(2)}, u32[]{:S(2)}) collective-permute-start(bf16[384,896]{1,0:T(8,128)(2,1)S(1)} %get-tuple-element.12.b0), channel_id=1, source_target_pairs={{0,1},{1,2},{2,3},{3,0},{4,5},{5,6},{6,7},{7,4},{8,9},{9,10},{10,1... | collective-permute-start | bytes 2064392 | tf_op jit(solution)/shard_map/ppermute | solution.py:33
  19.0 3.4 %collective-permute-start.2 = (bf16[384,896]{1,0:T(8,128)(2,1)S(1)}, bf16[384,896]{1,0:T(8,128)(2,1)S(1)}, u32[]{:S(2)}, u32[]{:S(2)}) collective-permute-start(bf16[384,896]{1,0:T(8,128)(2,1)S(1)} %get-tuple-element.12.b0), channel_id=1, source_target_pairs={{0,3},{1,0},{2,1},{3,2},{4,7},{5,4},{6,5},{7,6},{8,11},{9,8},{10,9... | collective-permute-start | bytes 2064392 | tf_op jit(solution)/shard_map/ppermute | solution.py:33
  22.4 3.4 %collective-permute-start.3 = (bf16[384,896]{1,0:T(8,128)(2,1)S(1)}, bf16[384,896]{1,0:T(8,128)(2,1)S(1)}, u32[]{:S(2)}, u32[]{:S(2)}) collective-permute-start(bf16[384,896]{1,0:T(8,128)(2,1)S(1)} %get-tuple-element.12.b0), channel_id=1, source_target_pairs={{0,2},{1,3},{2,0},{3,1},{4,6},{5,7},{6,4},{7,5},{8,10},{9,11},{10,... | collective-permute-start | bytes 2064392 | tf_op jit(solution)/shard_map/ppermute | solution.py:33
  25.9 4.3 %collective-permute-done.block = bf16[384,896]{1,0:T(8,128)(2,1)S(1)} collective-permute-done((bf16[384,896]{1,0:T(8,128)(2,1)S(1)}, bf16[384,896]{1,0:T(8,128)(2,1)S(1)}, u32[]{:S(2)}, u32[]{:S(2)}) %collective-permute-start) | collective-permute-done | bytes 688160 | tf_op jit(solution)/shard_map/ppermute | solution.py:37
  30.2 1.4 shard_map.69.b0
  31.7 3.3 %collective-permute-done.1.b1 = bf16[384,896]{1,0:T(8,128)(2,1)S(1)} collective-permute-done((bf16[384,896]{1,0:T(8,128)(2,1)S(1)}, bf16[384,896]{1,0:T(8,128)(2,1)S(1)}, u32[]{:S(2)}, u32[]{:S(2)}) %collective-permute-start.1) | collective-permute-done | bytes 688160 | tf_op jit(solution)/shard_map/ppermute | solution.py:33
  35.0 1.6 collective-permute-done.2.b2
  36.6 14.1 %collective-permute-done.3.b3 = bf16[384,896]{1,0:T(8,128)(2,1)S(1)} collective-permute-done((bf16[384,896]{1,0:T(8,128)(2,1)S(1)}, bf16[384,896]{1,0:T(8,128)(2,1)S(1)}, u32[]{:S(2)}, u32[]{:S(2)}) %collective-permute-start.3) | collective-permute-done | bytes 688160 | tf_op jit(solution)/shard_map/ppermute | solution.py:33
  51.5 4.4 %collective-permute-start.5 = (bf16[384,896]{1,0:T(8,128)(2,1)}, bf16[384,896]{1,0:T(8,128)(2,1)}, u32[]{:S(2)}, u32[]{:S(2)}) collective-permute-start(bf16[384,896]{1,0:T(8,128)(2,1)} %shard_map.69.b0), channel_id=1, source_target_pairs={{0,1},{1,2},{2,3},{3,0},{4,5},{5,6},{6,7},{7,4},{8,9},{9,10},{10,1... | collective-permute-start | bytes 2064392 | tf_op jit(solution)/shard_map/ppermute | solution.py:33
  55.9 2.5 %collective-permute-start.6 = (bf16[384,896]{1,0:T(8,128)(2,1)}, bf16[384,896]{1,0:T(8,128)(2,1)}, u32[]{:S(2)}, u32[]{:S(2)}) collective-permute-start(bf16[384,896]{1,0:T(8,128)(2,1)} %shard_map.69.b0), channel_id=1, source_target_pairs={{0,3},{1,0},{2,1},{3,2},{4,7},{5,4},{6,5},{7,6},{8,11},{9,8},{10,9... | collective-permute-start | bytes 2064392 | tf_op jit(solution)/shard_map/ppermute | solution.py:33
  58.4 3.1 %collective-permute-start.7 = (bf16[384,896]{1,0:T(8,128)(2,1)}, bf16[384,896]{1,0:T(8,128)(2,1)}, u32[]{:S(2)}, u32[]{:S(2)}) collective-permute-start(bf16[384,896]{1,0:T(8,128)(2,1)} %shard_map.69.b0), channel_id=1, source_target_pairs={{0,2},{1,3},{2,0},{3,1},{4,6},{5,7},{6,4},{7,5},{8,10},{9,11},{10,... | collective-permute-start | bytes 2064392 | tf_op jit(solution)/shard_map/ppermute | solution.py:33
  62.9 4.3 %all-to-all-start = ((bf16[8,2,128,128]{3,2,1,0:T(8,128)(2,1)}), bf16[8,2,128,128]{3,2,1,0:T(8,128)(2,1)S(1)}, u32[]{:S(2)}, u32[]{:S(2)}) async-start(bf16[8,2,128,128]{3,2,1,0:T(8,128)(2,1)} %copy-done), calls=%async_computation | async-start | bytes 1048576 | tf_op jit(solution)/shard_map/all_to_all | solution.py:131
  67.2 1.3 shard_map.72.table
  68.6 12.9 %all-to-all-done.near = bf16[8,2,128,128]{3,2,1,0:T(8,128)(2,1)S(1)} async-done(((bf16[8,2,128,128]{3,2,1,0:T(8,128)(2,1)}), bf16[8,2,128,128]{3,2,1,0:T(8,128)(2,1)S(1)}, u32[]{:S(2)}, u32[]{:S(2)}) %all-to-all-start) | async-done | bytes 524320 | tf_op jit(solution)/shard_map/all_to_all | solution.py:131
  81.4 6.1 %collective-permute-start.4 = (bf16[8,2,128,128]{3,2,1,0:T(8,128)(2,1)S(1)}, bf16[8,2,128,128]{3,2,1,0:T(8,128)(2,1)S(1)}, u32[]{:S(2)}, u32[]{:S(2)}) collective-permute-start(bf16[8,2,128,128]{3,2,1,0:T(8,128)(2,1)S(1)} %all-to-all-done.near), channel_id=1, source_target_pairs={{0,8},{8,0},{1,9},{9,1},{2,10},{10,2},{3,11},{11,3},{4,12},{12,4},... | collective-permute-start | bytes 1572872 | tf_op jit(solution)/shard_map/ppermute | solution.py:37
  87.6 1.9 shard_map.73.moved
  89.6 2.4 %shard_map.74 = bf16[8,3,32,896]{3,2,1,0:T(8,128)(2,1)S(1)} custom-call(s32[9]{0:T(128)S(1)} %copy-done.6, bf16[8,2,128,128]{3,2,1,0:T(8,128)(2,1)S(1)} %all-to-all-done.near, bf16[8,2,128,128]{3,2,1,0:T(8,128)(2,1)S(1)} %collective-permute-done.4.other, bf16[3,512,896]{2,1,0:T(8,128)(2,1)S(1)} %shard_map.70.kept, bf16[3,512,896]{2,1,0:T(8,128)(2,1)S(1)} %shard_map.73.moved), custom_call_target="tpu_custom_call" | custom-call | flops 1409286144 | bytes 8000000 | tf_op jit(solution)/shard_map/pallas_call | solution.py:21
  92.0 40.0 %all_to_all.20 = bf16[8,3,32,896]{3,2,1,0:T(8,128)(2,1)S(1)} all-to-all(bf16[8,3,32,896]{3,2,1,0:T(8,128)(2,1)S(1)} %shard_map.74), channel_id=1, replica_groups=mesh['y'=8,'zl'=4,'core'=2,'zh'=2,'x'=4] {'y'}, dimensions={0} | all-to-all | bytes 2752512 | tf_op jit(solution)/shard_map/all_to_all | solution.py:138
  132.4 35.5 %all_to_all.21.acts = bf16[8,3,32,896]{3,2,1,0:T(8,128)(2,1)S(1)} all-to-all(bf16[8,3,32,896]{3,2,1,0:T(8,128)(2,1)S(1)} %broadcast_in_dim.2), channel_id=1, replica_groups=mesh['y'=8,'zl'=4,'core'=2,'zh'=2,'x'=4] {'y'}, dimensions={0} | all-to-all | bytes 2752512 | tf_op jit(solution)/shard_map/all_to_all | solution.py:146
  167.9 2.6 %shard_map.75 = (f32[8,2,128,128]{3,2,1,0:T(8,128)S(1)}, f32[8,2,128,128]{3,2,1,0:T(8,128)S(1)}) custom-call(s32[9]{0:T(128)S(1)} %copy-done.6, bf16[8,3,32,896]{3,2,1,0:T(8,128)(2,1)S(1)} %all_to_all.21.acts, bf16[3,512,896]{2,1,0:T(8,128)(2,1)S(1)} %shard_map.70.kept, bf16[3,512,896]{2,1,0:T(8,128)(2,1)S(1)} %shard_map.73.moved), custom_call_target="tpu_custom_call" | custom-call | flops 1409286144 | bytes 8000000 | tf_op jit(solution)/shard_map/pallas_call | solution.py:21
  170.5 5.9 %collective-permute-start.8 = (f32[8,2,128,128]{3,2,1,0:T(8,128)S(1)}, f32[8,2,128,128]{3,2,1,0:T(8,128)S(1)}, u32[]{:S(2)}, u32[]{:S(2)}) collective-permute-start(f32[8,2,128,128]{3,2,1,0:T(8,128)S(1)} %get-tuple-element.19), channel_id=1, source_target_pairs={{0,8},{8,0},{1,9},{9,1},{2,10},{10,2},{3,11},{11,3},{4,12},{12,4},... | collective-permute-start | bytes 3145736 | tf_op jit(solution)/shard_map/ppermute | solution.py:37
  176.5 2.3 %collective-permute-done.8 = f32[8,2,128,128]{3,2,1,0:T(8,128)S(1)} collective-permute-done((f32[8,2,128,128]{3,2,1,0:T(8,128)S(1)}, f32[8,2,128,128]{3,2,1,0:T(8,128)S(1)}, u32[]{:S(2)}, u32[]{:S(2)}) %collective-permute-start.8) | collective-permute-done | bytes 1048608 | tf_op jit(solution)/shard_map/ppermute | solution.py:37
  178.8 19.5 %all_to_all.22 = bf16[8,2,128,128]{3,2,1,0:T(8,128)(2,1)S(1)} all-to-all(bf16[8,2,128,128]{3,2,1,0:T(8,128)(2,1)S(1)} %add_convert_fusion), channel_id=1, replica_groups=mesh['y'=8,'zl'=4,'core'=2,'zh'=2,'x'=4] {'zh','zl'}, dimensions={0} | all-to-all | bytes 1048576 | tf_op jit(solution)/shard_map/all_to_all | solution.py:153
  (33 shorter events, 7.2 us)
Async XLA Ops:
  0.7 1.0 copy-start.1
  1.7 1.0 copy-start.2
  2.8 1.0 copy-start.3
  3.8 57.7 %copy-start.4 = (s32[3]{0:T(128)}, s32[3]{0:T(128)S(1)}, u32[]{:S(2)}) copy-start(s32[3]{0:T(128)S(1)} %pad_add_fusion.place) | copy-start | bytes 40
  4.4 25.8 %collective-permute-start = (bf16[384,896]{1,0:T(8,128)(2,1)S(1)}, bf16[384,896]{1,0:T(8,128)(2,1)S(1)}, u32[]{:S(2)}, u32[]{:S(2)}) collective-permute-start(bf16[384,896]{1,0:T(8,128)(2,1)S(1)} %get-tuple-element.11), channel_id=1, source_target_pairs={{0,4},{4,0},{1,5},{5,1},{2,6},{6,2},{3,7},{7,3},{8,12},{12,8},{9,1... | collective-permute-start | bytes 2064392 | tf_op jit(solution)/shard_map/ppermute | solution.py:37
  15.9 19.1 %collective-permute-start.1 = (bf16[384,896]{1,0:T(8,128)(2,1)S(1)}, bf16[384,896]{1,0:T(8,128)(2,1)S(1)}, u32[]{:S(2)}, u32[]{:S(2)}) collective-permute-start(bf16[384,896]{1,0:T(8,128)(2,1)S(1)} %get-tuple-element.12.b0), channel_id=1, source_target_pairs={{0,1},{1,2},{2,3},{3,0},{4,5},{5,6},{6,7},{7,4},{8,9},{9,10},{10,1... | collective-permute-start | bytes 2064392 | tf_op jit(solution)/shard_map/ppermute | solution.py:33
  19.0 17.6 %collective-permute-start.2 = (bf16[384,896]{1,0:T(8,128)(2,1)S(1)}, bf16[384,896]{1,0:T(8,128)(2,1)S(1)}, u32[]{:S(2)}, u32[]{:S(2)}) collective-permute-start(bf16[384,896]{1,0:T(8,128)(2,1)S(1)} %get-tuple-element.12.b0), channel_id=1, source_target_pairs={{0,3},{1,0},{2,1},{3,2},{4,7},{5,4},{6,5},{7,6},{8,11},{9,8},{10,9... | collective-permute-start | bytes 2064392 | tf_op jit(solution)/shard_map/ppermute | solution.py:33
  22.4 28.3 %collective-permute-start.3 = (bf16[384,896]{1,0:T(8,128)(2,1)S(1)}, bf16[384,896]{1,0:T(8,128)(2,1)S(1)}, u32[]{:S(2)}, u32[]{:S(2)}) collective-permute-start(bf16[384,896]{1,0:T(8,128)(2,1)S(1)} %get-tuple-element.12.b0), channel_id=1, source_target_pairs={{0,2},{1,3},{2,0},{3,1},{4,6},{5,7},{6,4},{7,5},{8,10},{9,11},{10,... | collective-permute-start | bytes 2064392 | tf_op jit(solution)/shard_map/ppermute | solution.py:33
  31.6 29.9 %copy-start.7 = (bf16[128,128]{1,0:T(8,128)(2,1)S(1)}, bf16[128,128]{1,0:T(8,128)(2,1)}, u32[]{:S(2)}) copy-start(bf16[128,128]{1,0:T(8,128)(2,1)} %tokens) | copy-start | bytes 98308
  31.7 29.9 %copy-start.8 = (bf16[128,128]{1,0:T(8,128)(2,1)S(1)}, bf16[128,128]{1,0:T(8,128)(2,1)}, u32[]{:S(2)}) copy-start(bf16[128,128]{1,0:T(8,128)(2,1)} %grad.1) | copy-start | bytes 98308
  51.5 36.1 %collective-permute-start.5 = (bf16[384,896]{1,0:T(8,128)(2,1)}, bf16[384,896]{1,0:T(8,128)(2,1)}, u32[]{:S(2)}, u32[]{:S(2)}) collective-permute-start(bf16[384,896]{1,0:T(8,128)(2,1)} %shard_map.69.b0), channel_id=1, source_target_pairs={{0,1},{1,2},{2,3},{3,0},{4,5},{5,6},{6,7},{7,4},{8,9},{9,10},{10,1... | collective-permute-start | bytes 2064392 | tf_op jit(solution)/shard_map/ppermute | solution.py:33
  55.9 31.7 %collective-permute-start.6 = (bf16[384,896]{1,0:T(8,128)(2,1)}, bf16[384,896]{1,0:T(8,128)(2,1)}, u32[]{:S(2)}, u32[]{:S(2)}) collective-permute-start(bf16[384,896]{1,0:T(8,128)(2,1)} %shard_map.69.b0), channel_id=1, source_target_pairs={{0,3},{1,0},{2,1},{3,2},{4,7},{5,4},{6,5},{7,6},{8,11},{9,8},{10,9... | collective-permute-start | bytes 2064392 | tf_op jit(solution)/shard_map/ppermute | solution.py:33
  58.4 29.2 %collective-permute-start.7 = (bf16[384,896]{1,0:T(8,128)(2,1)}, bf16[384,896]{1,0:T(8,128)(2,1)}, u32[]{:S(2)}, u32[]{:S(2)}) collective-permute-start(bf16[384,896]{1,0:T(8,128)(2,1)} %shard_map.69.b0), channel_id=1, source_target_pairs={{0,2},{1,3},{2,0},{3,1},{4,6},{5,7},{6,4},{7,5},{8,10},{9,11},{10,... | collective-permute-start | bytes 2064392 | tf_op jit(solution)/shard_map/ppermute | solution.py:33
  62.2 0.8 copy-start
  62.9 18.5 %all-to-all-start = ((bf16[8,2,128,128]{3,2,1,0:T(8,128)(2,1)}), bf16[8,2,128,128]{3,2,1,0:T(8,128)(2,1)S(1)}, u32[]{:S(2)}, u32[]{:S(2)}) async-start(bf16[8,2,128,128]{3,2,1,0:T(8,128)(2,1)} %copy-done), calls=%async_computation | async-start | bytes 1048576 | tf_op jit(solution)/shard_map/all_to_all | solution.py:131
  67.2 20.4 %copy-start.5 = (s32[3]{0:T(128)S(1)}, s32[3]{0:T(128)}, u32[]{:S(2)}) copy-start(s32[3]{0:T(128)} %copy-done.4) | copy-start | bytes 40
  68.6 21.0 %copy-start.6 = (s32[9]{0:T(128)S(1)}, s32[9]{0:T(128)}, u32[]{:S(2)}) copy-start(s32[9]{0:T(128)} %shard_map.72.table) | copy-start | bytes 112
  81.4 8.1 %collective-permute-start.4 = (bf16[8,2,128,128]{3,2,1,0:T(8,128)(2,1)S(1)}, bf16[8,2,128,128]{3,2,1,0:T(8,128)(2,1)S(1)}, u32[]{:S(2)}, u32[]{:S(2)}) collective-permute-start(bf16[8,2,128,128]{3,2,1,0:T(8,128)(2,1)S(1)} %all-to-all-done.near), channel_id=1, source_target_pairs={{0,8},{8,0},{1,9},{9,1},{2,10},{10,2},{3,11},{11,3},{4,12},{12,4},... | collective-permute-start | bytes 1572872 | tf_op jit(solution)/shard_map/ppermute | solution.py:37
  170.5 8.2 %collective-permute-start.8 = (f32[8,2,128,128]{3,2,1,0:T(8,128)S(1)}, f32[8,2,128,128]{3,2,1,0:T(8,128)S(1)}, u32[]{:S(2)}, u32[]{:S(2)}) collective-permute-start(f32[8,2,128,128]{3,2,1,0:T(8,128)S(1)} %get-tuple-element.19), channel_id=1, source_target_pairs={{0,8},{8,0},{1,9},{9,1},{2,10},{10,2},{3,11},{11,3},{4,12},{12,4},... | collective-permute-start | bytes 3145736 | tf_op jit(solution)/shard_map/ppermute | solution.py:37

commit v9 on v8

--- a/solution.py
+++ b/solution.py
@@ -112,14 +112,15 @@
     block = exchange(send, "zh")
     kept = (shift(keep, 1), shift(keep, -1), shift(keep, 2))
     packed = jax.ShapeDtypeStruct((3, 512, 896), BF16)
-    (first,) = call(pack_kernel, [packed], (place, keep, *kept), [], 0, 0)
     (hold,) = call(hold_kernel, [half], (place, block), [], 30000000000, 1400000)
-    block, first, tokens = lax.optimization_barrier((hold, first, tokens))
+    block, left = lax.optimization_barrier((hold, kept[0]))
     moved = (block, shift(block, 1), shift(block, -1), shift(block, 2))
+    (first,) = call(pack_kernel, [packed], (place, keep, left, *kept[1:]), [], 0, 0)
+    first, tokens = lax.optimization_barrier((first, tokens))
     (second,) = call(pack_kernel, [packed], (place, *moved), [], 0, 0)
     weights = (first, second)
     (acts,) = call(
-        spread_kernel, [jax.ShapeDtypeStruct((8, 2, 128, 128), BF16)], (place, tokens, grad_mixed), [], 30000000000, 1000000
+        spread_kernel, [jax.ShapeDtypeStruct((8, 2, 128, 128), BF16)], (place, tokens, grad_mixed), [], 0, 0
     )
     table = pl.pallas_call(
         table_kernel,

time: 201 us -> 203 us (level)
  waiting for transfers between devices: 38.5 us -> 31.6 us
  blocking collectives: 94.9 us -> 101 us
  starting transfers between devices: 47.8 us -> 51.4 us
    all_to_all x1, starting transfers between devices: 4.29 us -> 13.8 us  [on_device(): lax.all_to_all(acts, RING, 0, 0, tiled=True)]
    ppermute x6, waiting for transfers between devices: 19.1 us -> 10.3 us  [shift(): return lax.ppermute(values, 'x', [(i, (i + step) % 4) for i in range(4)])]
    ppermute x3, starting transfers between devices: 23.5 us -> 18.9 us  [exchange(): return lax.ppermute(values, axis, [(0, 1), (1, 0)])]
    all_to_all x1, blocking collectives: 40 us -> 42.9 us  [on_device(): parts = lax.all_to_all(parts, 'y', 0, 0, tiled=True)]
    all_to_all x1, blocking collectives: 35.5 us -> 38 us  [on_device(): lax.all_to_all(jnp.broadcast_to(rows[None], (8, 3, 32, 896)), 'y', 0, 0,...]
  transfers between devices with their start and end apart: 10 -> 10, of which waited for: 6 -> 5; matrix products, arithmetic and copies ran while one was open for 0% -> 0% of each run, Pallas kernels for 3% -> 3%
where the time goes in v9:
time: 203 us; the launch traced here: 202 us
  blocking collectives  101 us (50%)
  starting transfers between devices  51.4 us (25%)
  waiting for transfers between devices  31.6 us (16%)
  Pallas kernels  11.7 us (6%)
  local copies, waits for them, and re-layouts  4.6 us (2%)
    all_to_all x1, blocking collectives, on_device(): parts = lax.all_to_all(parts, 'y', 0, 0, tiled=True)  42.9 us
    all_to_all x1, blocking collectives, on_device(): lax.all_to_all(jnp.broadcast_to(rows[None], (8, 3, 32, 896)), 'y', 0, 0,...  38 us
    all_to_all x1, blocking collectives, on_device(): terms = lax.all_to_all(terms, RING, 0, 0, tiled=True)  20.4 us
    ppermute x3, starting transfers between devices, exchange(): return lax.ppermute(values, axis, [(0, 1), (1, 0)])  18.9 us
    ppermute x6, starting transfers between devices, shift(): return lax.ppermute(values, 'x', [(i, (i + step) % 4) for i in range(4)])  18.7 us
    all_to_all x1, waiting for transfers between devices, on_device(): lax.all_to_all(acts, RING, 0, 0, tiled=True)  14.6 us
    all_to_all x1, starting transfers between devices, on_device(): lax.all_to_all(acts, RING, 0, 0, tiled=True)  13.8 us
    pallas_call x7, Pallas kernels, call(): pl.pallas_call(kernel, out_shape=outs, in_specs=[SMEM] + [VMEM] * (len(op...  10.4 us
  transfers between devices with their start and end apart: 10, of which 5 were waited for; matrix products, arithmetic and copies ran while one was open for 0% of the time, Pallas kernels for 3%

profile of v9, /device:TPU:1, one launch (start us, length us, event | category | flops | bytes accessed | tf_op | source)
XLA Modules:
  0.0 201.9 jit_solution(15898495663643917138)
XLA Ops:
  0.7 1.0 copy-done.1
  4.4 11.5 %collective-permute-start = (bf16[384,896]{1,0:T(8,128)(2,1)S(1)}, bf16[384,896]{1,0:T(8,128)(2,1)S(1)}, u32[]{:S(2)}, u32[]{:S(2)}) collective-permute-start(bf16[384,896]{1,0:T(8,128)(2,1)S(1)} %get-tuple-element.13), channel_id=1, source_target_pairs={{0,4},{4,0},{1,5},{5,1},{2,6},{6,2},{3,7},{7,3},{8,12},{12,8},{9,1... | collective-permute-start | bytes 2064392 | tf_op jit(solution)/shard_map/ppermute | solution.py:37
  15.9 3.1 %collective-permute-start.1 = (bf16[384,896]{1,0:T(8,128)(2,1)S(1)}, bf16[384,896]{1,0:T(8,128)(2,1)S(1)}, u32[]{:S(2)}, u32[]{:S(2)}) collective-permute-start(bf16[384,896]{1,0:T(8,128)(2,1)S(1)} %get-tuple-element.12.b0), channel_id=1, source_target_pairs={{0,1},{1,2},{2,3},{3,0},{4,5},{5,6},{6,7},{7,4},{8,9},{9,10},{10,1... | collective-permute-start | bytes 2064392 | tf_op jit(solution)/shard_map/ppermute | solution.py:33
  19.0 3.4 %collective-permute-start.2 = (bf16[384,896]{1,0:T(8,128)(2,1)S(1)}, bf16[384,896]{1,0:T(8,128)(2,1)S(1)}, u32[]{:S(2)}, u32[]{:S(2)}) collective-permute-start(bf16[384,896]{1,0:T(8,128)(2,1)S(1)} %get-tuple-element.12.b0), channel_id=1, source_target_pairs={{0,3},{1,0},{2,1},{3,2},{4,7},{5,4},{6,5},{7,6},{8,11},{9,8},{10,9... | collective-permute-start | bytes 2064392 | tf_op jit(solution)/shard_map/ppermute | solution.py:33
  22.4 3.4 %collective-permute-start.3 = (bf16[384,896]{1,0:T(8,128)(2,1)S(1)}, bf16[384,896]{1,0:T(8,128)(2,1)S(1)}, u32[]{:S(2)}, u32[]{:S(2)}) collective-permute-start(bf16[384,896]{1,0:T(8,128)(2,1)S(1)} %get-tuple-element.12.b0), channel_id=1, source_target_pairs={{0,2},{1,3},{2,0},{3,1},{4,6},{5,7},{6,4},{7,5},{8,10},{9,11},{10,... | collective-permute-start | bytes 2064392 | tf_op jit(solution)/shard_map/ppermute | solution.py:33
  25.9 4.3 %collective-permute-done.block = bf16[384,896]{1,0:T(8,128)(2,1)S(1)} collective-permute-done((bf16[384,896]{1,0:T(8,128)(2,1)S(1)}, bf16[384,896]{1,0:T(8,128)(2,1)S(1)}, u32[]{:S(2)}, u32[]{:S(2)}) %collective-permute-start) | collective-permute-done | bytes 688160 | tf_op jit(solution)/shard_map/ppermute | solution.py:37
  30.2 1.4 shard_map.69.b0
  31.7 3.3 %collective-permute-done.1.b1 = bf16[384,896]{1,0:T(8,128)(2,1)S(1)} collective-permute-done((bf16[384,896]{1,0:T(8,128)(2,1)S(1)}, bf16[384,896]{1,0:T(8,128)(2,1)S(1)}, u32[]{:S(2)}, u32[]{:S(2)}) %collective-permute-start.1) | collective-permute-done | bytes 688160 | tf_op jit(solution)/shard_map/ppermute | solution.py:33
  35.0 1.9 collective-permute-start.5
  36.9 4.6 %collective-permute-start.6 = (bf16[384,896]{1,0:T(8,128)(2,1)}, bf16[384,896]{1,0:T(8,128)(2,1)}, u32[]{:S(2)}, u32[]{:S(2)}) collective-permute-start(bf16[384,896]{1,0:T(8,128)(2,1)} %shard_map.69.b0), channel_id=1, source_target_pairs={{0,3},{1,0},{2,1},{3,2},{4,7},{5,4},{6,5},{7,6},{8,11},{9,8},{10,9... | collective-permute-start | bytes 2064392 | tf_op jit(solution)/shard_map/ppermute | solution.py:33
  41.5 2.3 %collective-permute-start.7 = (bf16[384,896]{1,0:T(8,128)(2,1)}, bf16[384,896]{1,0:T(8,128)(2,1)}, u32[]{:S(2)}, u32[]{:S(2)}) collective-permute-start(bf16[384,896]{1,0:T(8,128)(2,1)} %shard_map.69.b0), channel_id=1, source_target_pairs={{0,2},{1,3},{2,0},{3,1},{4,6},{5,7},{6,4},{7,5},{8,10},{9,11},{10,... | collective-permute-start | bytes 2064392 | tf_op jit(solution)/shard_map/ppermute | solution.py:33
  43.8 7.0 %collective-permute-done.3.b3 = bf16[384,896]{1,0:T(8,128)(2,1)S(1)} collective-permute-done((bf16[384,896]{1,0:T(8,128)(2,1)S(1)}, bf16[384,896]{1,0:T(8,128)(2,1)S(1)}, u32[]{:S(2)}, u32[]{:S(2)}) %collective-permute-start.3) | collective-permute-done | bytes 688160 | tf_op jit(solution)/shard_map/ppermute | solution.py:33
  53.0 13.8 %all-to-all-start = ((bf16[8,2,128,128]{3,2,1,0:T(8,128)(2,1)}), bf16[8,2,128,128]{3,2,1,0:T(8,128)(2,1)S(1)}, u32[]{:S(2)}, u32[]{:S(2)}) async-start(bf16[8,2,128,128]{3,2,1,0:T(8,128)(2,1)} %copy-done), calls=%async_computation | async-start | bytes 1048576 | tf_op jit(solution)/shard_map/all_to_all | solution.py:132
  66.8 1.3 shard_map.72.table
  68.1 14.6 %all-to-all-done.near = bf16[8,2,128,128]{3,2,1,0:T(8,128)(2,1)S(1)} async-done(((bf16[8,2,128,128]{3,2,1,0:T(8,128)(2,1)}), bf16[8,2,128,128]{3,2,1,0:T(8,128)(2,1)S(1)}, u32[]{:S(2)}, u32[]{:S(2)}) %all-to-all-start) | async-done | bytes 524320 | tf_op jit(solution)/shard_map/all_to_all | solution.py:132
  82.7 4.4 %collective-permute-start.4 = (bf16[8,2,128,128]{3,2,1,0:T(8,128)(2,1)S(1)}, bf16[8,2,128,128]{3,2,1,0:T(8,128)(2,1)S(1)}, u32[]{:S(2)}, u32[]{:S(2)}) collective-permute-start(bf16[8,2,128,128]{3,2,1,0:T(8,128)(2,1)S(1)} %all-to-all-done.near), channel_id=1, source_target_pairs={{0,8},{8,0},{1,9},{9,1},{2,10},{10,2},{3,11},{11,3},{4,12},{12,4},... | collective-permute-start | bytes 1572872 | tf_op jit(solution)/shard_map/ppermute | solution.py:37
  87.2 1.9 shard_map.73.moved
  89.1 2.4 %shard_map.74 = bf16[8,3,32,896]{3,2,1,0:T(8,128)(2,1)S(1)} custom-call(s32[9]{0:T(128)S(1)} %copy-done.8, bf16[8,2,128,128]{3,2,1,0:T(8,128)(2,1)S(1)} %all-to-all-done.near, bf16[8,2,128,128]{3,2,1,0:T(8,128)(2,1)S(1)} %collective-permute-done.4.other, bf16[3,512,896]{2,1,0:T(8,128)(2,1)S(1)} %shard_map.70.kept, bf16[3,512,896]{2,1,0:T(8,128)(2,1)S(1)} %shard_map.73.moved), custom_call_target="tpu_custom_call" | custom-call | flops 1409286144 | bytes 8000000 | tf_op jit(solution)/shard_map/pallas_call | solution.py:21
  91.5 42.9 %all_to_all.20 = bf16[8,3,32,896]{3,2,1,0:T(8,128)(2,1)S(1)} all-to-all(bf16[8,3,32,896]{3,2,1,0:T(8,128)(2,1)S(1)} %shard_map.74), channel_id=1, replica_groups=mesh['y'=8,'zl'=4,'core'=2,'zh'=2,'x'=4] {'y'}, dimensions={0} | all-to-all | bytes 2752512 | tf_op jit(solution)/shard_map/all_to_all | solution.py:139
  134.8 38.0 %all_to_all.21.acts = bf16[8,3,32,896]{3,2,1,0:T(8,128)(2,1)S(1)} all-to-all(bf16[8,3,32,896]{3,2,1,0:T(8,128)(2,1)S(1)} %broadcast_in_dim.2), channel_id=1, replica_groups=mesh['y'=8,'zl'=4,'core'=2,'zh'=2,'x'=4] {'y'}, dimensions={0} | all-to-all | bytes 2752512 | tf_op jit(solution)/shard_map/all_to_all | solution.py:147
  172.8 2.6 %shard_map.75 = (f32[8,2,128,128]{3,2,1,0:T(8,128)S(1)}, f32[8,2,128,128]{3,2,1,0:T(8,128)S(1)}) custom-call(s32[9]{0:T(128)S(1)} %copy-done.8, bf16[8,3,32,896]{3,2,1,0:T(8,128)(2,1)S(1)} %all_to_all.21.acts, bf16[3,512,896]{2,1,0:T(8,128)(2,1)S(1)} %shard_map.70.kept, bf16[3,512,896]{2,1,0:T(8,128)(2,1)S(1)} %shard_map.73.moved), custom_call_target="tpu_custom_call" | custom-call | flops 1409286144 | bytes 8000000 | tf_op jit(solution)/shard_map/pallas_call | solution.py:21
  175.4 3.0 %collective-permute-start.8 = (f32[8,2,128,128]{3,2,1,0:T(8,128)S(1)}, f32[8,2,128,128]{3,2,1,0:T(8,128)S(1)}, u32[]{:S(2)}, u32[]{:S(2)}) collective-permute-start(f32[8,2,128,128]{3,2,1,0:T(8,128)S(1)} %get-tuple-element.21), channel_id=1, source_target_pairs={{0,8},{8,0},{1,9},{9,1},{2,10},{10,2},{3,11},{11,3},{4,12},{12,4},... | collective-permute-start | bytes 3145736 | tf_op jit(solution)/shard_map/ppermute | solution.py:37
  178.4 2.3 %collective-permute-done.8 = f32[8,2,128,128]{3,2,1,0:T(8,128)S(1)} collective-permute-done((f32[8,2,128,128]{3,2,1,0:T(8,128)S(1)}, f32[8,2,128,128]{3,2,1,0:T(8,128)S(1)}, u32[]{:S(2)}, u32[]{:S(2)}) %collective-permute-start.8) | collective-permute-done | bytes 1048608 | tf_op jit(solution)/shard_map/ppermute | solution.py:37
  180.8 20.4 %all_to_all.22 = bf16[8,2,128,128]{3,2,1,0:T(8,128)(2,1)S(1)} all-to-all(bf16[8,2,128,128]{3,2,1,0:T(8,128)(2,1)S(1)} %add_convert_fusion), channel_id=1, replica_groups=mesh['y'=8,'zl'=4,'core'=2,'zh'=2,'x'=4] {'zh','zl'}, dimensions={0} | all-to-all | bytes 1048576 | tf_op jit(solution)/shard_map/all_to_all | solution.py:154
  (33 shorter events, 6.2 us)
Async XLA Ops:
  0.7 1.0 copy-start.1
  1.7 1.0 copy-start.2
  2.8 1.0 copy-start.3
  3.8 47.7 %copy-start.6 = (s32[3]{0:T(128)}, s32[3]{0:T(128)S(1)}, u32[]{:S(2)}) copy-start(s32[3]{0:T(128)S(1)} %pad_add_fusion.place) | copy-start | bytes 40
  4.4 25.8 %collective-permute-start = (bf16[384,896]{1,0:T(8,128)(2,1)S(1)}, bf16[384,896]{1,0:T(8,128)(2,1)S(1)}, u32[]{:S(2)}, u32[]{:S(2)}) collective-permute-start(bf16[384,896]{1,0:T(8,128)(2,1)S(1)} %get-tuple-element.13), channel_id=1, source_target_pairs={{0,4},{4,0},{1,5},{5,1},{2,6},{6,2},{3,7},{7,3},{8,12},{12,8},{9,1... | collective-permute-start | bytes 2064392 | tf_op jit(solution)/shard_map/ppermute | solution.py:37
  15.9 19.1 %collective-permute-start.1 = (bf16[384,896]{1,0:T(8,128)(2,1)S(1)}, bf16[384,896]{1,0:T(8,128)(2,1)S(1)}, u32[]{:S(2)}, u32[]{:S(2)}) collective-permute-start(bf16[384,896]{1,0:T(8,128)(2,1)S(1)} %get-tuple-element.12.b0), channel_id=1, source_target_pairs={{0,1},{1,2},{2,3},{3,0},{4,5},{5,6},{6,7},{7,4},{8,9},{9,10},{10,1... | collective-permute-start | bytes 2064392 | tf_op jit(solution)/shard_map/ppermute | solution.py:33
  19.0 24.7 %collective-permute-start.2 = (bf16[384,896]{1,0:T(8,128)(2,1)S(1)}, bf16[384,896]{1,0:T(8,128)(2,1)S(1)}, u32[]{:S(2)}, u32[]{:S(2)}) collective-permute-start(bf16[384,896]{1,0:T(8,128)(2,1)S(1)} %get-tuple-element.12.b0), channel_id=1, source_target_pairs={{0,3},{1,0},{2,1},{3,2},{4,7},{5,4},{6,5},{7,6},{8,11},{9,8},{10,9... | collective-permute-start | bytes 2064392 | tf_op jit(solution)/shard_map/ppermute | solution.py:33
  22.4 28.4 %collective-permute-start.3 = (bf16[384,896]{1,0:T(8,128)(2,1)S(1)}, bf16[384,896]{1,0:T(8,128)(2,1)S(1)}, u32[]{:S(2)}, u32[]{:S(2)}) collective-permute-start(bf16[384,896]{1,0:T(8,128)(2,1)S(1)} %get-tuple-element.12.b0), channel_id=1, source_target_pairs={{0,2},{1,3},{2,0},{3,1},{4,6},{5,7},{6,4},{7,5},{8,10},{9,11},{10,... | collective-permute-start | bytes 2064392 | tf_op jit(solution)/shard_map/ppermute | solution.py:33
  31.6 19.9 %copy-start.4 = (bf16[128,128]{1,0:T(8,128)(2,1)S(1)}, bf16[128,128]{1,0:T(8,128)(2,1)}, u32[]{:S(2)}) copy-start(bf16[128,128]{1,0:T(8,128)(2,1)} %tokens) | copy-start | bytes 98308
  31.7 19.9 %copy-start.5 = (bf16[128,128]{1,0:T(8,128)(2,1)S(1)}, bf16[128,128]{1,0:T(8,128)(2,1)}, u32[]{:S(2)}) copy-start(bf16[128,128]{1,0:T(8,128)(2,1)} %grad.1) | copy-start | bytes 98308
  35.0 52.1 %collective-permute-start.5 = (bf16[384,896]{1,0:T(8,128)(2,1)}, bf16[384,896]{1,0:T(8,128)(2,1)}, u32[]{:S(2)}, u32[]{:S(2)}) collective-permute-start(bf16[384,896]{1,0:T(8,128)(2,1)} %shard_map.69.b0), channel_id=1, source_target_pairs={{0,1},{1,2},{2,3},{3,0},{4,5},{5,6},{6,7},{7,4},{8,9},{9,10},{10,1... | collective-permute-start | bytes 2064392 | tf_op jit(solution)/shard_map/ppermute | solution.py:33
  36.9 50.2 %collective-permute-start.6 = (bf16[384,896]{1,0:T(8,128)(2,1)}, bf16[384,896]{1,0:T(8,128)(2,1)}, u32[]{:S(2)}, u32[]{:S(2)}) collective-permute-start(bf16[384,896]{1,0:T(8,128)(2,1)} %shard_map.69.b0), channel_id=1, source_target_pairs={{0,3},{1,0},{2,1},{3,2},{4,7},{5,4},{6,5},{7,6},{8,11},{9,8},{10,9... | collective-permute-start | bytes 2064392 | tf_op jit(solution)/shard_map/ppermute | solution.py:33
  41.5 45.7 %collective-permute-start.7 = (bf16[384,896]{1,0:T(8,128)(2,1)}, bf16[384,896]{1,0:T(8,128)(2,1)}, u32[]{:S(2)}, u32[]{:S(2)}) collective-permute-start(bf16[384,896]{1,0:T(8,128)(2,1)} %shard_map.69.b0), channel_id=1, source_target_pairs={{0,2},{1,3},{2,0},{3,1},{4,6},{5,7},{6,4},{7,5},{8,10},{9,11},{10,... | collective-permute-start | bytes 2064392 | tf_op jit(solution)/shard_map/ppermute | solution.py:33
  52.2 0.8 copy-start
  53.0 29.8 %all-to-all-start = ((bf16[8,2,128,128]{3,2,1,0:T(8,128)(2,1)}), bf16[8,2,128,128]{3,2,1,0:T(8,128)(2,1)S(1)}, u32[]{:S(2)}, u32[]{:S(2)}) async-start(bf16[8,2,128,128]{3,2,1,0:T(8,128)(2,1)} %copy-done), calls=%async_computation | async-start | bytes 1048576 | tf_op jit(solution)/shard_map/all_to_all | solution.py:132
  66.8 20.4 %copy-start.7 = (s32[3]{0:T(128)S(1)}, s32[3]{0:T(128)}, u32[]{:S(2)}) copy-start(s32[3]{0:T(128)} %copy-done.6) | copy-start | bytes 40
  68.1 21.0 %copy-start.8 = (s32[9]{0:T(128)S(1)}, s32[9]{0:T(128)}, u32[]{:S(2)}) copy-start(s32[9]{0:T(128)} %shard_map.72.table) | copy-start | bytes 112
  82.7 6.4 %collective-permute-start.4 = (bf16[8,2,128,128]{3,2,1,0:T(8,128)(2,1)S(1)}, bf16[8,2,128,128]{3,2,1,0:T(8,128)(2,1)S(1)}, u32[]{:S(2)}, u32[]{:S(2)}) collective-permute-start(bf16[8,2,128,128]{3,2,1,0:T(8,128)(2,1)S(1)} %all-to-all-done.near), channel_id=1, source_target_pairs={{0,8},{8,0},{1,9},{9,1},{2,10},{10,2},{3,11},{11,3},{4,12},{12,4},... | collective-permute-start | bytes 1572872 | tf_op jit(solution)/shard_map/ppermute | solution.py:37
  175.4 5.3 %collective-permute-start.8 = (f32[8,2,128,128]{3,2,1,0:T(8,128)S(1)}, f32[8,2,128,128]{3,2,1,0:T(8,128)S(1)}, u32[]{:S(2)}, u32[]{:S(2)}) collective-permute-start(f32[8,2,128,128]{3,2,1,0:T(8,128)S(1)} %get-tuple-element.21), channel_id=1, source_target_pairs={{0,8},{8,0},{1,9},{9,1},{2,10},{10,2},{3,11},{11,3},{4,12},{12,4},... | collective-permute-start | bytes 3145736 | tf_op jit(solution)/shard_map/ppermute | solution.py:37

commit v10 on v8

--- a/solution.py
+++ b/solution.py
@@ -85,7 +85,7 @@
         out[:, k] = total.astype(BF16).reshape(8, 32, 896)
 
 
-def output_kernel(table, acts, kept, moved, mine, theirs, held):
+def output_kernel(table, acts, kept, moved, mine, theirs):
     hidden, gate_grad, up_grad = (acts[:, k].reshape(256, 896) for k in range(3))
 
     def product(rows, block):
@@ -94,15 +94,25 @@
     for other_zh, rows in enumerate((kept, moved)):
         mixed = product(hidden, rows[DOWN])
         grad = product(gate_grad, rows[GATE]) + product(up_grad, rows[UP])
-        for slot in range(4):
-            f = table[4 * other_zh + slot]
-            side = (f + table[8]) % 2
-            for t in (0, 1):
-                part = (slice(128 * t, 128 * t + 128), slice(128 * slot, 128 * slot + 128))
-                held[side, 4 * t + f // 2, 0] = mixed[part]
-                held[side, 4 * t + f // 2, 1] = grad[part]
-    mine[...] = held[0]
-    theirs[...] = held[1]
+        for odd in (0, 1):
+
+            @pl.when((table[0] + table[8]) % 2 == odd)
+            def _(other_zh=other_zh, mixed=mixed, grad=grad, odd=odd):
+                for slot in range(4):
+                    f = table[4 * other_zh + slot]
+                    out = theirs if (odd + STEPS[slot]) % 2 else mine
+                    for t in (0, 1):
+                        part = (slice(128 * t, 128 * t + 128), slice(128 * slot, 128 * slot + 128))
+                        out[4 * t + f // 2, 0] = mixed[part]
+                        out[4 * t + f // 2, 1] = grad[part]
+
+
+def final_kernel(table, terms, mixed, tokens_grad):
+    for k, out in enumerate((mixed, tokens_grad)):
+        total = terms[0, k].astype(F32)
+        for i in range(1, 8):
+            total = total + terms[i, k].astype(F32)
+        out[...] = total.astype(BF16)
 
 
 def on_device(tokens, gate_weight, up_weight, down_weight, grad_mixed):
@@ -146,13 +156,13 @@
     rows = lax.all_to_all(jnp.broadcast_to(rows[None], (8, 3, 32, 896)), "y", 0, 0, tiled=True)
     terms = jax.ShapeDtypeStruct((8, 2, 128, 128), F32)
     mine, theirs = call(
-        output_kernel, [terms, terms], (table, rows, *weights), [pltpu.VMEM((2, 8, 2, 128, 128), F32)],
+        output_kernel, [terms, terms], (table, rows, *weights), [],
         6 * 256 * 1024 * 896, 8000000,
     )
     terms = (mine + exchange(theirs, "core")).astype(BF16)
     terms = lax.all_to_all(terms, RING, 0, 0, tiled=True)
-    both = jnp.sum(terms.astype(F32), axis=0).astype(BF16)
-    return both[0], both[1]
+    out = jax.ShapeDtypeStruct((128, 128), BF16)
+    return tuple(call(final_kernel, [out, out], (table, terms), [], 0, 0))
 
 
 def solution(mesh):

time: 201 us -> 202 us (level)
    pallas_call x7 -> x8, Pallas kernels: 10.3 us -> 11.7 us  [call(): pl.pallas_call(kernel, out_shape=outs, in_specs=[SMEM] + [VMEM] * (len(op...]
where the time goes in v10:
time: 202 us; the launch traced here: 200 us
  blocking collectives  94.2 us (47%)
  starting transfers between devices  48.5 us (24%)
  waiting for transfers between devices  38.5 us (19%)
  Pallas kernels  13 us (6%)
  local copies, waits for them, and re-layouts  3.96 us (2%)
    all_to_all x1, blocking collectives, on_device(): parts = lax.all_to_all(parts, 'y', 0, 0, tiled=True)  39.9 us
    all_to_all x1, blocking collectives, on_device(): lax.all_to_all(jnp.broadcast_to(rows[None], (8, 3, 32, 896)), 'y', 0, 0,...  34.7 us
    ppermute x3, starting transfers between devices, exchange(): return lax.ppermute(values, axis, [(0, 1), (1, 0)])  24.3 us
    ppermute x6, starting transfers between devices, shift(): return lax.ppermute(values, 'x', [(i, (i + step) % 4) for i in range(4)])  19.9 us
    all_to_all x1, blocking collectives, on_device(): terms = lax.all_to_all(terms, RING, 0, 0, tiled=True)  19.6 us
    ppermute x6, waiting for transfers between devices, shift(): return lax.ppermute(values, 'x', [(i, (i + step) % 4) for i in range(4)])  19.1 us
    all_to_all x1, waiting for transfers between devices, on_device(): lax.all_to_all(acts, RING, 0, 0, tiled=True)  12.9 us
    pallas_call x8, Pallas kernels, call(): pl.pallas_call(kernel, out_shape=outs, in_specs=[SMEM] + [VMEM] * (len(op...  11.7 us
  transfers between devices with their start and end apart: 10, of which 6 were waited for; matrix products, arithmetic and copies ran while one was open for 0% of the time, Pallas kernels for 3%

profile of v10, /device:TPU:1, one launch (start us, length us, event | category | flops | bytes accessed | tf_op | source)
XLA Modules:
  0.0 199.7 jit_solution(17944338870410742245)
XLA Ops:
  4.4 11.5 %collective-permute-start = (bf16[384,896]{1,0:T(8,128)(2,1)S(1)}, bf16[384,896]{1,0:T(8,128)(2,1)S(1)}, u32[]{:S(2)}, u32[]{:S(2)}) collective-permute-start(bf16[384,896]{1,0:T(8,128)(2,1)S(1)} %get-tuple-element.11), channel_id=1, source_target_pairs={{0,4},{4,0},{1,5},{5,1},{2,6},{6,2},{3,7},{7,3},{8,12},{12,8},{9,1... | collective-permute-start | bytes 2064392 | tf_op jit(solution)/shard_map/ppermute | solution.py:37
  15.9 3.1 %collective-permute-start.1 = (bf16[384,896]{1,0:T(8,128)(2,1)S(1)}, bf16[384,896]{1,0:T(8,128)(2,1)S(1)}, u32[]{:S(2)}, u32[]{:S(2)}) collective-permute-start(bf16[384,896]{1,0:T(8,128)(2,1)S(1)} %get-tuple-element.12.b0), channel_id=1, source_target_pairs={{0,1},{1,2},{2,3},{3,0},{4,5},{5,6},{6,7},{7,4},{8,9},{9,10},{10,1... | collective-permute-start | bytes 2064392 | tf_op jit(solution)/shard_map/ppermute | solution.py:33
  19.0 3.4 %collective-permute-start.2 = (bf16[384,896]{1,0:T(8,128)(2,1)S(1)}, bf16[384,896]{1,0:T(8,128)(2,1)S(1)}, u32[]{:S(2)}, u32[]{:S(2)}) collective-permute-start(bf16[384,896]{1,0:T(8,128)(2,1)S(1)} %get-tuple-element.12.b0), channel_id=1, source_target_pairs={{0,3},{1,0},{2,1},{3,2},{4,7},{5,4},{6,5},{7,6},{8,11},{9,8},{10,9... | collective-permute-start | bytes 2064392 | tf_op jit(solution)/shard_map/ppermute | solution.py:33
  22.4 3.4 %collective-permute-start.3 = (bf16[384,896]{1,0:T(8,128)(2,1)S(1)}, bf16[384,896]{1,0:T(8,128)(2,1)S(1)}, u32[]{:S(2)}, u32[]{:S(2)}) collective-permute-start(bf16[384,896]{1,0:T(8,128)(2,1)S(1)} %get-tuple-element.12.b0), channel_id=1, source_target_pairs={{0,2},{1,3},{2,0},{3,1},{4,6},{5,7},{6,4},{7,5},{8,10},{9,11},{10,... | collective-permute-start | bytes 2064392 | tf_op jit(solution)/shard_map/ppermute | solution.py:33
  25.9 4.3 %collective-permute-done.block = bf16[384,896]{1,0:T(8,128)(2,1)S(1)} collective-permute-done((bf16[384,896]{1,0:T(8,128)(2,1)S(1)}, bf16[384,896]{1,0:T(8,128)(2,1)S(1)}, u32[]{:S(2)}, u32[]{:S(2)}) %collective-permute-start) | collective-permute-done | bytes 688160 | tf_op jit(solution)/shard_map/ppermute | solution.py:37
  30.2 1.4 shard_map.69.b0
  31.7 3.3 %collective-permute-done.1.b1 = bf16[384,896]{1,0:T(8,128)(2,1)S(1)} collective-permute-done((bf16[384,896]{1,0:T(8,128)(2,1)S(1)}, bf16[384,896]{1,0:T(8,128)(2,1)S(1)}, u32[]{:S(2)}, u32[]{:S(2)}) %collective-permute-start.1) | collective-permute-done | bytes 688160 | tf_op jit(solution)/shard_map/ppermute | solution.py:33
  35.0 1.6 collective-permute-done.2.b2
  36.6 14.1 %collective-permute-done.3.b3 = bf16[384,896]{1,0:T(8,128)(2,1)S(1)} collective-permute-done((bf16[384,896]{1,0:T(8,128)(2,1)S(1)}, bf16[384,896]{1,0:T(8,128)(2,1)S(1)}, u32[]{:S(2)}, u32[]{:S(2)}) %collective-permute-start.3) | collective-permute-done | bytes 688160 | tf_op jit(solution)/shard_map/ppermute | solution.py:33
  51.5 4.4 %collective-permute-start.5 = (bf16[384,896]{1,0:T(8,128)(2,1)}, bf16[384,896]{1,0:T(8,128)(2,1)}, u32[]{:S(2)}, u32[]{:S(2)}) collective-permute-start(bf16[384,896]{1,0:T(8,128)(2,1)} %shard_map.69.b0), channel_id=1, source_target_pairs={{0,1},{1,2},{2,3},{3,0},{4,5},{5,6},{6,7},{7,4},{8,9},{9,10},{10,1... | collective-permute-start | bytes 2064392 | tf_op jit(solution)/shard_map/ppermute | solution.py:33
  55.9 2.5 %collective-permute-start.6 = (bf16[384,896]{1,0:T(8,128)(2,1)}, bf16[384,896]{1,0:T(8,128)(2,1)}, u32[]{:S(2)}, u32[]{:S(2)}) collective-permute-start(bf16[384,896]{1,0:T(8,128)(2,1)} %shard_map.69.b0), channel_id=1, source_target_pairs={{0,3},{1,0},{2,1},{3,2},{4,7},{5,4},{6,5},{7,6},{8,11},{9,8},{10,9... | collective-permute-start | bytes 2064392 | tf_op jit(solution)/shard_map/ppermute | solution.py:33
  58.4 3.1 %collective-permute-start.7 = (bf16[384,896]{1,0:T(8,128)(2,1)}, bf16[384,896]{1,0:T(8,128)(2,1)}, u32[]{:S(2)}, u32[]{:S(2)}) collective-permute-start(bf16[384,896]{1,0:T(8,128)(2,1)} %shard_map.69.b0), channel_id=1, source_target_pairs={{0,2},{1,3},{2,0},{3,1},{4,6},{5,7},{6,4},{7,5},{8,10},{9,11},{10,... | collective-permute-start | bytes 2064392 | tf_op jit(solution)/shard_map/ppermute | solution.py:33
  62.9 4.3 %all-to-all-start = ((bf16[8,2,128,128]{3,2,1,0:T(8,128)(2,1)}), bf16[8,2,128,128]{3,2,1,0:T(8,128)(2,1)S(1)}, u32[]{:S(2)}, u32[]{:S(2)}) async-start(bf16[8,2,128,128]{3,2,1,0:T(8,128)(2,1)} %copy-done), calls=%async_computation | async-start | bytes 1048576 | tf_op jit(solution)/shard_map/all_to_all | solution.py:141
  67.2 1.3 shard_map.72.table
  68.6 12.9 %all-to-all-done.near = bf16[8,2,128,128]{3,2,1,0:T(8,128)(2,1)S(1)} async-done(((bf16[8,2,128,128]{3,2,1,0:T(8,128)(2,1)}), bf16[8,2,128,128]{3,2,1,0:T(8,128)(2,1)S(1)}, u32[]{:S(2)}, u32[]{:S(2)}) %all-to-all-start) | async-done | bytes 524320 | tf_op jit(solution)/shard_map/all_to_all | solution.py:141
  81.4 6.1 %collective-permute-start.4 = (bf16[8,2,128,128]{3,2,1,0:T(8,128)(2,1)S(1)}, bf16[8,2,128,128]{3,2,1,0:T(8,128)(2,1)S(1)}, u32[]{:S(2)}, u32[]{:S(2)}) collective-permute-start(bf16[8,2,128,128]{3,2,1,0:T(8,128)(2,1)S(1)} %all-to-all-done.near), channel_id=1, source_target_pairs={{0,8},{8,0},{1,9},{9,1},{2,10},{10,2},{3,11},{11,3},{4,12},{12,4},... | collective-permute-start | bytes 1572872 | tf_op jit(solution)/shard_map/ppermute | solution.py:37
  87.6 1.9 shard_map.73.moved
  89.6 2.4 %shard_map.74 = bf16[8,3,32,896]{3,2,1,0:T(8,128)(2,1)S(1)} custom-call(s32[9]{0:T(128)S(1)} %copy-done.6, bf16[8,2,128,128]{3,2,1,0:T(8,128)(2,1)S(1)} %all-to-all-done.near, bf16[8,2,128,128]{3,2,1,0:T(8,128)(2,1)S(1)} %collective-permute-done.4.other, bf16[3,512,896]{2,1,0:T(8,128)(2,1)S(1)} %shard_map.70.kept, bf16[3,512,896]{2,1,0:T(8,128)(2,1)S(1)} %shard_map.73.moved), custom_call_target="tpu_custom_call" | custom-call | flops 1409286144 | bytes 8000000 | tf_op jit(solution)/shard_map/pallas_call | solution.py:21
  92.0 39.9 %all_to_all.20 = bf16[8,3,32,896]{3,2,1,0:T(8,128)(2,1)S(1)} all-to-all(bf16[8,3,32,896]{3,2,1,0:T(8,128)(2,1)S(1)} %shard_map.74), channel_id=1, replica_groups=mesh['y'=8,'zl'=4,'core'=2,'zh'=2,'x'=4] {'y'}, dimensions={0} | all-to-all | bytes 2752512 | tf_op jit(solution)/shard_map/all_to_all | solution.py:148
  132.3 34.7 %all_to_all.21.acts = bf16[8,3,32,896]{3,2,1,0:T(8,128)(2,1)S(1)} all-to-all(bf16[8,3,32,896]{3,2,1,0:T(8,128)(2,1)S(1)} %broadcast_in_dim.2), channel_id=1, replica_groups=mesh['y'=8,'zl'=4,'core'=2,'zh'=2,'x'=4] {'y'}, dimensions={0} | all-to-all | bytes 2752512 | tf_op jit(solution)/shard_map/all_to_all | solution.py:156
  167.1 2.7 %shard_map.75 = (f32[8,2,128,128]{3,2,1,0:T(8,128)S(1)}, f32[8,2,128,128]{3,2,1,0:T(8,128)S(1)}) custom-call(s32[9]{0:T(128)S(1)} %copy-done.6, bf16[8,3,32,896]{3,2,1,0:T(8,128)(2,1)S(1)} %all_to_all.21.acts, bf16[3,512,896]{2,1,0:T(8,128)(2,1)S(1)} %shard_map.70.kept, bf16[3,512,896]{2,1,0:T(8,128)(2,1)S(1)} %shard_map.73.moved), custom_call_target="tpu_custom_call" | custom-call | flops 1409286144 | bytes 8000000 | tf_op jit(solution)/shard_map/pallas_call | solution.py:21
  169.8 6.7 %collective-permute-start.8 = (f32[8,2,128,128]{3,2,1,0:T(8,128)S(1)}, f32[8,2,128,128]{3,2,1,0:T(8,128)S(1)}, u32[]{:S(2)}, u32[]{:S(2)}) collective-permute-start(f32[8,2,128,128]{3,2,1,0:T(8,128)S(1)} %get-tuple-element.19), channel_id=1, source_target_pairs={{0,8},{8,0},{1,9},{9,1},{2,10},{10,2},{3,11},{11,3},{4,12},{12,4},... | collective-permute-start | bytes 3145736 | tf_op jit(solution)/shard_map/ppermute | solution.py:37
  176.5 2.3 %collective-permute-done.8 = f32[8,2,128,128]{3,2,1,0:T(8,128)S(1)} collective-permute-done((f32[8,2,128,128]{3,2,1,0:T(8,128)S(1)}, f32[8,2,128,128]{3,2,1,0:T(8,128)S(1)}, u32[]{:S(2)}, u32[]{:S(2)}) %collective-permute-start.8) | collective-permute-done | bytes 1048608 | tf_op jit(solution)/shard_map/ppermute | solution.py:37
  178.9 19.6 %all_to_all.22.terms = bf16[8,2,128,128]{3,2,1,0:T(8,128)(2,1)S(1)} all-to-all(bf16[8,2,128,128]{3,2,1,0:T(8,128)(2,1)S(1)} %add_convert_fusion), channel_id=1, replica_groups=mesh['y'=8,'zl'=4,'core'=2,'zh'=2,'x'=4] {'zh','zl'}, dimensions={0} | all-to-all | bytes 1048576 | tf_op jit(solution)/shard_map/all_to_all | solution.py:163
  (32 shorter events, 7.7 us)
Async XLA Ops:
  0.7 1.0 copy-start.1
  1.7 1.0 copy-start.2
  2.8 1.0 copy-start.3
  3.8 57.7 %copy-start.4 = (s32[3]{0:T(128)}, s32[3]{0:T(128)S(1)}, u32[]{:S(2)}) copy-start(s32[3]{0:T(128)S(1)} %pad_add_fusion.place) | copy-start | bytes 40
  4.4 25.8 %collective-permute-start = (bf16[384,896]{1,0:T(8,128)(2,1)S(1)}, bf16[384,896]{1,0:T(8,128)(2,1)S(1)}, u32[]{:S(2)}, u32[]{:S(2)}) collective-permute-start(bf16[384,896]{1,0:T(8,128)(2,1)S(1)} %get-tuple-element.11), channel_id=1, source_target_pairs={{0,4},{4,0},{1,5},{5,1},{2,6},{6,2},{3,7},{7,3},{8,12},{12,8},{9,1... | collective-permute-start | bytes 2064392 | tf_op jit(solution)/shard_map/ppermute | solution.py:37
  15.9 19.1 %collective-permute-start.1 = (bf16[384,896]{1,0:T(8,128)(2,1)S(1)}, bf16[384,896]{1,0:T(8,128)(2,1)S(1)}, u32[]{:S(2)}, u32[]{:S(2)}) collective-permute-start(bf16[384,896]{1,0:T(8,128)(2,1)S(1)} %get-tuple-element.12.b0), channel_id=1, source_target_pairs={{0,1},{1,2},{2,3},{3,0},{4,5},{5,6},{6,7},{7,4},{8,9},{9,10},{10,1... | collective-permute-start | bytes 2064392 | tf_op jit(solution)/shard_map/ppermute | solution.py:33
  19.0 17.6 %collective-permute-start.2 = (bf16[384,896]{1,0:T(8,128)(2,1)S(1)}, bf16[384,896]{1,0:T(8,128)(2,1)S(1)}, u32[]{:S(2)}, u32[]{:S(2)}) collective-permute-start(bf16[384,896]{1,0:T(8,128)(2,1)S(1)} %get-tuple-element.12.b0), channel_id=1, source_target_pairs={{0,3},{1,0},{2,1},{3,2},{4,7},{5,4},{6,5},{7,6},{8,11},{9,8},{10,9... | collective-permute-start | bytes 2064392 | tf_op jit(solution)/shard_map/ppermute | solution.py:33
  22.4 28.3 %collective-permute-start.3 = (bf16[384,896]{1,0:T(8,128)(2,1)S(1)}, bf16[384,896]{1,0:T(8,128)(2,1)S(1)}, u32[]{:S(2)}, u32[]{:S(2)}) collective-permute-start(bf16[384,896]{1,0:T(8,128)(2,1)S(1)} %get-tuple-element.12.b0), channel_id=1, source_target_pairs={{0,2},{1,3},{2,0},{3,1},{4,6},{5,7},{6,4},{7,5},{8,10},{9,11},{10,... | collective-permute-start | bytes 2064392 | tf_op jit(solution)/shard_map/ppermute | solution.py:33
  31.6 29.9 %copy-start.7 = (bf16[128,128]{1,0:T(8,128)(2,1)S(1)}, bf16[128,128]{1,0:T(8,128)(2,1)}, u32[]{:S(2)}) copy-start(bf16[128,128]{1,0:T(8,128)(2,1)} %tokens) | copy-start | bytes 98308
  31.7 29.9 %copy-start.8 = (bf16[128,128]{1,0:T(8,128)(2,1)S(1)}, bf16[128,128]{1,0:T(8,128)(2,1)}, u32[]{:S(2)}) copy-start(bf16[128,128]{1,0:T(8,128)(2,1)} %grad.1) | copy-start | bytes 98308
  51.5 36.1 %collective-permute-start.5 = (bf16[384,896]{1,0:T(8,128)(2,1)}, bf16[384,896]{1,0:T(8,128)(2,1)}, u32[]{:S(2)}, u32[]{:S(2)}) collective-permute-start(bf16[384,896]{1,0:T(8,128)(2,1)} %shard_map.69.b0), channel_id=1, source_target_pairs={{0,1},{1,2},{2,3},{3,0},{4,5},{5,6},{6,7},{7,4},{8,9},{9,10},{10,1... | collective-permute-start | bytes 2064392 | tf_op jit(solution)/shard_map/ppermute | solution.py:33
  55.9 31.7 %collective-permute-start.6 = (bf16[384,896]{1,0:T(8,128)(2,1)}, bf16[384,896]{1,0:T(8,128)(2,1)}, u32[]{:S(2)}, u32[]{:S(2)}) collective-permute-start(bf16[384,896]{1,0:T(8,128)(2,1)} %shard_map.69.b0), channel_id=1, source_target_pairs={{0,3},{1,0},{2,1},{3,2},{4,7},{5,4},{6,5},{7,6},{8,11},{9,8},{10,9... | collective-permute-start | bytes 2064392 | tf_op jit(solution)/shard_map/ppermute | solution.py:33
  58.4 29.2 %collective-permute-start.7 = (bf16[384,896]{1,0:T(8,128)(2,1)}, bf16[384,896]{1,0:T(8,128)(2,1)}, u32[]{:S(2)}, u32[]{:S(2)}) collective-permute-start(bf16[384,896]{1,0:T(8,128)(2,1)} %shard_map.69.b0), channel_id=1, source_target_pairs={{0,2},{1,3},{2,0},{3,1},{4,6},{5,7},{6,4},{7,5},{8,10},{9,11},{10,... | collective-permute-start | bytes 2064392 | tf_op jit(solution)/shard_map/ppermute | solution.py:33
  62.2 0.8 copy-start
  62.9 18.5 %all-to-all-start = ((bf16[8,2,128,128]{3,2,1,0:T(8,128)(2,1)}), bf16[8,2,128,128]{3,2,1,0:T(8,128)(2,1)S(1)}, u32[]{:S(2)}, u32[]{:S(2)}) async-start(bf16[8,2,128,128]{3,2,1,0:T(8,128)(2,1)} %copy-done), calls=%async_computation | async-start | bytes 1048576 | tf_op jit(solution)/shard_map/all_to_all | solution.py:141
  67.2 20.4 %copy-start.5 = (s32[3]{0:T(128)S(1)}, s32[3]{0:T(128)}, u32[]{:S(2)}) copy-start(s32[3]{0:T(128)} %copy-done.4) | copy-start | bytes 40
  68.6 21.0 %copy-start.6 = (s32[9]{0:T(128)S(1)}, s32[9]{0:T(128)}, u32[]{:S(2)}) copy-start(s32[9]{0:T(128)} %shard_map.72.table) | copy-start | bytes 112
  81.4 8.1 %collective-permute-start.4 = (bf16[8,2,128,128]{3,2,1,0:T(8,128)(2,1)S(1)}, bf16[8,2,128,128]{3,2,1,0:T(8,128)(2,1)S(1)}, u32[]{:S(2)}, u32[]{:S(2)}) collective-permute-start(bf16[8,2,128,128]{3,2,1,0:T(8,128)(2,1)S(1)} %all-to-all-done.near), channel_id=1, source_target_pairs={{0,8},{8,0},{1,9},{9,1},{2,10},{10,2},{3,11},{11,3},{4,12},{12,4},... | collective-permute-start | bytes 1572872 | tf_op jit(solution)/shard_map/ppermute | solution.py:37
  169.8 9.0 %collective-permute-start.8 = (f32[8,2,128,128]{3,2,1,0:T(8,128)S(1)}, f32[8,2,128,128]{3,2,1,0:T(8,128)S(1)}, u32[]{:S(2)}, u32[]{:S(2)}) collective-permute-start(f32[8,2,128,128]{3,2,1,0:T(8,128)S(1)} %get-tuple-element.19), channel_id=1, source_target_pairs={{0,8},{8,0},{1,9},{9,1},{2,10},{10,2},{3,11},{11,3},{4,12},{12,4},... | collective-permute-start | bytes 3145736 | tf_op jit(solution)/shard_map/ppermute | solution.py:37

commit v11 on v8

--- a/solution.py
+++ b/solution.py
@@ -70,7 +70,19 @@
         out[i, 1] = grad[...]
 
 
-def sums_kernel(table, near, other, kept, moved, out, wide):
+def sums_kernel(table, near, other, kept, b0, b1, b2, b3, out, moved, wide, sems):
+    copies = [
+        [
+            pltpu.make_async_copy(
+                block.at[pl.ds(128 * k, 128)], moved.at[k, pl.ds(128 * slot, 128)], sems.at[4 * k + slot]
+            )
+            for slot, block in enumerate((b0, b1, b2, b3))
+        ]
+        for k in range(3)
+    ]
+    for k in range(3):
+        for copy in copies[k]:
+            copy.start()
     for other_zh in (0, 1):
         for slot in range(4):
             f = table[4 * other_zh + slot]
@@ -81,6 +93,8 @@
                     wide[which, pl.ds(128 * t, 128), pl.ds(512 * other_zh + 128 * slot, 128)] = tile
     for k in range(3):
         total = jnp.dot(wide[WHICH[k], :, :512], kept[k], preferred_element_type=F32)
+        for copy in copies[k]:
+            copy.wait()
         total = total + jnp.dot(wide[WHICH[k], :, 512:], moved[k], preferred_element_type=F32)
         out[:, k] = total.astype(BF16).reshape(8, 32, 896)
 
@@ -116,8 +130,6 @@
     (hold,) = call(hold_kernel, [half], (place, block), [], 30000000000, 1400000)
     block, first, tokens = lax.optimization_barrier((hold, first, tokens))
     moved = (block, shift(block, 1), shift(block, -1), shift(block, 2))
-    (second,) = call(pack_kernel, [packed], (place, *moved), [], 0, 0)
-    weights = (first, second)
     (acts,) = call(
         spread_kernel, [jax.ShapeDtypeStruct((8, 2, 128, 128), BF16)], (place, tokens, grad_mixed), [], 30000000000, 1000000
     )
@@ -130,11 +142,15 @@
     )(place)
     near, table = lax.optimization_barrier((lax.all_to_all(acts, RING, 0, 0, tiled=True), table))
 
-    (parts,) = call(
-        sums_kernel, [jax.ShapeDtypeStruct((8, 3, 32, 896), BF16)],
-        (table, near, exchange(near, "core"), *weights), [pltpu.VMEM((2, 256, 1024), BF16)],
-        6 * 256 * 1024 * 896, 8000000,
-    )
+    parts, second = pl.pallas_call(
+        sums_kernel,
+        out_shape=[jax.ShapeDtypeStruct((8, 3, 32, 896), BF16), packed],
+        in_specs=[SMEM] + [VMEM] * 3 + [pl.BlockSpec(memory_space=pl.ANY)] * 4,
+        out_specs=[VMEM, VMEM],
+        scratch_shapes=[pltpu.VMEM((2, 256, 1024), BF16), pltpu.SemaphoreType.DMA((12,))],
+        cost_estimate=pl.CostEstimate(flops=6 * 256 * 1024 * 896, bytes_accessed=8000000, transcendentals=0),
+        compiler_params=pltpu.CompilerParams(vmem_limit_bytes=12 << 20),
+    )(table, near, exchange(near, "core"), first, *moved)
     parts = lax.all_to_all(parts, "y", 0, 0, tiled=True)
     gate_value, hidden_grad, up_value = (jnp.sum(parts[:, k].astype(F32), axis=0) for k in range(3))
     sig = jax.nn.sigmoid(gate_value)
@@ -146,7 +162,7 @@
     rows = lax.all_to_all(jnp.broadcast_to(rows[None], (8, 3, 32, 896)), "y", 0, 0, tiled=True)
     terms = jax.ShapeDtypeStruct((8, 2, 128, 128), F32)
     mine, theirs = call(
-        output_kernel, [terms, terms], (table, rows, *weights), [pltpu.VMEM((2, 8, 2, 128, 128), F32)],
+        output_kernel, [terms, terms], (table, rows, first, second), [pltpu.VMEM((2, 8, 2, 128, 128), F32)],
         6 * 256 * 1024 * 896, 8000000,
     )
     terms = (mine + exchange(theirs, "core")).astype(BF16)

time: 201 us -> 205 us (1.020)
  waiting for transfers between devices: 38.5 us -> 42.7 us
  blocking collectives: 94.9 us -> 98.4 us
  starting transfers between devices: 47.8 us -> 44.8 us
    pallas_call x7 -> x5, Pallas kernels: 10.3 us -> 6.06 us  [call(): pl.pallas_call(kernel, out_shape=outs, in_specs=[SMEM] + [VMEM] * (len(op...]
    pallas_call x0 -> x1, Pallas kernels: none -> 4.27 us  [on_device(): pl.pallas_call(sums_kernel, out_shape=[jax.ShapeDtypeStruct((8, 3, 32, 89...]
    ppermute x3, starting transfers between devices: 23.5 us -> 20.6 us  [exchange(): return lax.ppermute(values, axis, [(0, 1), (1, 0)])]
  transfers between devices with their start and end apart: 10 -> 10, of which waited for: 6 -> 7; matrix products, arithmetic and copies ran while one was open for 0% -> 0% of each run, Pallas kernels for 3% -> 2%
where the time goes in v11:
time: 205 us; the launch traced here: 204 us
  blocking collectives  98.4 us (48%)
  starting transfers between devices  44.8 us (22%)
  waiting for transfers between devices  42.7 us (21%)
  Pallas kernels  11.5 us (6%)
  local copies, waits for them, and re-layouts  5.25 us (3%)
    all_to_all x1, blocking collectives, on_device(): parts = lax.all_to_all(parts, 'y', 0, 0, tiled=True)  41.9 us
    all_to_all x1, blocking collectives, on_device(): lax.all_to_all(jnp.broadcast_to(rows[None], (8, 3, 32, 896)), 'y', 0, 0,...  36.2 us
    ppermute x3, starting transfers between devices, exchange(): return lax.ppermute(values, axis, [(0, 1), (1, 0)])  20.6 us
    all_to_all x1, blocking collectives, on_device(): terms = lax.all_to_all(terms, RING, 0, 0, tiled=True)  20.4 us
    ppermute x6, starting transfers between devices, shift(): return lax.ppermute(values, 'x', [(i, (i + step) % 4) for i in range(4)])  19.9 us
    ppermute x6, waiting for transfers between devices, shift(): return lax.ppermute(values, 'x', [(i, (i + step) % 4) for i in range(4)])  19.7 us
    all_to_all x1, waiting for transfers between devices, on_device(): lax.all_to_all(acts, RING, 0, 0, tiled=True)  14.8 us
    ppermute x3, waiting for transfers between devices, exchange(): return lax.ppermute(values, axis, [(0, 1), (1, 0)])  8.09 us
  transfers between devices with their start and end apart: 10, of which 7 were waited for; matrix products, arithmetic and copies ran while one was open for 0% of the time, Pallas kernels for 2%

profile of v11, /device:TPU:1, one launch (start us, length us, event | category | flops | bytes accessed | tf_op | source)
XLA Modules:
  0.0 204.1 jit_solution(12686730843545874005)
XLA Ops:
  0.7 1.0 copy-done.1
  4.4 11.5 %collective-permute-start = (bf16[384,896]{1,0:T(8,128)(2,1)S(1)}, bf16[384,896]{1,0:T(8,128)(2,1)S(1)}, u32[]{:S(2)}, u32[]{:S(2)}) collective-permute-start(bf16[384,896]{1,0:T(8,128)(2,1)S(1)} %get-tuple-element.13), channel_id=1, source_target_pairs={{0,4},{4,0},{1,5},{5,1},{2,6},{6,2},{3,7},{7,3},{8,12},{12,8},{9,1... | collective-permute-start | bytes 2064392 | tf_op jit(solution)/shard_map/ppermute | solution.py:37
  15.9 4.7 %collective-permute-start.3 = (bf16[384,896]{1,0:T(8,128)(2,1)S(1)}, bf16[384,896]{1,0:T(8,128)(2,1)S(1)}, u32[]{:S(2)}, u32[]{:S(2)}) collective-permute-start(bf16[384,896]{1,0:T(8,128)(2,1)S(1)} %get-tuple-element.14.b0), channel_id=1, source_target_pairs={{0,2},{1,3},{2,0},{3,1},{4,6},{5,7},{6,4},{7,5},{8,10},{9,11},{10,... | collective-permute-start | bytes 2064392 | tf_op jit(solution)/shard_map/ppermute | solution.py:33
  20.6 2.8 %collective-permute-start.2 = (bf16[384,896]{1,0:T(8,128)(2,1)S(1)}, bf16[384,896]{1,0:T(8,128)(2,1)S(1)}, u32[]{:S(2)}, u32[]{:S(2)}) collective-permute-start(bf16[384,896]{1,0:T(8,128)(2,1)S(1)} %get-tuple-element.14.b0), channel_id=1, source_target_pairs={{0,3},{1,0},{2,1},{3,2},{4,7},{5,4},{6,5},{7,6},{8,11},{9,8},{10,9... | collective-permute-start | bytes 2064392 | tf_op jit(solution)/shard_map/ppermute | solution.py:33
  23.3 2.5 %collective-permute-start.1 = (bf16[384,896]{1,0:T(8,128)(2,1)S(1)}, bf16[384,896]{1,0:T(8,128)(2,1)S(1)}, u32[]{:S(2)}, u32[]{:S(2)}) collective-permute-start(bf16[384,896]{1,0:T(8,128)(2,1)S(1)} %get-tuple-element.14.b0), channel_id=1, source_target_pairs={{0,1},{1,2},{2,3},{3,0},{4,5},{5,6},{6,7},{7,4},{8,9},{9,10},{10,1... | collective-permute-start | bytes 2064392 | tf_op jit(solution)/shard_map/ppermute | solution.py:33
  25.9 4.3 %collective-permute-done.block = bf16[384,896]{1,0:T(8,128)(2,1)S(1)} collective-permute-done((bf16[384,896]{1,0:T(8,128)(2,1)S(1)}, bf16[384,896]{1,0:T(8,128)(2,1)S(1)}, u32[]{:S(2)}, u32[]{:S(2)}) %collective-permute-start) | collective-permute-done | bytes 688160 | tf_op jit(solution)/shard_map/ppermute | solution.py:37
  30.2 1.4 shard_map.69.b0
  31.7 3.7 %collective-permute-done.3.b3 = bf16[384,896]{1,0:T(8,128)(2,1)S(1)} collective-permute-done((bf16[384,896]{1,0:T(8,128)(2,1)S(1)}, bf16[384,896]{1,0:T(8,128)(2,1)S(1)}, u32[]{:S(2)}, u32[]{:S(2)}) %collective-permute-start.3) | collective-permute-done | bytes 688160 | tf_op jit(solution)/shard_map/ppermute | solution.py:33
  35.3 15.1 %collective-permute-done.2.b2 = bf16[384,896]{1,0:T(8,128)(2,1)S(1)} collective-permute-done((bf16[384,896]{1,0:T(8,128)(2,1)S(1)}, bf16[384,896]{1,0:T(8,128)(2,1)S(1)}, u32[]{:S(2)}, u32[]{:S(2)}) %collective-permute-start.2) | collective-permute-done | bytes 688160 | tf_op jit(solution)/shard_map/ppermute | solution.py:33
  52.2 4.7 %collective-permute-start.7 = (bf16[384,896]{1,0:T(8,128)(2,1)}, bf16[384,896]{1,0:T(8,128)(2,1)}, u32[]{:S(2)}, u32[]{:S(2)}) collective-permute-start(bf16[384,896]{1,0:T(8,128)(2,1)} %shard_map.69.b0), channel_id=1, source_target_pairs={{0,2},{1,3},{2,0},{3,1},{4,6},{5,7},{6,4},{7,5},{8,10},{9,11},{10,... | collective-permute-start | bytes 2064392 | tf_op jit(solution)/shard_map/ppermute | solution.py:33
  56.8 2.8 %collective-permute-start.6 = (bf16[384,896]{1,0:T(8,128)(2,1)}, bf16[384,896]{1,0:T(8,128)(2,1)}, u32[]{:S(2)}, u32[]{:S(2)}) collective-permute-start(bf16[384,896]{1,0:T(8,128)(2,1)} %shard_map.69.b0), channel_id=1, source_target_pairs={{0,3},{1,0},{2,1},{3,2},{4,7},{5,4},{6,5},{7,6},{8,11},{9,8},{10,9... | collective-permute-start | bytes 2064392 | tf_op jit(solution)/shard_map/ppermute | solution.py:33
  59.6 2.5 %collective-permute-start.5 = (bf16[384,896]{1,0:T(8,128)(2,1)}, bf16[384,896]{1,0:T(8,128)(2,1)}, u32[]{:S(2)}, u32[]{:S(2)}) collective-permute-start(bf16[384,896]{1,0:T(8,128)(2,1)} %shard_map.69.b0), channel_id=1, source_target_pairs={{0,1},{1,2},{2,3},{3,0},{4,5},{5,6},{6,7},{7,4},{8,9},{9,10},{10,1... | collective-permute-start | bytes 2064392 | tf_op jit(solution)/shard_map/ppermute | solution.py:33
  63.6 4.3 %all-to-all-start = ((bf16[8,2,128,128]{3,2,1,0:T(8,128)(2,1)}), bf16[8,2,128,128]{3,2,1,0:T(8,128)(2,1)S(1)}, u32[]{:S(2)}, u32[]{:S(2)}) async-start(bf16[8,2,128,128]{3,2,1,0:T(8,128)(2,1)} %copy-done), calls=%async_computation | async-start | bytes 1048576 | tf_op jit(solution)/shard_map/all_to_all | solution.py:143
  67.9 1.2 shard_map.72.table
  69.1 14.8 %all-to-all-done.near = bf16[8,2,128,128]{3,2,1,0:T(8,128)(2,1)S(1)} async-done(((bf16[8,2,128,128]{3,2,1,0:T(8,128)(2,1)}), bf16[8,2,128,128]{3,2,1,0:T(8,128)(2,1)S(1)}, u32[]{:S(2)}, u32[]{:S(2)}) %all-to-all-start) | async-done | bytes 524320 | tf_op jit(solution)/shard_map/all_to_all | solution.py:143
  83.9 4.3 %collective-permute-start.4 = (bf16[8,2,128,128]{3,2,1,0:T(8,128)(2,1)S(1)}, bf16[8,2,128,128]{3,2,1,0:T(8,128)(2,1)S(1)}, u32[]{:S(2)}, u32[]{:S(2)}) collective-permute-start(bf16[8,2,128,128]{3,2,1,0:T(8,128)(2,1)S(1)} %all-to-all-done.near), channel_id=1, source_target_pairs={{0,8},{8,0},{1,9},{9,1},{2,10},{10,2},{3,11},{11,3},{4,12},{12,4},... | collective-permute-start | bytes 1572872 | tf_op jit(solution)/shard_map/ppermute | solution.py:37
  88.2 1.5 collective-permute-done.4.other
  90.4 4.3 %shard_map.73 = (bf16[8,3,32,896]{3,2,1,0:T(8,128)(2,1)S(1)}, bf16[3,512,896]{2,1,0:T(8,128)(2,1)S(1)}) custom-call(s32[9]{0:T(128)S(1)} %copy-done.5, bf16[8,2,128,128]{3,2,1,0:T(8,128)(2,1)S(1)} %all-to-all-done.near, bf16[8,2,128,128]{3,2,1,0:T(8,128)(2,1)S(1)} %collective-permute-done.4.other, bf16[3,512,896]{2,1,0:T(8,128)(2,1)S(1)} %shard_map.70.kept, ...), custom_call_target="tpu_custom_call" | custom-call | flops 1409286144 | bytes 8000000 | tf_op jit(solution)/shard_map/pallas_call | solution.py:145
  94.7 41.9 %all_to_all.20 = bf16[8,3,32,896]{3,2,1,0:T(8,128)(2,1)S(1)} all-to-all(bf16[8,3,32,896]{3,2,1,0:T(8,128)(2,1)S(1)} %get-tuple-element.20), channel_id=1, replica_groups=mesh['y'=8,'zl'=4,'core'=2,'zh'=2,'x'=4] {'y'}, dimensions={0} | all-to-all | bytes 2752512 | tf_op jit(solution)/shard_map/all_to_all | solution.py:154
  136.9 36.2 %all_to_all.21.acts = bf16[8,3,32,896]{3,2,1,0:T(8,128)(2,1)S(1)} all-to-all(bf16[8,3,32,896]{3,2,1,0:T(8,128)(2,1)S(1)} %broadcast_in_dim.2), channel_id=1, replica_groups=mesh['y'=8,'zl'=4,'core'=2,'zh'=2,'x'=4] {'y'}, dimensions={0} | all-to-all | bytes 2752512 | tf_op jit(solution)/shard_map/all_to_all | solution.py:162
  173.1 2.6 %shard_map.74 = (f32[8,2,128,128]{3,2,1,0:T(8,128)S(1)}, f32[8,2,128,128]{3,2,1,0:T(8,128)S(1)}) custom-call(s32[9]{0:T(128)S(1)} %copy-done.6, bf16[8,3,32,896]{3,2,1,0:T(8,128)(2,1)S(1)} %all_to_all.21.acts, bf16[3,512,896]{2,1,0:T(8,128)(2,1)S(1)} %shard_map.70.kept, bf16[3,512,896]{2,1,0:T(8,128)(2,1)S(1)} %get-tuple-element.21.moved), custom_call_target="tpu_custom_call" | custom-call | flops 1409286144 | bytes 8000000 | tf_op jit(solution)/shard_map/pallas_call | solution.py:21
  175.8 4.8 %collective-permute-start.8 = (f32[8,2,128,128]{3,2,1,0:T(8,128)S(1)}, f32[8,2,128,128]{3,2,1,0:T(8,128)S(1)}, u32[]{:S(2)}, u32[]{:S(2)}) collective-permute-start(f32[8,2,128,128]{3,2,1,0:T(8,128)S(1)} %get-tuple-element.23), channel_id=1, source_target_pairs={{0,8},{8,0},{1,9},{9,1},{2,10},{10,2},{3,11},{11,3},{4,12},{12,4},... | collective-permute-start | bytes 3145736 | tf_op jit(solution)/shard_map/ppermute | solution.py:37
  180.6 2.3 %collective-permute-done.8 = f32[8,2,128,128]{3,2,1,0:T(8,128)S(1)} collective-permute-done((f32[8,2,128,128]{3,2,1,0:T(8,128)S(1)}, f32[8,2,128,128]{3,2,1,0:T(8,128)S(1)}, u32[]{:S(2)}, u32[]{:S(2)}) %collective-permute-start.8) | collective-permute-done | bytes 1048608 | tf_op jit(solution)/shard_map/ppermute | solution.py:37
  183.0 20.4 %all_to_all.22 = bf16[8,2,128,128]{3,2,1,0:T(8,128)(2,1)S(1)} all-to-all(bf16[8,2,128,128]{3,2,1,0:T(8,128)(2,1)S(1)} %add_convert_fusion), channel_id=1, replica_groups=mesh['y'=8,'zl'=4,'core'=2,'zh'=2,'x'=4] {'zh','zl'}, dimensions={0} | all-to-all | bytes 1048576 | tf_op jit(solution)/shard_map/all_to_all | solution.py:169
  (32 shorter events, 7.7 us)
Async XLA Ops:
  0.7 1.0 copy-start.1
  1.7 1.0 copy-start.2
  2.8 1.0 copy-start.3
  3.8 58.3 %copy-start.4 = (s32[3]{0:T(128)}, s32[3]{0:T(128)S(1)}, u32[]{:S(2)}) copy-start(s32[3]{0:T(128)S(1)} %pad_add_fusion.place) | copy-start | bytes 40
  4.4 25.8 %collective-permute-start = (bf16[384,896]{1,0:T(8,128)(2,1)S(1)}, bf16[384,896]{1,0:T(8,128)(2,1)S(1)}, u32[]{:S(2)}, u32[]{:S(2)}) collective-permute-start(bf16[384,896]{1,0:T(8,128)(2,1)S(1)} %get-tuple-element.13), channel_id=1, source_target_pairs={{0,4},{4,0},{1,5},{5,1},{2,6},{6,2},{3,7},{7,3},{8,12},{12,8},{9,1... | collective-permute-start | bytes 2064392 | tf_op jit(solution)/shard_map/ppermute | solution.py:37
  15.9 19.4 %collective-permute-start.3 = (bf16[384,896]{1,0:T(8,128)(2,1)S(1)}, bf16[384,896]{1,0:T(8,128)(2,1)S(1)}, u32[]{:S(2)}, u32[]{:S(2)}) collective-permute-start(bf16[384,896]{1,0:T(8,128)(2,1)S(1)} %get-tuple-element.14.b0), channel_id=1, source_target_pairs={{0,2},{1,3},{2,0},{3,1},{4,6},{5,7},{6,4},{7,5},{8,10},{9,11},{10,... | collective-permute-start | bytes 2064392 | tf_op jit(solution)/shard_map/ppermute | solution.py:33
  20.6 29.9 %collective-permute-start.2 = (bf16[384,896]{1,0:T(8,128)(2,1)S(1)}, bf16[384,896]{1,0:T(8,128)(2,1)S(1)}, u32[]{:S(2)}, u32[]{:S(2)}) collective-permute-start(bf16[384,896]{1,0:T(8,128)(2,1)S(1)} %get-tuple-element.14.b0), channel_id=1, source_target_pairs={{0,3},{1,0},{2,1},{3,2},{4,7},{5,4},{6,5},{7,6},{8,11},{9,8},{10,9... | collective-permute-start | bytes 2064392 | tf_op jit(solution)/shard_map/ppermute | solution.py:33
  23.3 28.1 %collective-permute-start.1 = (bf16[384,896]{1,0:T(8,128)(2,1)S(1)}, bf16[384,896]{1,0:T(8,128)(2,1)S(1)}, u32[]{:S(2)}, u32[]{:S(2)}) collective-permute-start(bf16[384,896]{1,0:T(8,128)(2,1)S(1)} %get-tuple-element.14.b0), channel_id=1, source_target_pairs={{0,1},{1,2},{2,3},{3,0},{4,5},{5,6},{6,7},{7,4},{8,9},{9,10},{10,1... | collective-permute-start | bytes 2064392 | tf_op jit(solution)/shard_map/ppermute | solution.py:33
  31.7 30.5 %copy-start.7 = (bf16[128,128]{1,0:T(8,128)(2,1)S(1)}, bf16[128,128]{1,0:T(8,128)(2,1)}, u32[]{:S(2)}) copy-start(bf16[128,128]{1,0:T(8,128)(2,1)} %tokens) | copy-start | bytes 98308
  31.7 30.5 %copy-start.8 = (bf16[128,128]{1,0:T(8,128)(2,1)S(1)}, bf16[128,128]{1,0:T(8,128)(2,1)}, u32[]{:S(2)}) copy-start(bf16[128,128]{1,0:T(8,128)(2,1)} %grad.1) | copy-start | bytes 98308
  52.2 36.1 %collective-permute-start.7 = (bf16[384,896]{1,0:T(8,128)(2,1)}, bf16[384,896]{1,0:T(8,128)(2,1)}, u32[]{:S(2)}, u32[]{:S(2)}) collective-permute-start(bf16[384,896]{1,0:T(8,128)(2,1)} %shard_map.69.b0), channel_id=1, source_target_pairs={{0,2},{1,3},{2,0},{3,1},{4,6},{5,7},{6,4},{7,5},{8,10},{9,11},{10,... | collective-permute-start | bytes 2064392 | tf_op jit(solution)/shard_map/ppermute | solution.py:33
  56.8 31.4 %collective-permute-start.6 = (bf16[384,896]{1,0:T(8,128)(2,1)}, bf16[384,896]{1,0:T(8,128)(2,1)}, u32[]{:S(2)}, u32[]{:S(2)}) collective-permute-start(bf16[384,896]{1,0:T(8,128)(2,1)} %shard_map.69.b0), channel_id=1, source_target_pairs={{0,3},{1,0},{2,1},{3,2},{4,7},{5,4},{6,5},{7,6},{8,11},{9,8},{10,9... | collective-permute-start | bytes 2064392 | tf_op jit(solution)/shard_map/ppermute | solution.py:33
  59.6 28.6 %collective-permute-start.5 = (bf16[384,896]{1,0:T(8,128)(2,1)}, bf16[384,896]{1,0:T(8,128)(2,1)}, u32[]{:S(2)}, u32[]{:S(2)}) collective-permute-start(bf16[384,896]{1,0:T(8,128)(2,1)} %shard_map.69.b0), channel_id=1, source_target_pairs={{0,1},{1,2},{2,3},{3,0},{4,5},{5,6},{6,7},{7,4},{8,9},{9,10},{10,1... | collective-permute-start | bytes 2064392 | tf_op jit(solution)/shard_map/ppermute | solution.py:33
  62.8 0.8 copy-start
  63.6 20.3 %all-to-all-start = ((bf16[8,2,128,128]{3,2,1,0:T(8,128)(2,1)}), bf16[8,2,128,128]{3,2,1,0:T(8,128)(2,1)S(1)}, u32[]{:S(2)}, u32[]{:S(2)}) async-start(bf16[8,2,128,128]{3,2,1,0:T(8,128)(2,1)} %copy-done), calls=%async_computation | async-start | bytes 1048576 | tf_op jit(solution)/shard_map/all_to_all | solution.py:143
  83.9 5.8 %collective-permute-start.4 = (bf16[8,2,128,128]{3,2,1,0:T(8,128)(2,1)S(1)}, bf16[8,2,128,128]{3,2,1,0:T(8,128)(2,1)S(1)}, u32[]{:S(2)}, u32[]{:S(2)}) collective-permute-start(bf16[8,2,128,128]{3,2,1,0:T(8,128)(2,1)S(1)} %all-to-all-done.near), channel_id=1, source_target_pairs={{0,8},{8,0},{1,9},{9,1},{2,10},{10,2},{3,11},{11,3},{4,12},{12,4},... | collective-permute-start | bytes 1572872 | tf_op jit(solution)/shard_map/ppermute | solution.py:37
  89.7 0.7 copy-start.5
  136.9 36.2 %copy-start.6 = (s32[9]{0:T(128)S(1)}, s32[9]{0:T(128)}, u32[]{:S(2)}) copy-start(s32[9]{0:T(128)} %shard_map.72.table) | copy-start | bytes 112
  175.8 7.1 %collective-permute-start.8 = (f32[8,2,128,128]{3,2,1,0:T(8,128)S(1)}, f32[8,2,128,128]{3,2,1,0:T(8,128)S(1)}, u32[]{:S(2)}, u32[]{:S(2)}) collective-permute-start(f32[8,2,128,128]{3,2,1,0:T(8,128)S(1)} %get-tuple-element.23), channel_id=1, source_target_pairs={{0,8},{8,0},{1,9},{9,1},{2,10},{10,2},{3,11},{11,3},{4,12},{12,4},... | collective-permute-start | bytes 3145736 | tf_op jit(solution)/shard_map/ppermute | solution.py:37

commit v12 on v8

--- a/solution.py
+++ b/solution.py
@@ -25,7 +25,7 @@
         out_specs=[VMEM] * len(outs),
         scratch_shapes=scratch,
         cost_estimate=pl.CostEstimate(flops=flops, bytes_accessed=moved, transcendentals=0),
-        compiler_params=pltpu.CompilerParams(vmem_limit_bytes=12 << 20),
+        compiler_params=pltpu.CompilerParams(vmem_limit_bytes=24 << 20),
     )(*operands)
 
 

time: 201 us -> 201 us (level)
  no operation moved by 1% of the time
where the time goes in v12:
time: 201 us; the launch traced here: 199 us
  blocking collectives  94.9 us (47%)
  starting transfers between devices  47.8 us (24%)
  waiting for transfers between devices  38.5 us (19%)
  Pallas kernels  11.7 us (6%)
  local copies, waits for them, and re-layouts  4.6 us (2%)
    all_to_all x1, blocking collectives, on_device(): parts = lax.all_to_all(parts, 'y', 0, 0, tiled=True)  40 us
    all_to_all x1, blocking collectives, on_device(): lax.all_to_all(jnp.broadcast_to(rows[None], (8, 3, 32, 896)), 'y', 0, 0,...  35.5 us
    ppermute x3, starting transfers between devices, exchange(): return lax.ppermute(values, axis, [(0, 1), (1, 0)])  23.5 us
    ppermute x6, starting transfers between devices, shift(): return lax.ppermute(values, 'x', [(i, (i + step) % 4) for i in range(4)])  19.9 us
    all_to_all x1, blocking collectives, on_device(): terms = lax.all_to_all(terms, RING, 0, 0, tiled=True)  19.5 us
    ppermute x6, waiting for transfers between devices, shift(): return lax.ppermute(values, 'x', [(i, (i + step) % 4) for i in range(4)])  19.1 us
    all_to_all x1, waiting for transfers between devices, on_device(): lax.all_to_all(acts, RING, 0, 0, tiled=True)  12.9 us
    pallas_call x7, Pallas kernels, call(): pl.pallas_call(kernel, out_shape=outs, in_specs=[SMEM] + [VMEM] * (len(op...  10.3 us
  transfers between devices with their start and end apart: 10, of which 6 were waited for; matrix products, arithmetic and copies ran while one was open for 0% of the time, Pallas kernels for 3%

profile of v12, /device:TPU:1, one launch (start us, length us, event | category | flops | bytes accessed | tf_op | source)
XLA Modules:
  0.0 199.0 jit_solution(8378733958628380771)
XLA Ops:
  4.4 11.5 %collective-permute-start = (bf16[384,896]{1,0:T(8,128)(2,1)S(1)}, bf16[384,896]{1,0:T(8,128)(2,1)S(1)}, u32[]{:S(2)}, u32[]{:S(2)}) collective-permute-start(bf16[384,896]{1,0:T(8,128)(2,1)S(1)} %get-tuple-element.11), channel_id=1, source_target_pairs={{0,4},{4,0},{1,5},{5,1},{2,6},{6,2},{3,7},{7,3},{8,12},{12,8},{9,1... | collective-permute-start | bytes 2064392 | tf_op jit(solution)/shard_map/ppermute | solution.py:37
  15.9 3.1 %collective-permute-start.1 = (bf16[384,896]{1,0:T(8,128)(2,1)S(1)}, bf16[384,896]{1,0:T(8,128)(2,1)S(1)}, u32[]{:S(2)}, u32[]{:S(2)}) collective-permute-start(bf16[384,896]{1,0:T(8,128)(2,1)S(1)} %get-tuple-element.12.b0), channel_id=1, source_target_pairs={{0,1},{1,2},{2,3},{3,0},{4,5},{5,6},{6,7},{7,4},{8,9},{9,10},{10,1... | collective-permute-start | bytes 2064392 | tf_op jit(solution)/shard_map/ppermute | solution.py:33
  19.0 3.4 %collective-permute-start.2 = (bf16[384,896]{1,0:T(8,128)(2,1)S(1)}, bf16[384,896]{1,0:T(8,128)(2,1)S(1)}, u32[]{:S(2)}, u32[]{:S(2)}) collective-permute-start(bf16[384,896]{1,0:T(8,128)(2,1)S(1)} %get-tuple-element.12.b0), channel_id=1, source_target_pairs={{0,3},{1,0},{2,1},{3,2},{4,7},{5,4},{6,5},{7,6},{8,11},{9,8},{10,9... | collective-permute-start | bytes 2064392 | tf_op jit(solution)/shard_map/ppermute | solution.py:33
  22.4 3.4 %collective-permute-start.3 = (bf16[384,896]{1,0:T(8,128)(2,1)S(1)}, bf16[384,896]{1,0:T(8,128)(2,1)S(1)}, u32[]{:S(2)}, u32[]{:S(2)}) collective-permute-start(bf16[384,896]{1,0:T(8,128)(2,1)S(1)} %get-tuple-element.12.b0), channel_id=1, source_target_pairs={{0,2},{1,3},{2,0},{3,1},{4,6},{5,7},{6,4},{7,5},{8,10},{9,11},{10,... | collective-permute-start | bytes 2064392 | tf_op jit(solution)/shard_map/ppermute | solution.py:33
  25.9 4.3 %collective-permute-done.block = bf16[384,896]{1,0:T(8,128)(2,1)S(1)} collective-permute-done((bf16[384,896]{1,0:T(8,128)(2,1)S(1)}, bf16[384,896]{1,0:T(8,128)(2,1)S(1)}, u32[]{:S(2)}, u32[]{:S(2)}) %collective-permute-start) | collective-permute-done | bytes 688160 | tf_op jit(solution)/shard_map/ppermute | solution.py:37
  30.2 1.4 shard_map.69.b0
  31.7 3.3 %collective-permute-done.1.b1 = bf16[384,896]{1,0:T(8,128)(2,1)S(1)} collective-permute-done((bf16[384,896]{1,0:T(8,128)(2,1)S(1)}, bf16[384,896]{1,0:T(8,128)(2,1)S(1)}, u32[]{:S(2)}, u32[]{:S(2)}) %collective-permute-start.1) | collective-permute-done | bytes 688160 | tf_op jit(solution)/shard_map/ppermute | solution.py:33
  35.0 1.6 collective-permute-done.2.b2
  36.6 14.1 %collective-permute-done.3.b3 = bf16[384,896]{1,0:T(8,128)(2,1)S(1)} collective-permute-done((bf16[384,896]{1,0:T(8,128)(2,1)S(1)}, bf16[384,896]{1,0:T(8,128)(2,1)S(1)}, u32[]{:S(2)}, u32[]{:S(2)}) %collective-permute-start.3) | collective-permute-done | bytes 688160 | tf_op jit(solution)/shard_map/ppermute | solution.py:33
  51.5 4.4 %collective-permute-start.5 = (bf16[384,896]{1,0:T(8,128)(2,1)}, bf16[384,896]{1,0:T(8,128)(2,1)}, u32[]{:S(2)}, u32[]{:S(2)}) collective-permute-start(bf16[384,896]{1,0:T(8,128)(2,1)} %shard_map.69.b0), channel_id=1, source_target_pairs={{0,1},{1,2},{2,3},{3,0},{4,5},{5,6},{6,7},{7,4},{8,9},{9,10},{10,1... | collective-permute-start | bytes 2064392 | tf_op jit(solution)/shard_map/ppermute | solution.py:33
  55.9 2.5 %collective-permute-start.6 = (bf16[384,896]{1,0:T(8,128)(2,1)}, bf16[384,896]{1,0:T(8,128)(2,1)}, u32[]{:S(2)}, u32[]{:S(2)}) collective-permute-start(bf16[384,896]{1,0:T(8,128)(2,1)} %shard_map.69.b0), channel_id=1, source_target_pairs={{0,3},{1,0},{2,1},{3,2},{4,7},{5,4},{6,5},{7,6},{8,11},{9,8},{10,9... | collective-permute-start | bytes 2064392 | tf_op jit(solution)/shard_map/ppermute | solution.py:33
  58.4 3.1 %collective-permute-start.7 = (bf16[384,896]{1,0:T(8,128)(2,1)}, bf16[384,896]{1,0:T(8,128)(2,1)}, u32[]{:S(2)}, u32[]{:S(2)}) collective-permute-start(bf16[384,896]{1,0:T(8,128)(2,1)} %shard_map.69.b0), channel_id=1, source_target_pairs={{0,2},{1,3},{2,0},{3,1},{4,6},{5,7},{6,4},{7,5},{8,10},{9,11},{10,... | collective-permute-start | bytes 2064392 | tf_op jit(solution)/shard_map/ppermute | solution.py:33
  62.9 4.3 %all-to-all-start = ((bf16[8,2,128,128]{3,2,1,0:T(8,128)(2,1)}), bf16[8,2,128,128]{3,2,1,0:T(8,128)(2,1)S(1)}, u32[]{:S(2)}, u32[]{:S(2)}) async-start(bf16[8,2,128,128]{3,2,1,0:T(8,128)(2,1)} %copy-done), calls=%async_computation | async-start | bytes 1048576 | tf_op jit(solution)/shard_map/all_to_all | solution.py:131
  67.2 1.3 shard_map.72.table
  68.6 12.9 %all-to-all-done.near = bf16[8,2,128,128]{3,2,1,0:T(8,128)(2,1)S(1)} async-done(((bf16[8,2,128,128]{3,2,1,0:T(8,128)(2,1)}), bf16[8,2,128,128]{3,2,1,0:T(8,128)(2,1)S(1)}, u32[]{:S(2)}, u32[]{:S(2)}) %all-to-all-start) | async-done | bytes 524320 | tf_op jit(solution)/shard_map/all_to_all | solution.py:131
  81.4 6.1 %collective-permute-start.4 = (bf16[8,2,128,128]{3,2,1,0:T(8,128)(2,1)S(1)}, bf16[8,2,128,128]{3,2,1,0:T(8,128)(2,1)S(1)}, u32[]{:S(2)}, u32[]{:S(2)}) collective-permute-start(bf16[8,2,128,128]{3,2,1,0:T(8,128)(2,1)S(1)} %all-to-all-done.near), channel_id=1, source_target_pairs={{0,8},{8,0},{1,9},{9,1},{2,10},{10,2},{3,11},{11,3},{4,12},{12,4},... | collective-permute-start | bytes 1572872 | tf_op jit(solution)/shard_map/ppermute | solution.py:37
  87.6 1.9 shard_map.73.moved
  89.6 2.4 %shard_map.74 = bf16[8,3,32,896]{3,2,1,0:T(8,128)(2,1)S(1)} custom-call(s32[9]{0:T(128)S(1)} %copy-done.6, bf16[8,2,128,128]{3,2,1,0:T(8,128)(2,1)S(1)} %all-to-all-done.near, bf16[8,2,128,128]{3,2,1,0:T(8,128)(2,1)S(1)} %collective-permute-done.4.other, bf16[3,512,896]{2,1,0:T(8,128)(2,1)S(1)} %shard_map.70.kept, bf16[3,512,896]{2,1,0:T(8,128)(2,1)S(1)} %shard_map.73.moved), custom_call_target="tpu_custom_call" | custom-call | flops 1409286144 | bytes 8000000 | tf_op jit(solution)/shard_map/pallas_call | solution.py:21
  92.0 40.0 %all_to_all.20 = bf16[8,3,32,896]{3,2,1,0:T(8,128)(2,1)S(1)} all-to-all(bf16[8,3,32,896]{3,2,1,0:T(8,128)(2,1)S(1)} %shard_map.74), channel_id=1, replica_groups=mesh['y'=8,'zl'=4,'core'=2,'zh'=2,'x'=4] {'y'}, dimensions={0} | all-to-all | bytes 2752512 | tf_op jit(solution)/shard_map/all_to_all | solution.py:138
  132.4 35.5 %all_to_all.21.acts = bf16[8,3,32,896]{3,2,1,0:T(8,128)(2,1)S(1)} all-to-all(bf16[8,3,32,896]{3,2,1,0:T(8,128)(2,1)S(1)} %broadcast_in_dim.2), channel_id=1, replica_groups=mesh['y'=8,'zl'=4,'core'=2,'zh'=2,'x'=4] {'y'}, dimensions={0} | all-to-all | bytes 2752512 | tf_op jit(solution)/shard_map/all_to_all | solution.py:146
  167.9 2.6 %shard_map.75 = (f32[8,2,128,128]{3,2,1,0:T(8,128)S(1)}, f32[8,2,128,128]{3,2,1,0:T(8,128)S(1)}) custom-call(s32[9]{0:T(128)S(1)} %copy-done.6, bf16[8,3,32,896]{3,2,1,0:T(8,128)(2,1)S(1)} %all_to_all.21.acts, bf16[3,512,896]{2,1,0:T(8,128)(2,1)S(1)} %shard_map.70.kept, bf16[3,512,896]{2,1,0:T(8,128)(2,1)S(1)} %shard_map.73.moved), custom_call_target="tpu_custom_call" | custom-call | flops 1409286144 | bytes 8000000 | tf_op jit(solution)/shard_map/pallas_call | solution.py:21
  170.5 5.9 %collective-permute-start.8 = (f32[8,2,128,128]{3,2,1,0:T(8,128)S(1)}, f32[8,2,128,128]{3,2,1,0:T(8,128)S(1)}, u32[]{:S(2)}, u32[]{:S(2)}) collective-permute-start(f32[8,2,128,128]{3,2,1,0:T(8,128)S(1)} %get-tuple-element.19), channel_id=1, source_target_pairs={{0,8},{8,0},{1,9},{9,1},{2,10},{10,2},{3,11},{11,3},{4,12},{12,4},... | collective-permute-start | bytes 3145736 | tf_op jit(solution)/shard_map/ppermute | solution.py:37
  176.5 2.3 %collective-permute-done.8 = f32[8,2,128,128]{3,2,1,0:T(8,128)S(1)} collective-permute-done((f32[8,2,128,128]{3,2,1,0:T(8,128)S(1)}, f32[8,2,128,128]{3,2,1,0:T(8,128)S(1)}, u32[]{:S(2)}, u32[]{:S(2)}) %collective-permute-start.8) | collective-permute-done | bytes 1048608 | tf_op jit(solution)/shard_map/ppermute | solution.py:37
  178.8 19.5 %all_to_all.22 = bf16[8,2,128,128]{3,2,1,0:T(8,128)(2,1)S(1)} all-to-all(bf16[8,2,128,128]{3,2,1,0:T(8,128)(2,1)S(1)} %add_convert_fusion), channel_id=1, replica_groups=mesh['y'=8,'zl'=4,'core'=2,'zh'=2,'x'=4] {'zh','zl'}, dimensions={0} | all-to-all | bytes 1048576 | tf_op jit(solution)/shard_map/all_to_all | solution.py:153
  (33 shorter events, 7.2 us)
Async XLA Ops:
  0.7 1.0 copy-start.1
  1.7 1.0 copy-start.2
  2.8 1.0 copy-start.3
  3.8 57.7 %copy-start.4 = (s32[3]{0:T(128)}, s32[3]{0:T(128)S(1)}, u32[]{:S(2)}) copy-start(s32[3]{0:T(128)S(1)} %pad_add_fusion.place) | copy-start | bytes 40
  4.4 25.8 %collective-permute-start = (bf16[384,896]{1,0:T(8,128)(2,1)S(1)}, bf16[384,896]{1,0:T(8,128)(2,1)S(1)}, u32[]{:S(2)}, u32[]{:S(2)}) collective-permute-start(bf16[384,896]{1,0:T(8,128)(2,1)S(1)} %get-tuple-element.11), channel_id=1, source_target_pairs={{0,4},{4,0},{1,5},{5,1},{2,6},{6,2},{3,7},{7,3},{8,12},{12,8},{9,1... | collective-permute-start | bytes 2064392 | tf_op jit(solution)/shard_map/ppermute | solution.py:37
  15.9 19.1 %collective-permute-start.1 = (bf16[384,896]{1,0:T(8,128)(2,1)S(1)}, bf16[384,896]{1,0:T(8,128)(2,1)S(1)}, u32[]{:S(2)}, u32[]{:S(2)}) collective-permute-start(bf16[384,896]{1,0:T(8,128)(2,1)S(1)} %get-tuple-element.12.b0), channel_id=1, source_target_pairs={{0,1},{1,2},{2,3},{3,0},{4,5},{5,6},{6,7},{7,4},{8,9},{9,10},{10,1... | collective-permute-start | bytes 2064392 | tf_op jit(solution)/shard_map/ppermute | solution.py:33
  19.0 17.6 %collective-permute-start.2 = (bf16[384,896]{1,0:T(8,128)(2,1)S(1)}, bf16[384,896]{1,0:T(8,128)(2,1)S(1)}, u32[]{:S(2)}, u32[]{:S(2)}) collective-permute-start(bf16[384,896]{1,0:T(8,128)(2,1)S(1)} %get-tuple-element.12.b0), channel_id=1, source_target_pairs={{0,3},{1,0},{2,1},{3,2},{4,7},{5,4},{6,5},{7,6},{8,11},{9,8},{10,9... | collective-permute-start | bytes 2064392 | tf_op jit(solution)/shard_map/ppermute | solution.py:33
  22.4 28.3 %collective-permute-start.3 = (bf16[384,896]{1,0:T(8,128)(2,1)S(1)}, bf16[384,896]{1,0:T(8,128)(2,1)S(1)}, u32[]{:S(2)}, u32[]{:S(2)}) collective-permute-start(bf16[384,896]{1,0:T(8,128)(2,1)S(1)} %get-tuple-element.12.b0), channel_id=1, source_target_pairs={{0,2},{1,3},{2,0},{3,1},{4,6},{5,7},{6,4},{7,5},{8,10},{9,11},{10,... | collective-permute-start | bytes 2064392 | tf_op jit(solution)/shard_map/ppermute | solution.py:33
  31.6 29.9 %copy-start.7 = (bf16[128,128]{1,0:T(8,128)(2,1)S(1)}, bf16[128,128]{1,0:T(8,128)(2,1)}, u32[]{:S(2)}) copy-start(bf16[128,128]{1,0:T(8,128)(2,1)} %tokens) | copy-start | bytes 98308
  31.7 29.9 %copy-start.8 = (bf16[128,128]{1,0:T(8,128)(2,1)S(1)}, bf16[128,128]{1,0:T(8,128)(2,1)}, u32[]{:S(2)}) copy-start(bf16[128,128]{1,0:T(8,128)(2,1)} %grad.1) | copy-start | bytes 98308
  51.5 36.1 %collective-permute-start.5 = (bf16[384,896]{1,0:T(8,128)(2,1)}, bf16[384,896]{1,0:T(8,128)(2,1)}, u32[]{:S(2)}, u32[]{:S(2)}) collective-permute-start(bf16[384,896]{1,0:T(8,128)(2,1)} %shard_map.69.b0), channel_id=1, source_target_pairs={{0,1},{1,2},{2,3},{3,0},{4,5},{5,6},{6,7},{7,4},{8,9},{9,10},{10,1... | collective-permute-start | bytes 2064392 | tf_op jit(solution)/shard_map/ppermute | solution.py:33
  55.9 31.7 %collective-permute-start.6 = (bf16[384,896]{1,0:T(8,128)(2,1)}, bf16[384,896]{1,0:T(8,128)(2,1)}, u32[]{:S(2)}, u32[]{:S(2)}) collective-permute-start(bf16[384,896]{1,0:T(8,128)(2,1)} %shard_map.69.b0), channel_id=1, source_target_pairs={{0,3},{1,0},{2,1},{3,2},{4,7},{5,4},{6,5},{7,6},{8,11},{9,8},{10,9... | collective-permute-start | bytes 2064392 | tf_op jit(solution)/shard_map/ppermute | solution.py:33
  58.4 29.2 %collective-permute-start.7 = (bf16[384,896]{1,0:T(8,128)(2,1)}, bf16[384,896]{1,0:T(8,128)(2,1)}, u32[]{:S(2)}, u32[]{:S(2)}) collective-permute-start(bf16[384,896]{1,0:T(8,128)(2,1)} %shard_map.69.b0), channel_id=1, source_target_pairs={{0,2},{1,3},{2,0},{3,1},{4,6},{5,7},{6,4},{7,5},{8,10},{9,11},{10,... | collective-permute-start | bytes 2064392 | tf_op jit(solution)/shard_map/ppermute | solution.py:33
  62.2 0.8 copy-start
  62.9 18.5 %all-to-all-start = ((bf16[8,2,128,128]{3,2,1,0:T(8,128)(2,1)}), bf16[8,2,128,128]{3,2,1,0:T(8,128)(2,1)S(1)}, u32[]{:S(2)}, u32[]{:S(2)}) async-start(bf16[8,2,128,128]{3,2,1,0:T(8,128)(2,1)} %copy-done), calls=%async_computation | async-start | bytes 1048576 | tf_op jit(solution)/shard_map/all_to_all | solution.py:131
  67.2 20.4 %copy-start.5 = (s32[3]{0:T(128)S(1)}, s32[3]{0:T(128)}, u32[]{:S(2)}) copy-start(s32[3]{0:T(128)} %copy-done.4) | copy-start | bytes 40
  68.6 21.0 %copy-start.6 = (s32[9]{0:T(128)S(1)}, s32[9]{0:T(128)}, u32[]{:S(2)}) copy-start(s32[9]{0:T(128)} %shard_map.72.table) | copy-start | bytes 112
  81.4 8.1 %collective-permute-start.4 = (bf16[8,2,128,128]{3,2,1,0:T(8,128)(2,1)S(1)}, bf16[8,2,128,128]{3,2,1,0:T(8,128)(2,1)S(1)}, u32[]{:S(2)}, u32[]{:S(2)}) collective-permute-start(bf16[8,2,128,128]{3,2,1,0:T(8,128)(2,1)S(1)} %all-to-all-done.near), channel_id=1, source_target_pairs={{0,8},{8,0},{1,9},{9,1},{2,10},{10,2},{3,11},{11,3},{4,12},{12,4},... | collective-permute-start | bytes 1572872 | tf_op jit(solution)/shard_map/ppermute | solution.py:37
  170.5 8.2 %collective-permute-start.8 = (f32[8,2,128,128]{3,2,1,0:T(8,128)S(1)}, f32[8,2,128,128]{3,2,1,0:T(8,128)S(1)}, u32[]{:S(2)}, u32[]{:S(2)}) collective-permute-start(f32[8,2,128,128]{3,2,1,0:T(8,128)S(1)} %get-tuple-element.19), channel_id=1, source_target_pairs={{0,8},{8,0},{1,9},{9,1},{2,10},{10,2},{3,11},{11,3},{4,12},{12,4},... | collective-permute-start | bytes 3145736 | tf_op jit(solution)/shard_map/ppermute | solution.py:37
